TPU v7x, 32 devices: a whole 2x2x4 slice. The times are simulated.
32 devices in a mesh: rep: 4 (over y, x), grp: 8 (over z, core).
Axes of the slice: x: 2, y: 2, z: 4, core: 2. Of those that a mesh axis runs over, the one named last changes fastest.
Arguments:
- activations: bfloat16 [16384, 512], P(('rep', 'grp')), may hold values from -6 to 6
- out_grads: bfloat16 [16384, 1024], P(('rep', 'grp')), may hold values from -0.00390625 to 0.00390625
- stats_old: float32 [4, 512, 512], P(None, 'grp'), as said below
Outputs:
- stats_new: float32 [4, 512, 512], P(None, 'grp')
- update: float32 [2, 512, 512], P(None, 'grp')
Inputs may be any that keep to these rules, and one draw needn't show every extreme that they name: Each stats_old[c] is symmetric positive definite.
All inputs are finite; a program needn't handle non-finite values.
Results may differ from a plain program's by a relative error of at most 0.0009.
The roundings to bfloat16 on the way count: a program that leaves them out, or rounds other values in their place, can miss the bound.
Values may be sent and summed in bfloat16 or wider, within the bound.
No kernel may reach another device: no remote copies, remote signals or barrier semaphores. Data moves between devices by JAX's collectives and lax.ppermute only.
A program may use at most 64 MiB of HBM per device.

v0:
```python
import math

import jax
import jax.numpy as jnp
from jax import lax
from jax.sharding import PartitionSpec as P

ITERS = 2


DAMPING = 0.01


def chain_product(start, wholes):
    running = jnp.einsum("crb,cbd->crd", start, wholes[1], preferred_element_type=jnp.float32)
    return running


def on_device(activations, out_grads, stats_old):
    block_order = activations.shape[1]
    token_count = activations.shape[0]
    tile_count = out_grads.shape[1] // block_order
    rows_dev = stats_old.shape[1]
    row_start = lax.axis_index("grp") * rows_dev
    grads_three = out_grads.reshape(token_count, tile_count, block_order)
    term_rows = jnp.einsum(
        "ktc,ki->cti", grads_three, activations, preferred_element_type=jnp.float32
    )
    partial_rows = lax.psum_scatter(
        term_rows.reshape(rows_dev * lax.axis_size("grp"), tile_count * block_order),
        "grp",
        scatter_dimension=0,
        tiled=True,
    )
    summed = lax.psum(partial_rows, "rep")
    grad_full = lax.all_gather(summed.astype(jnp.bfloat16), "grp", axis=0, tiled=True)
    grad_three = grad_full.reshape(block_order, tile_count, block_order)
    left_cols = lax.dynamic_slice_in_dim(grad_three, row_start, rows_dev, 2)
    left_rows = jnp.einsum(
        "jtr,jti->tri", left_cols, grad_three, preferred_element_type=jnp.float32
    )
    right_part = lax.dynamic_slice_in_dim(grad_three, row_start, rows_dev, 0)
    right_rows = jnp.einsum(
        "rti,jti->trj", right_part, grad_three, preferred_element_type=jnp.float32
    )
    stats_new = stats_old + jnp.concatenate([left_rows, right_rows], axis=0)
    column_ids = lax.broadcasted_iota(jnp.int32, (rows_dev, block_order), 1)
    row_ids = lax.broadcasted_iota(jnp.int32, (rows_dev, block_order), 0) + row_start
    eye_rows = (column_ids == row_ids).astype(jnp.float32)
    damped = stats_new + DAMPING * eye_rows
    squares = lax.psum(jnp.sum(damped * damped, axis=(1, 2)), "grp")
    scales = 2.5 / jnp.sqrt(squares)
    quarter = scales**0.25
    iterate_all = scales[:, None, None] * damped
    iterate = iterate_all
    whole_list = []
    first_rows = None
    for iteration in range(ITERS):
        factor = ((5.0 * eye_rows - iterate) * 0.25).astype(jnp.bfloat16)
        if iteration == 0:
            first_rows = factor
        newton_whole_factor = lax.all_gather(factor, "grp", axis=1, tiled=True)
        whole_list.append(newton_whole_factor)
        if iteration + 1 < ITERS:
            upcast = newton_whole_factor.astype(jnp.float32)
            for repeat in range(4):
                iterate = jnp.einsum(
                    "crb,cbd->crd", iterate, upcast, precision=lax.Precision.HIGHEST
                )
    first_rows, wholes = (first_rows, whole_list)
    left_wholes = [whole_factor[:tile_count] for whole_factor in wholes]
    right_wholes = [whole_factor[tile_count:] for whole_factor in wholes]
    left_roots = (
        quarter[:tile_count, None, None] * chain_product(left_wholes[0], left_wholes)
    ).astype(jnp.bfloat16)
    right_roots = (
        quarter[tile_count:, None, None] * chain_product(first_rows[tile_count:], right_wholes)
    ).astype(jnp.bfloat16)
    inner_rows = jnp.einsum(
        "trj,jti->tri", right_roots, grad_three, preferred_element_type=jnp.float32
    )
    update = jnp.einsum(
        "trm,tmi->tri", inner_rows, left_roots.astype(jnp.float32), precision=lax.Precision.HIGHEST
    ) * math.sqrt(block_order)
    return (stats_new, update)


def solution(mesh):
    in_specs = (P(("rep", "grp"), None), P(("rep", "grp"), None), P(None, "grp", None))
    out_specs = (P(None, "grp", None), P(None, "grp", None))
    return jax.shard_map(
        on_device, mesh=mesh, in_specs=in_specs, out_specs=out_specs, check_vma=False
    )
```

profile of v0, /device:TPU:0, one launch (start us, length us, event | category | flops | bytes accessed | tf_op | source)
XLA Modules:
  0.0 185.5 jit_solution(2597735935797385937)
XLA Ops:
  7.2 0.0 reduce-scatter.4.cloned.1.call-start
  7.2 1.0 copy-done
  8.2 1.9 %fusion.3 = f32[512,2,512]{2,0,1:T(8,128)S(1)} fusion(bf16[64,2,8,512]{3,2,1,0:T(8,128)(2,1)} %bitcast.31, bf16[512,512]{1,0:T(8,128)(2,1)S(1)} %copy-done), kind=kOutput, calls=%fused_computation.7 | convolution fusion | flops 536870912 | bytes 3670016 | tf_op jit(solution)/shard_map/ktc,ki->cti/dot_general | solution.py:26
  10.2 1.8 copy.34
  12.0 0.0 reduce-scatter.4.cloned.1.call-update
  12.0 0.0 all-gather.4.cloned.1.call-start
  12.1 38.6 %reduce-scatter.4.cloned.1.call-done = f32[64,1024]{1,0:T(8,128)} async-done(((f32[512,1024]{1,0:T(8,128)}), f32[64,1024]{1,0:T(8,128)}) %reduce-scatter.4.cloned.1.call-update) | async-done | bytes 262160 | tf_op jit(solution)/shard_map/reduce_scatter | solution.py:29
  50.6 21.2 %all-reduce.1 = bf16[64,1024]{1,0:T(8,128)(2,1)} all-reduce(f32[64,1024]{1,0:T(8,128)} %reduce-scatter.4.cloned.1.call-done), channel_id=1, replica_groups=mesh['rep'=4,'grp'=8] {'rep'}, use_global_device_ids=true, to_apply=%region_1.0 | all-reduce | flops 65536 | bytes 393216 | tf_op jit(solution)/shard_map/psum | solution.py:35
  71.9 0.0 all-gather.4.cloned.1.call-update
  71.9 0.0 all-gather.6.cloned.1.call-start
  72.0 0.1 fusion.16
  72.1 19.2 %all-gather.4.cloned.1.call-done = bf16[512,1024]{1,0:T(8,128)(2,1)} async-done(((bf16[64,1024]{1,0:T(8,128)(2,1)}), bf16[512,1024]{1,0:T(8,128)(2,1)}) %all-gather.4.cloned.1.call-update) | async-done | bytes 1048592 | tf_op jit(solution)/shard_map/all_gather | solution.py:36
  91.3 1.5 copy.24
  92.8 0.4 fusion.14
  93.3 0.4 fusion.18
  93.7 0.2 multiply_reduce_fusion
  93.9 15.4 %psum.15 = f32[4]{0:T(128)S(1)} all-reduce(f32[4]{0:T(128)S(1)} %get-tuple-element.2), channel_id=1, replica_groups=mesh['rep'=4,'grp'=8] {'grp'}, use_global_device_ids=true, to_apply=%region_3.0 | all-reduce | flops 4 | bytes 32 | tf_op jit(solution)/shard_map/psum | solution.py:51
  109.3 0.8 multiply_convert_fusion.1
  110.2 0.0 all-gather.6.cloned.1.call-update
  110.2 0.0 all-gather.8.cloned.1.call-start
  110.2 27.2 %all-gather.6.cloned.1.call-done = bf16[4,512,512]{2,1,0:T(8,128)(2,1)} async-done(((bf16[4,64,512]{2,1,0:T(8,128)(2,1)}), bf16[4,512,512]{2,1,0:T(8,128)(2,1)}) %all-gather.6.cloned.1.call-update) | async-done | bytes 2097168 | tf_op jit(solution)/shard_map/all_gather | solution.py:62
  137.5 3.0 %fusion.9 = f32[4,64,512]{2,1,0:T(8,128)S(1)} fusion(bf16[4,512,512]{2,1,0:T(8,128)(2,1)} %all-gather.6.cloned.1.call-done, f32[4,64,512]{2,1,0:T(8,128)S(1)} %get-tuple-element.3, f32[4]{0:T(128)S(1)} %get-tuple-element.7, f32[64,512]{1,0:T(8,128)S(1)} %get-tuple-element.9), kind=kOutput, calls=%fused_computation.16 | convolution fusion | flops 805568512 | bytes 3276816 | tf_op jit(solution)/shard_map/crb,cbd->crd/dot_general | solution.py:67
  140.5 1.2 fusion.23
  141.7 1.2 fusion.24
  142.9 1.9 %fusion.1 = bf16[4,64,512]{2,1,0:T(8,128)(2,1)} fusion(f32[4,64,512]{2,1,0:T(8,128)S(1)} %fusion.24, bf16[4,512,512]{2,1,0:T(8,128)(2,1)S(1)} %copy-done.1, f32[64,512]{1,0:T(8,128)S(1)} %get-tuple-element.8), kind=kOutput, calls=%fused_computation.3 | convolution fusion | flops 805699584 | bytes 3014656 | tf_op jit(solution)/shard_map/crb,cbd->crd/dot_general | solution.py:67
  144.8 0.0 all-gather.8.cloned.1.call-update
  144.8 0.1 fusion.22
  144.9 28.7 %all-gather.8.cloned.1.call-done = bf16[4,512,512]{2,1,0:T(8,128)(2,1)} async-done(((bf16[4,64,512]{2,1,0:T(8,128)(2,1)}), bf16[4,512,512]{2,1,0:T(8,128)(2,1)}) %all-gather.8.cloned.1.call-update) | async-done | bytes 2097168 | tf_op jit(solution)/shard_map/all_gather | solution.py:62
  173.6 1.7 fusion.2
  175.2 1.7 fusion.25
  176.9 0.7 multiply_convert_fusion
  177.6 1.4 convolution_multiply_fusion.1
  (15 shorter events, 0.1 us)
Async XLA Ops:
  7.2 1.0 copy-start
  7.2 43.5 %reduce-scatter.4.cloned.1.call-start = ((), (), s32[]{:S(2)}) async-start(), calls=%async_computation.4 | async-start | bytes 2359296 | tf_op jit(solution)/shard_map/reduce_scatter | solution.py:29
  12.0 79.3 %all-gather.4.cloned.1.call-start = ((), (), s32[]{:S(2)}) async-start(), calls=%async_computation.1 | async-start | bytes 1179648 | tf_op jit(solution)/shard_map/all_gather | solution.py:36
  71.9 65.6 %all-gather.6.cloned.1.call-start = ((), (), s32[]{:S(2)}) async-start(), calls=%async_computation.2 | async-start | bytes 2359296 | tf_op jit(solution)/shard_map/all_gather | solution.py:62
  72.1 21.7 %copy-start.5 = (f32[4,64,512]{2,1,0:T(8,128)S(1)}, f32[4,64,512]{2,1,0:T(8,128)}, u32[]{:S(2)}) copy-start(f32[4,64,512]{2,1,0:T(8,128)} %param.5) | copy-start | bytes 1572868
  92.8 1.1 copy-start.2
  93.9 46.5 %copy-start.3 = (f32[4,64,512]{2,1,0:T(8,128)}, f32[4,64,512]{2,1,0:T(8,128)S(1)}, u32[]{:S(2)}) copy-start(f32[4,64,512]{2,1,0:T(8,128)S(1)} %get-tuple-element.3) | copy-start | bytes 1572868
  110.2 63.4 %all-gather.8.cloned.1.call-start = ((), (), s32[]{:S(2)}) async-start(), calls=%async_computation.3 | async-start | bytes 2359296 | tf_op jit(solution)/shard_map/all_gather | solution.py:62
  137.5 3.0 %copy-start.1 = (bf16[4,512,512]{2,1,0:T(8,128)(2,1)S(1)}, bf16[4,512,512]{2,1,0:T(8,128)(2,1)}, u32[]{:S(2)}) copy-start(bf16[4,512,512]{2,1,0:T(8,128)(2,1)} %all-gather.6.cloned.1.call-done) | copy-start | bytes 6291460
  142.9 30.7 %copy-start.4 = (bf16[4,64,512]{2,1,0:T(8,128)(2,1)S(1)}, bf16[4,64,512]{2,1,0:T(8,128)(2,1)}, u32[]{:S(2)}) copy-start(bf16[4,64,512]{2,1,0:T(8,128)(2,1)} %multiply_convert_fusion.1) | copy-start | bytes 786436
  173.6 3.3 %copy-start.6 = (bf16[4,512,512]{2,1,0:T(8,128)(2,1)S(1)}, bf16[4,512,512]{2,1,0:T(8,128)(2,1)}, u32[]{:S(2)}) copy-start(bf16[4,512,512]{2,1,0:T(8,128)(2,1)} %all-gather.8.cloned.1.call-done) | copy-start | bytes 6291460
Sparse Core Ops, SparseCore 0:
  12.2 38.4 reduce-scatter.3
  72.0 19.2 all-gather.3
  110.3 27.1 all-gather.5
  144.9 28.5 all-gather.7
where the time goes:
time: 186 us
  waiting for transfers between devices  114 us (61%)
  blocking collectives  36.6 us (20%)
  matrix products  15.5 us (8%)
  between operations  13.9 us (7%)
  local copies, waits for them, and re-layouts  4.43 us (2%)
    all_gather x2, waiting for transfers between devices, on_device(): newton_whole_factor = lax.all_gather(factor, 'grp', axis=1, tiled=True)  55.9 us
    reduce_scatter x1, waiting for transfers between devices, on_device(): lax.psum_scatter(term_rows.reshape(rows_dev * lax.axis_size('grp'), tile_...  38.6 us
    psum x1, blocking collectives, on_device(): summed = lax.psum(partial_rows, 'rep')  21.2 us
    all_gather x1, waiting for transfers between devices, on_device(): lax.all_gather(summed.astype(jnp.bfloat16), 'grp', axis=0, tiled=True)  19.2 us
    psum x1, blocking collectives, on_device(): squares = lax.psum(jnp.sum(damped * damped, axis=(1, 2)), 'grp')  15.4 us
    dot_general x4, matrix products, on_device(): jnp.einsum('crb,cbd->crd', iterate, upcast, precision=lax.Precision.HIGHEST)  7.3 us
  transfers between devices with their start and end apart: 4, of which 4 were waited for; matrix products, arithmetic and copies ran while one was open for 0% of the time, Pallas kernels for 0%

commit v1 on v0

v1 whole, which is shorter than its diff:
```python
import functools
import math

import jax
import jax.numpy as jnp
from jax import lax
from jax.experimental import pallas as pl
from jax.experimental.pallas import tpu as pltpu
from jax.sharding import PartitionSpec as P

F32 = jnp.float32
BF16 = jnp.bfloat16
DAMPING = 0.01
TILE = 16
RADIX = 4


def swap(array, axis, mask):
    size = lax.axis_size(axis)
    return lax.ppermute(array, axis, [(i, i ^ mask) for i in range(size)])


def plan(axis, low, size, rows):
    steps = []
    shift, left = low + size.bit_length() - 1, size
    while left > 1:
        radix = min(RADIX, left)
        splits = rows // radix >= TILE and rows % radix == 0
        if not splits:
            radix = 2
        shift -= radix.bit_length() - 1
        left //= radix
        rows = rows // radix if splits else rows
        steps.append((axis, shift, radix, splits))
    return steps, rows


def vmem(count):
    return [pl.BlockSpec(memory_space=pltpu.VMEM)] * count


SMEM = pl.BlockSpec(memory_space=pltpu.SMEM)


def dot(a, b, contract=(1, 0)):
    return lax.dot_general(
        a, b, (((contract[0],), (contract[1],)), ((), ())), preferred_element_type=F32
    )


def term_kernel(place, grads, acts, out, *, other, rows):
    order = acts.shape[1]
    tile = place[0] ^ other
    columns = pl.ds(pl.multiple_of(tile * order, order), order)
    term = dot(grads[:, columns], acts[...], (0, 0))
    for block in range(order // rows):
        start = pl.multiple_of((block ^ place[1]) * rows, rows)
        out[pl.ds(start, rows), :] = term[block * rows : (block + 1) * rows]


def gradient_term(place, grads, acts, other, rows):
    tokens, order = acts.shape
    return pl.pallas_call(
        functools.partial(term_kernel, other=other, rows=rows),
        out_shape=jax.ShapeDtypeStruct((order, order), F32),
        in_specs=[SMEM] + vmem(2),
        out_specs=vmem(1)[0],
        compiler_params=pltpu.CompilerParams(vmem_limit_bytes=16 << 20),
        cost_estimate=pl.CostEstimate(
            flops=2 * tokens * order * order, bytes_accessed=4 * tokens * order, transcendentals=0
        ),
        name="gradient_term",
    )(place, grads, acts)


def on_diagonal(rows, columns, start):
    row = lax.broadcasted_iota(jnp.int32, (rows, columns), 0) + start
    return lax.broadcasted_iota(jnp.int32, (rows, columns), 1) == row


def pack_kernel(place, stats, keep, send, *, tiles):
    rows, order = stats.shape[1:]
    diagonal = on_diagonal(rows, order, place[3])
    for out, other in ((keep, 0), (send, 1)):
        extra = []
        for side in range(2):
            values = stats[side * tiles + (place[0] ^ other)]
            high = values.astype(BF16)
            out[side * rows : (side + 1) * rows, :] = high
            rest = values - high.astype(F32)
            rest = jnp.sum(jnp.where(diagonal, rest, 0.0), axis=0, keepdims=True)
            middle = rest.astype(BF16).astype(F32)
            extra += [middle, rest - middle]
        row = lax.broadcasted_iota(jnp.int32, (TILE, order), 0)
        tail = jnp.zeros((TILE, order), F32)
        for index, vector in enumerate(extra):
            tail = jnp.where(row == index, vector, tail)
        out[2 * rows :, :] = tail.astype(BF16)


def unpack_kernel(place, *refs, rows):
    parts, out = refs[:-1], refs[-1]
    order = out.shape[2]
    height = 2 * rows + TILE
    vectors = [jnp.full((1, order), DAMPING, F32) for _ in range(2)]
    for part in parts:
        for core in range(2):
            tail = part[core * height + 2 * rows : (core + 1) * height, :].astype(F32)
            for side in range(2):
                vectors[side] += tail[2 * side : 2 * side + 1] + tail[2 * side + 1 : 2 * side + 2]
    for index, part in enumerate(parts):
        for core in range(2):
            start = ((place[2] ^ index) * 2 + (place[0] ^ core)) * rows
            start = pl.multiple_of(start, rows)
            diagonal = on_diagonal(rows, order, start)
            for side in range(2):
                low = core * height + side * rows
                values = part[low : low + rows, :].astype(F32)
                out[side, pl.ds(start, rows), :] = values + jnp.where(diagonal, vectors[side], 0.0)


def step_kernel(place, damped, *refs, pieces, rows, band):
    parts = refs[:pieces]
    own, sent, grad, gram, scaled, power, factors, offs, seconds, left_root, right_rows = refs[pieces:]
    order = grad.shape[0]
    for index, part in enumerate(parts):
        for low in range(0, part.shape[0], rows):
            block = (index * part.shape[0] + low) // rows
            start = pl.multiple_of((block ^ place[1]) * rows, rows)
            grad[pl.ds(start, rows), :] = part[low : low + rows, :]
    row_own = pl.ds(pl.multiple_of(place[3], band), band)
    row_sent = pl.ds(pl.multiple_of(place[4], band), band)
    step = min(order, 256)
    strips = [slice(low, low + step) for low in range(0, order, step)]
    eyes = [on_diagonal(step, order, low) for low in range(0, order, step)]
    sides = range(2)
    sums = [jnp.zeros((1, 1), F32) for _ in sides]
    for side in sides:
        gram[side] = dot(grad[...], grad[...], (side, side))
        for strip in strips:
            damp = gram[side, strip, :] + damped[side, strip, :]
            scaled[side, strip, :] = damp
            sums[side] += jnp.sum(damp * damp, keepdims=True)
        own[side] = gram[side, row_own, :]
        sent[side] = gram[side, row_sent, :]
    scales = [2.5 / jnp.sqrt(total) for total in sums]
    for side in sides:
        for strip, eye in zip(strips, eyes):
            iterate = scaled[side, strip, :] * scales[side]
            scaled[side, strip, :] = iterate
            factor = ((jnp.where(eye, 5.0, 0.0) - iterate) * 0.25).astype(BF16)
            factors[side, strip, :] = factor
            offs[side, strip, :] = (factor.astype(F32) - jnp.where(eye, 1.25, 0.0)).astype(BF16)
    across = [jnp.zeros((1, order), F32) for _ in sides]
    for side in sides:
        power[side] = dot(offs[side], offs[side])
        for strip, eye in zip(strips, eyes):
            value = power[side, strip, :] + 2.5 * offs[side, strip, :].astype(F32)
            power[side, strip, :] = value
            across[side] += jnp.sum(jnp.where(eye, value, 0.0), axis=0, keepdims=True)
            seconds[side, strip, :] = jnp.where(eye, 0.0, value).astype(BF16)
    beside = [jnp.zeros((1, order), F32) for _ in sides]
    for side in sides:
        gram[side] = dot(seconds[side], seconds[side])
        for strip, eye in zip(strips, eyes):
            value = power[side, strip, :]
            down = jnp.sum(jnp.where(eye, value, 0.0), axis=1, keepdims=True)
            value = gram[side, strip, :] + value * (3.125 + down + across[side]) - jnp.where(eye, down * down, 0.0)
            power[side, strip, :] = value
            beside[side] += jnp.sum(jnp.where(eye, value, 0.0), axis=0, keepdims=True)
            offs[side, strip, :] = jnp.where(eye, 0.0, value).astype(BF16)
            seconds[side, strip, :] = jnp.where(eye, 0.0, scaled[side, strip, :]).astype(BF16)
    for side in sides:
        gram[side] = dot(seconds[side], offs[side])
        for strip, eye in zip(strips, eyes):
            first, value = scaled[side, strip, :], power[side, strip, :]
            down = jnp.sum(jnp.where(eye, first, 0.0), axis=1, keepdims=True)
            iterate = gram[side, strip, :] + 2.44140625 * first + down * value
            iterate += jnp.where(eye, 0.0, first) * beside[side]
            factor = ((jnp.where(eye, 5.0, 0.0) - iterate) * 0.25).astype(BF16)
            offs[side, strip, :] = factor
    quarters = [jnp.sqrt(jnp.sqrt(scale)) for scale in scales]
    left_root[...] = (dot(factors[0], offs[0]) * quarters[0]).astype(BF16)
    right_rows[:band] = factors[1, row_own, :]
    right_rows[band:] = factors[1, row_sent, :]
    right_root = (dot(right_rows[...], offs[1]) * quarters[1]).astype(BF16)
    inner = dot(right_root, grad[...])
    high = inner.astype(BF16)
    low = (inner - high.astype(F32)).astype(BF16)
    update = (dot(high, left_root[...]) + dot(low, left_root[...])) * math.sqrt(order)
    own[2] = update[:band]
    sent[2] = update[band:]


def on_device(activations, out_grads, stats_old):
    order = activations.shape[1]
    tiles = out_grads.shape[1] // order
    band = stats_old.shape[1]
    rep, grp = lax.axis_index("rep"), lax.axis_index("grp")
    reps, lines = lax.axis_size("rep"), lax.axis_size("grp") // 2
    core, line = grp & 1, grp >> 1

    across, rows = plan("rep", 0, reps, order)
    along, rows = plan("grp", 1, lines, rows)
    steps = across + along
    here = jnp.int32(0)
    for axis, shift, radix, splits in steps:
        if splits:
            here = here * radix + ((lax.axis_index(axis) >> shift) & (radix - 1))
    place = jnp.stack([core, here, line, grp * band, (grp ^ 1) * band]).astype(jnp.int32)

    sent = gradient_term(place, out_grads, activations, 1, rows)
    sent = swap(sent, "grp", 1)
    total = gradient_term(place, out_grads, activations, 0, rows)

    packed = jax.ShapeDtypeStruct((2 * band + TILE, order), BF16)
    keep, send = pl.pallas_call(
        functools.partial(pack_kernel, tiles=tiles),
        out_shape=(packed, packed),
        in_specs=[SMEM] + vmem(1),
        out_specs=tuple(vmem(2)),
        compiler_params=pltpu.CompilerParams(vmem_limit_bytes=8 << 20),
        cost_estimate=pl.CostEstimate(flops=band * order * 20, bytes_accessed=band * order * 32, transcendentals=0),
        name="pack_stats",
    )(place, stats_old)
    packed = jnp.concatenate([keep, swap(send, "grp", 1)], axis=0)

    total = total + sent
    for axis, shift, radix, splits in across + along:
        if splits:
            total = total.reshape(radix, -1, order)
            parts = [swap(total[digit], axis, digit << shift) for digit in range(1, radix)]
            total = sum(parts, total[0])
        else:
            total = total + swap(total, axis, 1 << shift)
    stats = [packed]
    for digit in range(1, lines):
        stats.append(swap(packed, "grp", digit << 1))
    damped = pl.pallas_call(
        functools.partial(unpack_kernel, rows=band),
        out_shape=jax.ShapeDtypeStruct((2, order, order), F32),
        in_specs=[SMEM] + vmem(len(stats)),
        out_specs=vmem(1)[0],
        compiler_params=pltpu.CompilerParams(vmem_limit_bytes=16 << 20),
        cost_estimate=pl.CostEstimate(flops=order * order * 8, bytes_accessed=order * order * 12, transcendentals=0),
        name="unpack_stats",
    )(place, *stats)

    pieces = [total.astype(BF16)]
    for axis, shift, radix, splits in reversed(steps):
        if splits:
            whole = pieces[0] if len(pieces) == 1 else jnp.concatenate(pieces, axis=0)
            pieces = [whole] + [swap(whole, axis, digit << shift) for digit in range(1, radix)]

    result = jax.ShapeDtypeStruct((3, band, order), F32)
    square = (2, order, order)
    own, sent = pl.pallas_call(
        functools.partial(step_kernel, pieces=len(pieces), rows=rows, band=band),
        out_shape=(result, result),
        in_specs=[SMEM] + vmem(1 + len(pieces)),
        out_specs=tuple(vmem(2)),
        scratch_shapes=[
            pltpu.VMEM((order, order), BF16),
            pltpu.VMEM(square, F32),
            pltpu.VMEM(square, F32),
            pltpu.VMEM(square, F32),
            pltpu.VMEM(square, BF16),
            pltpu.VMEM(square, BF16),
            pltpu.VMEM(square, BF16),
            pltpu.VMEM((order, order), BF16),
            pltpu.VMEM((2 * band, order), BF16),
        ],
        compiler_params=pltpu.CompilerParams(vmem_limit_bytes=32 << 20),
        cost_estimate=pl.CostEstimate(flops=20 * order**3, bytes_accessed=order * order * 16, transcendentals=0),
        name="precondition",
    )(place, damped, *pieces)
    sent = swap(sent, "grp", 1)
    first = core == 0
    low, high = jnp.where(first, own, sent), jnp.where(first, sent, own)
    stats_new = stats_old + jnp.stack([low[0], high[0], low[1], high[1]])
    return stats_new, jnp.stack([low[2], high[2]])


def solution(mesh):
    in_specs = (P(("rep", "grp"), None), P(("rep", "grp"), None), P(None, "grp", None))
    out_specs = (P(None, "grp", None), P(None, "grp", None))
    return jax.shard_map(
        on_device, mesh=mesh, in_specs=in_specs, out_specs=out_specs, check_vma=False
    )
```

time: 186 us -> 80.3 us (0.43)
  waiting for transfers between devices: 114 us -> 42.8 us
  blocking collectives: 36.6 us -> 0 us
  starting transfers between devices: 0.16 us -> 23.4 us
  matrix products: 15.5 us -> 0 us
  between operations: 13.9 us -> 0.77 us
  Pallas kernels: 0 us -> 8.63 us
  local copies, waits for them, and re-layouts: 4.43 us -> 2.53 us
    all_gather x3 -> x0, waiting for transfers between devices: 75.2 us -> none  [the longest x2 55.9 us: on_device(): newton_whole_factor = lax.all_gather(factor, 'grp', axis=1, tiled=True)]
    ppermute x0 -> x18, waiting for transfers between devices: none -> 42.8 us  [swap(): return lax.ppermute(array, axis, [(i, i ^ mask) for i in range(size)])]
    reduce_scatter x1 -> x0, waiting for transfers between devices: 38.6 us -> none  [on_device(): lax.psum_scatter(term_rows.reshape(rows_dev * lax.axis_size('grp'), tile_...]
    psum x2 -> x0, blocking collectives: 36.6 us -> none  [the longest x1 21.2 us: on_device(): summed = lax.psum(partial_rows, 'rep')]
    ppermute x0 -> x18, starting transfers between devices: none -> 23.4 us  [swap(): return lax.ppermute(array, axis, [(i, i ^ mask) for i in range(size)])]
    dot_general x11 -> x0, matrix products: 15.5 us -> none  [the longest x4 7.3 us: on_device(): jnp.einsum('crb,cbd->crd', iterate, upcast, precision=lax.Precision.HIGHEST)]
    pallas_call x0 -> x5, Pallas kernels: none -> 8.63 us  [the longest x1 4.97 us: on_device(): pl.pallas_call(functools.partial(step_kernel, pieces=len(pieces), rows=ro...]
  transfers between devices with their start and end apart: 4 -> 18, of which waited for: 4 -> 11; matrix products, arithmetic and copies ran while one was open for 0% -> 0% of each run, Pallas kernels for 0% -> 3%
where the time goes in v1:
time: 80.3 us; the launch traced here: 80.1 us
  waiting for transfers between devices  42.8 us (53%)
  starting transfers between devices  23.4 us (29%)
  Pallas kernels  8.63 us (11%)
  local copies, waits for them, and re-layouts  2.53 us (3%)
  other arithmetic  2.03 us (3%)
    ppermute x18, waiting for transfers between devices, swap(): return lax.ppermute(array, axis, [(i, i ^ mask) for i in range(size)])  42.8 us
    ppermute x18, starting transfers between devices, swap(): return lax.ppermute(array, axis, [(i, i ^ mask) for i in range(size)])  23.4 us
    pallas_call x1, Pallas kernels, on_device(): pl.pallas_call(functools.partial(step_kernel, pieces=len(pieces), rows=ro...  4.97 us
    unnamed x7, local copies, waits for them, and re-layouts  2.28 us
    pallas_call x2, Pallas kernels, gradient_term(): pl.pallas_call(functools.partial(term_kernel, other=other, rows=rows), ou...  2.03 us
  transfers between devices with their start and end apart: 18, of which 11 were waited for; matrix products, arithmetic and copies ran while one was open for 0% of the time, Pallas kernels for 3%

profile of v1, /device:TPU:0, one launch (start us, length us, event | category | flops | bytes accessed | tf_op | source)
XLA Modules:
  0.0 80.1 jit_solution(17044045545531176626)
XLA Ops:
  0.7 1.2 %copy-done = bf16[512,1024]{1,0:T(8,128)(2,1)S(1)} copy-done((bf16[512,1024]{1,0:T(8,128)(2,1)S(1)}, bf16[512,1024]{1,0:T(8,128)(2,1)}, u32[]{:S(2)}) %copy-start) | copy-done | bytes 1048600
  2.0 1.0 %copy-done.2 = bf16[512,512]{1,0:T(8,128)(2,1)S(1)} copy-done((bf16[512,512]{1,0:T(8,128)(2,1)S(1)}, bf16[512,512]{1,0:T(8,128)(2,1)}, u32[]{:S(2)}) %copy-start.2) | copy-done | bytes 524312
  3.0 1.0 %gradient_term.3 = f32[512,512]{1,0:T(8,128)S(1)} custom-call(s32[5]{0:T(128)S(1)} %stack.29.place, bf16[512,1024]{1,0:T(8,128)(2,1)S(1)} %copy-done, bf16[512,512]{1,0:T(8,128)(2,1)S(1)} %copy-done.2), custom_call_target="tpu_custom_call" | custom-call | flops 268435456 | bytes 1048576 | tf_op jit(solution)/shard_map/gradient_term/pallas_call | solution.py:63
  4.0 0.5 collective-permute-start.4
  4.5 1.0 %gradient_term.2 = f32[512,512]{1,0:T(8,128)S(1)} custom-call(s32[5]{0:T(128)S(1)} %stack.29.place, bf16[512,1024]{1,0:T(8,128)(2,1)S(1)} %copy-done, bf16[512,512]{1,0:T(8,128)(2,1)S(1)} %copy-done.2), custom_call_target="tpu_custom_call" | custom-call | flops 268435456 | bytes 1048576 | tf_op jit(solution)/shard_map/gradient_term/pallas_call | solution.py:63
  5.6 1.3 %collective-permute-done.4 = f32[512,512]{1,0:T(8,128)S(1)} collective-permute-done((f32[512,512]{1,0:T(8,128)S(1)}, f32[512,512]{1,0:T(8,128)S(1)}, u32[]{:S(2)}, u32[]{:S(2)}) %collective-permute-start.4) | collective-permute-done | bytes 1048608 | tf_op jit(solution)/shard_map/ppermute | solution.py:20
  7.1 2.9 %collective-permute-start.5 = (f32[128,512]{1,0:T(8,128)S(1)}, f32[128,512]{1,0:T(8,128)S(1)}, u32[]{:S(2)}, u32[]{:S(2)}) collective-permute-start(f32[128,512]{1,0:T(8,128)S(1)} %get-tuple-element.10), channel_id=1, source_target_pairs={{0,8},{8,0},{16,24},{24,16},{1,9},{9,1},{17,25},{25,17},{2,10},{10... | collective-permute-start | bytes 786440 | tf_op jit(solution)/shard_map/ppermute | solution.py:20
  10.0 1.5 %collective-permute-start.6 = (f32[128,512]{1,0:T(8,128)S(1)}, f32[128,512]{1,0:T(8,128)S(1)}, u32[]{:S(2)}, u32[]{:S(2)}) collective-permute-start(f32[128,512]{1,0:T(8,128)S(1)} %get-tuple-element.12), channel_id=1, source_target_pairs={{0,16},{8,24},{16,0},{24,8},{1,17},{9,25},{17,1},{25,9},{2,18},{10... | collective-permute-start | bytes 786440 | tf_op jit(solution)/shard_map/ppermute | solution.py:20
  11.6 0.7 pack_stats.1
  12.3 4.8 %collective-permute-done.5 = f32[128,512]{1,0:T(8,128)S(1)} collective-permute-done((f32[128,512]{1,0:T(8,128)S(1)}, f32[128,512]{1,0:T(8,128)S(1)}, u32[]{:S(2)}, u32[]{:S(2)}) %collective-permute-start.5) | collective-permute-done | bytes 262176 | tf_op jit(solution)/shard_map/ppermute | solution.py:20
  17.1 6.6 %collective-permute-done.6 = f32[128,512]{1,0:T(8,128)S(1)} collective-permute-done((f32[128,512]{1,0:T(8,128)S(1)}, f32[128,512]{1,0:T(8,128)S(1)}, u32[]{:S(2)}, u32[]{:S(2)}) %collective-permute-start.6) | collective-permute-done | bytes 262176 | tf_op jit(solution)/shard_map/ppermute | solution.py:20
  23.8 3.7 %collective-permute-start.10 = (f32[32,512]{1,0:T(8,128)S(1)}, f32[32,512]{1,0:T(8,128)S(1)}, u32[]{:S(2)}, u32[]{:S(2)}) collective-permute-start(f32[32,512]{1,0:T(8,128)S(1)} %get-tuple-element.22), channel_id=1, source_target_pairs={{0,6},{1,7},{2,4},{3,5},{4,2},{5,3},{6,0},{7,1},{8,14},{9,15},{10,... | collective-permute-start | bytes 196616 | tf_op jit(solution)/shard_map/ppermute | solution.py:20
  27.5 0.8 collective-permute-start.9
  28.3 1.3 %collective-permute-start.1 = (bf16[288,512]{1,0:T(8,128)(2,1)S(1)}, bf16[288,512]{1,0:T(8,128)(2,1)S(1)}, u32[]{:S(2)}, u32[]{:S(2)}) collective-permute-start(bf16[288,512]{1,0:T(8,128)(2,1)S(1)} %constant_dynamic-update-slice_fusion.refs_0_), channel_id=1, source_target_pairs={{0,2},{1,3},{2,0},{3,1},{4,6},{5,7},{6,4},{7,5},{8,10},{9,11},{10,... | collective-permute-start | bytes 884744 | tf_op jit(solution)/shard_map/ppermute | solution.py:20
  30.1 3.2 %collective-permute-done.8 = f32[32,512]{1,0:T(8,128)S(1)} collective-permute-done((f32[32,512]{1,0:T(8,128)S(1)}, f32[32,512]{1,0:T(8,128)S(1)}, u32[]{:S(2)}, u32[]{:S(2)}) %collective-permute-start.8) | collective-permute-done | bytes 65568 | tf_op jit(solution)/shard_map/ppermute | solution.py:20
  33.3 2.3 %collective-permute-start.11 = (bf16[32,512]{1,0:T(8,128)(2,1)S(1)}, bf16[32,512]{1,0:T(8,128)(2,1)S(1)}, u32[]{:S(2)}, u32[]{:S(2)}) collective-permute-start(bf16[32,512]{1,0:T(8,128)(2,1)S(1)} %fusion.4), channel_id=1, source_target_pairs={{0,2},{1,3},{2,0},{3,1},{4,6},{5,7},{6,4},{7,5},{8,10},{9,11},{10,... | collective-permute-start | bytes 98312 | tf_op jit(solution)/shard_map/ppermute | solution.py:20
  35.5 0.9 %collective-permute-start.2 = (bf16[288,512]{1,0:T(8,128)(2,1)S(1)}, bf16[288,512]{1,0:T(8,128)(2,1)S(1)}, u32[]{:S(2)}, u32[]{:S(2)}) collective-permute-start(bf16[288,512]{1,0:T(8,128)(2,1)S(1)} %constant_dynamic-update-slice_fusion.refs_0_), channel_id=1, source_target_pairs={{0,4},{1,5},{2,6},{3,7},{4,0},{5,1},{6,2},{7,3},{8,12},{9,13},{10,... | collective-permute-start | bytes 884744 | tf_op jit(solution)/shard_map/ppermute | solution.py:20
  36.4 1.6 %collective-permute-start.3 = (bf16[288,512]{1,0:T(8,128)(2,1)S(1)}, bf16[288,512]{1,0:T(8,128)(2,1)S(1)}, u32[]{:S(2)}, u32[]{:S(2)}) collective-permute-start(bf16[288,512]{1,0:T(8,128)(2,1)S(1)} %constant_dynamic-update-slice_fusion.refs_0_), channel_id=1, source_target_pairs={{0,6},{1,7},{2,4},{3,5},{4,2},{5,3},{6,0},{7,1},{8,14},{9,15},{10,... | collective-permute-start | bytes 884744 | tf_op jit(solution)/shard_map/ppermute | solution.py:20
  38.0 1.8 %collective-permute-start.12 = (bf16[32,512]{1,0:T(8,128)(2,1)S(1)}, bf16[32,512]{1,0:T(8,128)(2,1)S(1)}, u32[]{:S(2)}, u32[]{:S(2)}) collective-permute-start(bf16[32,512]{1,0:T(8,128)(2,1)S(1)} %fusion.4), channel_id=1, source_target_pairs={{0,4},{1,5},{2,6},{3,7},{4,0},{5,1},{6,2},{7,3},{8,12},{9,13},{10,... | collective-permute-start | bytes 98312 | tf_op jit(solution)/shard_map/ppermute | solution.py:20
  39.8 3.1 %collective-permute-done.11 = bf16[32,512]{1,0:T(8,128)(2,1)S(1)} collective-permute-done((bf16[32,512]{1,0:T(8,128)(2,1)S(1)}, bf16[32,512]{1,0:T(8,128)(2,1)S(1)}, u32[]{:S(2)}, u32[]{:S(2)}) %collective-permute-start.11) | collective-permute-done | bytes 32800 | tf_op jit(solution)/shard_map/ppermute | solution.py:20
  42.9 2.4 %collective-permute-start.13 = (bf16[32,512]{1,0:T(8,128)(2,1)S(1)}, bf16[32,512]{1,0:T(8,128)(2,1)S(1)}, u32[]{:S(2)}, u32[]{:S(2)}) collective-permute-start(bf16[32,512]{1,0:T(8,128)(2,1)S(1)} %fusion.4), channel_id=1, source_target_pairs={{0,6},{1,7},{2,4},{3,5},{4,2},{5,3},{6,0},{7,1},{8,14},{9,15},{10,... | collective-permute-start | bytes 98312 | tf_op jit(solution)/shard_map/ppermute | solution.py:20
  45.3 18.4 %collective-permute-done.12 = bf16[32,512]{1,0:T(8,128)(2,1)S(1)} collective-permute-done((bf16[32,512]{1,0:T(8,128)(2,1)S(1)}, bf16[32,512]{1,0:T(8,128)(2,1)S(1)}, u32[]{:S(2)}, u32[]{:S(2)}) %collective-permute-start.12) | collective-permute-done | bytes 32800 | tf_op jit(solution)/shard_map/ppermute | solution.py:20
  63.7 1.5 %collective-permute-start.14 = (bf16[128,512]{1,0:T(8,128)(2,1)S(1)}, bf16[128,512]{1,0:T(8,128)(2,1)S(1)}, u32[]{:S(2)}, u32[]{:S(2)}) collective-permute-start(bf16[128,512]{1,0:T(8,128)(2,1)S(1)} %pad_maximum_fusion.1.refs_0_), channel_id=1, source_target_pairs={{0,8},{8,0},{16,24},{24,16},{1,9},{9,1},{17,25},{25,17},{2,10},{10... | collective-permute-start | bytes 393224 | tf_op jit(solution)/shard_map/ppermute | solution.py:20
  65.2 0.5 collective-permute-start.15
  65.7 1.6 %collective-permute-start.16 = (bf16[128,512]{1,0:T(8,128)(2,1)S(1)}, bf16[128,512]{1,0:T(8,128)(2,1)S(1)}, u32[]{:S(2)}, u32[]{:S(2)}) collective-permute-start(bf16[128,512]{1,0:T(8,128)(2,1)S(1)} %pad_maximum_fusion.1.refs_0_), channel_id=1, source_target_pairs={{0,24},{8,16},{16,8},{24,0},{1,25},{9,17},{17,9},{25,1},{2,26},{10... | collective-permute-start | bytes 393224 | tf_op jit(solution)/shard_map/ppermute | solution.py:20
  67.3 1.0 %unpack_stats.1.damped = f32[2,512,512]{2,1,0:T(8,128)S(1)} custom-call(s32[5]{0:T(128)S(1)} %stack.29.place, bf16[288,512]{1,0:T(8,128)(2,1)S(1)} %constant_dynamic-update-slice_fusion.refs_0_, bf16[288,512]{1,0:T(8,128)(2,1)S(1)} %collective-permute-done.1.refs_1_, bf16[288,512]{1,0:T(8,128)(2,1)S(1)} %collective-permute-done.2.refs_2_, ...), custom_call_target="tpu_custom_call" | custom-call | flops 2097152 | bytes 3145728 | tf_op jit(solution)/shard_map/unpack_stats/pallas_call | solution.py:239
  68.8 1.4 %collective-permute-done.15.refs_2_ = bf16[128,512]{1,0:T(8,128)(2,1)S(1)} collective-permute-done((bf16[128,512]{1,0:T(8,128)(2,1)S(1)}, bf16[128,512]{1,0:T(8,128)(2,1)S(1)}, u32[]{:S(2)}, u32[]{:S(2)}) %collective-permute-start.15) | collective-permute-done | bytes 131104 | tf_op jit(solution)/shard_map/ppermute | solution.py:20
  70.1 1.4 %collective-permute-done.16.refs_3_ = bf16[128,512]{1,0:T(8,128)(2,1)S(1)} collective-permute-done((bf16[128,512]{1,0:T(8,128)(2,1)S(1)}, bf16[128,512]{1,0:T(8,128)(2,1)S(1)}, u32[]{:S(2)}, u32[]{:S(2)}) %collective-permute-start.16) | collective-permute-done | bytes 131104 | tf_op jit(solution)/shard_map/ppermute | solution.py:20
  71.6 5.0 %precondition.1 = (f32[3,64,512]{2,1,0:T(8,128)S(1)}, f32[3,64,512]{2,1,0:T(8,128)S(1)}) custom-call(s32[5]{0:T(128)S(1)} %stack.29.place, f32[2,512,512]{2,1,0:T(8,128)S(1)} %unpack_stats.1.damped, bf16[128,512]{1,0:T(8,128)(2,1)S(1)} %pad_maximum_fusion.1.refs_0_, bf16[128,512]{1,0:T(8,128)(2,1)S(1)} %collective-permute-done.14.refs_1_, ...), custom_call_target="tpu_custom_call" | custom-call | flops 2684354560 | bytes 4194304 | tf_op jit(solution)/shard_map/precondition/pallas_call | solution.py:257
  76.6 1.7 %collective-permute-done.17 = f32[3,64,512]{2,1,0:T(8,128)S(1)} collective-permute-done((f32[3,64,512]{2,1,0:T(8,128)S(1)}, f32[3,64,512]{2,1,0:T(8,128)S(1)}, u32[]{:S(2)}, u32[]{:S(2)}) %collective-permute-start.17) | collective-permute-done | bytes 393248 | tf_op jit(solution)/shard_map/ppermute | solution.py:20
  78.5 0.7 pad_maximum_fusion
  79.2 0.9 %maximum_add_fusion = f32[4,64,512]{2,1,0:T(8,128)} fusion(f32[4,64,512]{2,1,0:T(8,128)S(1)} %copy-done.1, f32[1,64,512]{2,1,0:T(8,128)S(1)} %get-tuple-element.25, f32[1,64,512]{2,1,0:T(8,128)S(1)} %get-tuple-element.16, f32[1,64,512]{2,1,0:T(8,128)S(1)} %get-tuple-element.24, f32[1,64,512]{2,1,0:T(8,128)S(1)} %get-tuple-element.17), kind=kLoop, calls=%fused_computation | loop fusion | flops 524288 | bytes 1572864 | tf_op jit(solution)/shard_map/add | solution.py:280
  (28 shorter events, 1.8 us)
Async XLA Ops:
  0.7 1.2 %copy-start = (bf16[512,1024]{1,0:T(8,128)(2,1)S(1)}, bf16[512,1024]{1,0:T(8,128)(2,1)}, u32[]{:S(2)}) copy-start(bf16[512,1024]{1,0:T(8,128)(2,1)} %grads.3) | copy-start | bytes 3145732
  2.0 1.0 %copy-start.2 = (bf16[512,512]{1,0:T(8,128)(2,1)S(1)}, bf16[512,512]{1,0:T(8,128)(2,1)}, u32[]{:S(2)}) copy-start(bf16[512,512]{1,0:T(8,128)(2,1)} %acts.3) | copy-start | bytes 1572868
  4.0 2.8 %collective-permute-start.4 = (f32[512,512]{1,0:T(8,128)S(1)}, f32[512,512]{1,0:T(8,128)S(1)}, u32[]{:S(2)}, u32[]{:S(2)}) collective-permute-start(f32[512,512]{1,0:T(8,128)S(1)} %gradient_term.3), channel_id=1, source_target_pairs={{0,1},{1,0},{2,3},{3,2},{4,5},{5,4},{6,7},{7,6},{8,9},{9,8},{10,11... | collective-permute-start | bytes 3145736 | tf_op jit(solution)/shard_map/ppermute | solution.py:20
  5.5 6.0 %copy-start.1 = (f32[4,64,512]{2,1,0:T(8,128)S(1)}, f32[4,64,512]{2,1,0:T(8,128)}, u32[]{:S(2)}) copy-start(f32[4,64,512]{2,1,0:T(8,128)} %stats.1) | copy-start | bytes 1572868
  7.1 10.0 %collective-permute-start.5 = (f32[128,512]{1,0:T(8,128)S(1)}, f32[128,512]{1,0:T(8,128)S(1)}, u32[]{:S(2)}, u32[]{:S(2)}) collective-permute-start(f32[128,512]{1,0:T(8,128)S(1)} %get-tuple-element.10), channel_id=1, source_target_pairs={{0,8},{8,0},{16,24},{24,16},{1,9},{9,1},{17,25},{25,17},{2,10},{10... | collective-permute-start | bytes 786440 | tf_op jit(solution)/shard_map/ppermute | solution.py:20
  10.0 13.7 %collective-permute-start.6 = (f32[128,512]{1,0:T(8,128)S(1)}, f32[128,512]{1,0:T(8,128)S(1)}, u32[]{:S(2)}, u32[]{:S(2)}) collective-permute-start(f32[128,512]{1,0:T(8,128)S(1)} %get-tuple-element.12), channel_id=1, source_target_pairs={{0,16},{8,24},{16,0},{24,8},{1,17},{9,25},{17,1},{25,9},{2,18},{10... | collective-permute-start | bytes 786440 | tf_op jit(solution)/shard_map/ppermute | solution.py:20
  11.5 12.2 %collective-permute-start.7 = (f32[128,512]{1,0:T(8,128)S(1)}, f32[128,512]{1,0:T(8,128)S(1)}, u32[]{:S(2)}, u32[]{:S(2)}) collective-permute-start(f32[128,512]{1,0:T(8,128)S(1)} %get-tuple-element.11), channel_id=1, source_target_pairs={{0,24},{8,16},{16,8},{24,0},{1,25},{9,17},{17,9},{25,1},{2,26},{10... | collective-permute-start | bytes 786440 | tf_op jit(solution)/shard_map/ppermute | solution.py:20
  12.2 16.0 %collective-permute-start = (bf16[144,512]{1,0:T(8,128)(2,1)S(1)}, bf16[144,512]{1,0:T(8,128)(2,1)S(1)}, u32[]{:S(2)}, u32[]{:S(2)}) collective-permute-start(bf16[144,512]{1,0:T(8,128)(2,1)S(1)} %get-tuple-element.7), channel_id=1, source_target_pairs={{0,1},{1,0},{2,3},{3,2},{4,5},{5,4},{6,7},{7,6},{8,9},{9,8},{10,11... | collective-permute-start | bytes 442376 | tf_op jit(solution)/shard_map/ppermute | solution.py:20
  23.8 6.2 %collective-permute-start.10 = (f32[32,512]{1,0:T(8,128)S(1)}, f32[32,512]{1,0:T(8,128)S(1)}, u32[]{:S(2)}, u32[]{:S(2)}) collective-permute-start(f32[32,512]{1,0:T(8,128)S(1)} %get-tuple-element.22), channel_id=1, source_target_pairs={{0,6},{1,7},{2,4},{3,5},{4,2},{5,3},{6,0},{7,1},{8,14},{9,15},{10,... | collective-permute-start | bytes 196616 | tf_op jit(solution)/shard_map/ppermute | solution.py:20
  27.5 5.7 %collective-permute-start.8 = (f32[32,512]{1,0:T(8,128)S(1)}, f32[32,512]{1,0:T(8,128)S(1)}, u32[]{:S(2)}, u32[]{:S(2)}) collective-permute-start(f32[32,512]{1,0:T(8,128)S(1)} %get-tuple-element.21), channel_id=1, source_target_pairs={{0,2},{1,3},{2,0},{3,1},{4,6},{5,7},{6,4},{7,5},{8,10},{9,11},{10,... | collective-permute-start | bytes 196616 | tf_op jit(solution)/shard_map/ppermute | solution.py:20
  27.5 5.7 %collective-permute-start.9 = (f32[32,512]{1,0:T(8,128)S(1)}, f32[32,512]{1,0:T(8,128)S(1)}, u32[]{:S(2)}, u32[]{:S(2)}) collective-permute-start(f32[32,512]{1,0:T(8,128)S(1)} %get-tuple-element.23), channel_id=1, source_target_pairs={{0,4},{1,5},{2,6},{3,7},{4,0},{5,1},{6,2},{7,3},{8,12},{9,13},{10,... | collective-permute-start | bytes 196616 | tf_op jit(solution)/shard_map/ppermute | solution.py:20
  28.3 37.4 %collective-permute-start.1 = (bf16[288,512]{1,0:T(8,128)(2,1)S(1)}, bf16[288,512]{1,0:T(8,128)(2,1)S(1)}, u32[]{:S(2)}, u32[]{:S(2)}) collective-permute-start(bf16[288,512]{1,0:T(8,128)(2,1)S(1)} %constant_dynamic-update-slice_fusion.refs_0_), channel_id=1, source_target_pairs={{0,2},{1,3},{2,0},{3,1},{4,6},{5,7},{6,4},{7,5},{8,10},{9,11},{10,... | collective-permute-start | bytes 884744 | tf_op jit(solution)/shard_map/ppermute | solution.py:20
  33.3 9.6 %collective-permute-start.11 = (bf16[32,512]{1,0:T(8,128)(2,1)S(1)}, bf16[32,512]{1,0:T(8,128)(2,1)S(1)}, u32[]{:S(2)}, u32[]{:S(2)}) collective-permute-start(bf16[32,512]{1,0:T(8,128)(2,1)S(1)} %fusion.4), channel_id=1, source_target_pairs={{0,2},{1,3},{2,0},{3,1},{4,6},{5,7},{6,4},{7,5},{8,10},{9,11},{10,... | collective-permute-start | bytes 98312 | tf_op jit(solution)/shard_map/ppermute | solution.py:20
  35.5 31.7 %collective-permute-start.2 = (bf16[288,512]{1,0:T(8,128)(2,1)S(1)}, bf16[288,512]{1,0:T(8,128)(2,1)S(1)}, u32[]{:S(2)}, u32[]{:S(2)}) collective-permute-start(bf16[288,512]{1,0:T(8,128)(2,1)S(1)} %constant_dynamic-update-slice_fusion.refs_0_), channel_id=1, source_target_pairs={{0,4},{1,5},{2,6},{3,7},{4,0},{5,1},{6,2},{7,3},{8,12},{9,13},{10,... | collective-permute-start | bytes 884744 | tf_op jit(solution)/shard_map/ppermute | solution.py:20
  36.4 30.9 %collective-permute-start.3 = (bf16[288,512]{1,0:T(8,128)(2,1)S(1)}, bf16[288,512]{1,0:T(8,128)(2,1)S(1)}, u32[]{:S(2)}, u32[]{:S(2)}) collective-permute-start(bf16[288,512]{1,0:T(8,128)(2,1)S(1)} %constant_dynamic-update-slice_fusion.refs_0_), channel_id=1, source_target_pairs={{0,6},{1,7},{2,4},{3,5},{4,2},{5,3},{6,0},{7,1},{8,14},{9,15},{10,... | collective-permute-start | bytes 884744 | tf_op jit(solution)/shard_map/ppermute | solution.py:20
  38.0 25.7 %collective-permute-start.12 = (bf16[32,512]{1,0:T(8,128)(2,1)S(1)}, bf16[32,512]{1,0:T(8,128)(2,1)S(1)}, u32[]{:S(2)}, u32[]{:S(2)}) collective-permute-start(bf16[32,512]{1,0:T(8,128)(2,1)S(1)} %fusion.4), channel_id=1, source_target_pairs={{0,4},{1,5},{2,6},{3,7},{4,0},{5,1},{6,2},{7,3},{8,12},{9,13},{10,... | collective-permute-start | bytes 98312 | tf_op jit(solution)/shard_map/ppermute | solution.py:20
  42.9 20.8 %collective-permute-start.13 = (bf16[32,512]{1,0:T(8,128)(2,1)S(1)}, bf16[32,512]{1,0:T(8,128)(2,1)S(1)}, u32[]{:S(2)}, u32[]{:S(2)}) collective-permute-start(bf16[32,512]{1,0:T(8,128)(2,1)S(1)} %fusion.4), channel_id=1, source_target_pairs={{0,6},{1,7},{2,4},{3,5},{4,2},{5,3},{6,0},{7,1},{8,14},{9,15},{10,... | collective-permute-start | bytes 98312 | tf_op jit(solution)/shard_map/ppermute | solution.py:20
  63.7 5.0 %collective-permute-start.14 = (bf16[128,512]{1,0:T(8,128)(2,1)S(1)}, bf16[128,512]{1,0:T(8,128)(2,1)S(1)}, u32[]{:S(2)}, u32[]{:S(2)}) collective-permute-start(bf16[128,512]{1,0:T(8,128)(2,1)S(1)} %pad_maximum_fusion.1.refs_0_), channel_id=1, source_target_pairs={{0,8},{8,0},{16,24},{24,16},{1,9},{9,1},{17,25},{25,17},{2,10},{10... | collective-permute-start | bytes 393224 | tf_op jit(solution)/shard_map/ppermute | solution.py:20
  65.2 5.0 %collective-permute-start.15 = (bf16[128,512]{1,0:T(8,128)(2,1)S(1)}, bf16[128,512]{1,0:T(8,128)(2,1)S(1)}, u32[]{:S(2)}, u32[]{:S(2)}) collective-permute-start(bf16[128,512]{1,0:T(8,128)(2,1)S(1)} %pad_maximum_fusion.1.refs_0_), channel_id=1, source_target_pairs={{0,16},{8,24},{16,0},{24,8},{1,17},{9,25},{17,1},{25,9},{2,18},{10... | collective-permute-start | bytes 393224 | tf_op jit(solution)/shard_map/ppermute | solution.py:20
  65.7 5.9 %collective-permute-start.16 = (bf16[128,512]{1,0:T(8,128)(2,1)S(1)}, bf16[128,512]{1,0:T(8,128)(2,1)S(1)}, u32[]{:S(2)}, u32[]{:S(2)}) collective-permute-start(bf16[128,512]{1,0:T(8,128)(2,1)S(1)} %pad_maximum_fusion.1.refs_0_), channel_id=1, source_target_pairs={{0,24},{8,16},{16,8},{24,0},{1,25},{9,17},{17,9},{25,1},{2,26},{10... | collective-permute-start | bytes 393224 | tf_op jit(solution)/shard_map/ppermute | solution.py:20
  76.5 1.8 %collective-permute-start.17 = (f32[3,64,512]{2,1,0:T(8,128)S(1)}, f32[3,64,512]{2,1,0:T(8,128)S(1)}, u32[]{:S(2)}, u32[]{:S(2)}) collective-permute-start(f32[3,64,512]{2,1,0:T(8,128)S(1)} %get-tuple-element.9), channel_id=1, source_target_pairs={{0,1},{1,0},{2,3},{3,2},{4,5},{5,4},{6,7},{7,6},{8,9},{9,8},{10,11... | collective-permute-start | bytes 1179656 | tf_op jit(solution)/shard_map/ppermute | solution.py:20

commit v2 on v1

--- a/solution.py
+++ b/solution.py
@@ -12,6 +12,7 @@
 BF16 = jnp.bfloat16
 DAMPING = 0.01
 TILE = 16
+LANES = 128
 RADIX = 4
 
 
@@ -78,45 +79,99 @@
     return lax.broadcasted_iota(jnp.int32, (rows, columns), 1) == row
 
 
-def pack_kernel(place, stats, keep, send, *, tiles):
+def halves_of(lines):
+    others = lines - 1
+    return {
+        digit: [other for other in range(1, lines) if 0 < (other - digit) % others <= (others - 1) // 2]
+        for digit in range(1, lines)
+    }
+
+
+def stage_kernel(place, stats, whole, *outs, tiles, lines):
     rows, order = stats.shape[1:]
+    width = order // lines
+    height = 2 * rows + TILE
     diagonal = on_diagonal(rows, order, place[3])
-    for out, other in ((keep, 0), (send, 1)):
-        extra = []
+    row = lax.broadcasted_iota(jnp.int32, (TILE, order), 0)
+    for other in range(2):
+        tail = jnp.zeros((TILE, order), F32)
         for side in range(2):
             values = stats[side * tiles + (place[0] ^ other)]
             high = values.astype(BF16)
-            out[side * rows : (side + 1) * rows, :] = high
+            low = other * height + side * rows
+            whole[low : low + rows, :] = high
             rest = values - high.astype(F32)
             rest = jnp.sum(jnp.where(diagonal, rest, 0.0), axis=0, keepdims=True)
             middle = rest.astype(BF16).astype(F32)
-            extra += [middle, rest - middle]
-        row = lax.broadcasted_iota(jnp.int32, (TILE, order), 0)
-        tail = jnp.zeros((TILE, order), F32)
-        for index, vector in enumerate(extra):
-            tail = jnp.where(row == index, vector, tail)
-        out[2 * rows :, :] = tail.astype(BF16)
-
-
-def unpack_kernel(place, *refs, rows):
+            tail = jnp.where(row == 2 * side, middle, jnp.where(row == 2 * side + 1, rest - middle, tail))
+        low = other * height + 2 * rows
+        whole[low : low + TILE, :] = tail.astype(BF16)
+    shares = halves_of(lines)
+    for digit, out in enumerate(outs, 1):
+        columns = [0] + [digit ^ other for other in shares[digit]]
+        for index, column in enumerate(columns):
+            start = pl.multiple_of((place[2] ^ column) * width, width)
+            out[:, index * width : (index + 1) * width] = whole[:, pl.ds(start, width)]
+
+
+def mirror_kernel(place, whole, swapped, *refs, rows):
     parts, out = refs[:-1], refs[-1]
     order = out.shape[2]
-    height = 2 * rows + TILE
+    lines = len(parts) + 1
+    width = order // lines
+    share = parts[0].shape[1] if parts else 0
+    shares = halves_of(lines)
+    diagonal = on_diagonal(width, width, 0)
+
+    def at(digit):
+        return pl.ds(pl.multiple_of((place[2] ^ digit) * width, width), width)
+
+    def rows_of(digit, core):
+        start = ((place[2] ^ digit) * 2 + (place[0] ^ core)) * rows
+        return pl.ds(pl.multiple_of(start, rows), rows)
+
+    def damp(side, digit, tails):
+        vector = jnp.full((1, width), DAMPING, F32)
+        for tail in tails:
+            tail = tail.astype(F32)
+            vector += tail[2 * side : 2 * side + 1] + tail[2 * side + 1 : 2 * side + 2]
+        out[side, at(digit), at(digit)] += jnp.where(diagonal, vector, 0.0)
+
+    for side in range(2):
+        low, tail = slice(side * rows, (side + 1) * rows), slice(2 * rows, 2 * rows + TILE)
+        out[side, rows_of(0, 0), :] = whole[low, :].astype(F32)
+        out[side, rows_of(0, 1), :] = swapped[low, :order].astype(F32)
+        for digit in range(1, lines):
+            out[side, at(digit), at(0)] = out[side, at(0), at(digit)].T
+        damp(side, 0, [whole[tail, at(0)], swapped[tail, at(0)]])
+        for digit, part in enumerate(parts, 1):
+            start = order + (digit - 1) * share
+            for index, other in enumerate([digit] + shares[digit]):
+                lanes = slice(index * width, (index + 1) * width)
+                out[side, rows_of(digit, 0), at(other)] = part[low, lanes].astype(F32)
+                lanes = slice(start + index * width, start + (index + 1) * width)
+                out[side, rows_of(digit, 1), at(other)] = swapped[low, lanes].astype(F32)
+                if index:
+                    out[side, at(other), at(digit)] = out[side, at(digit), at(other)].T
+            damp(side, digit, [part[tail, :width], swapped[tail, start : start + width]])
+
+
+def collect_kernel(place, *refs, rows):
+    parts, out = refs[:-1], refs[-1]
+    order = out.shape[2]
+    tail = slice(2 * rows, 2 * rows + TILE)
     vectors = [jnp.full((1, order), DAMPING, F32) for _ in range(2)]
     for part in parts:
-        for core in range(2):
-            tail = part[core * height + 2 * rows : (core + 1) * height, :].astype(F32)
-            for side in range(2):
-                vectors[side] += tail[2 * side : 2 * side + 1] + tail[2 * side + 1 : 2 * side + 2]
+        values = part[tail, :].astype(F32)
+        for side in range(2):
+            vectors[side] += values[2 * side : 2 * side + 1] + values[2 * side + 1 : 2 * side + 2]
     for index, part in enumerate(parts):
-        for core in range(2):
-            start = ((place[2] ^ index) * 2 + (place[0] ^ core)) * rows
-            start = pl.multiple_of(start, rows)
-            diagonal = on_diagonal(rows, order, start)
-            for side in range(2):
-                low = core * height + side * rows
-                values = part[low : low + rows, :].astype(F32)
-                out[side, pl.ds(start, rows), :] = values + jnp.where(diagonal, vectors[side], 0.0)
+        start = ((place[2] ^ index // 2) * 2 + (place[0] ^ index % 2)) * rows
+        start = pl.multiple_of(start, rows)
+        diagonal = on_diagonal(rows, order, start)
+        for side in range(2):
+            values = part[side * rows : (side + 1) * rows, :].astype(F32)
+            out[side, pl.ds(start, rows), :] = values + jnp.where(diagonal, vectors[side], 0.0)
 
 
 def step_kernel(place, damped, *refs, pieces, rows, band):
@@ -192,6 +247,45 @@
     sent[2] = update[band:]
 
 
+def stage_stats(place, stats_old, tiles, lines):
+    band, order = stats_old.shape[1:]
+    height, width = 2 * (2 * band + TILE), order // lines
+    mirrored = width % LANES == 0
+    share = jax.ShapeDtypeStruct((height, width * (1 + (lines - 2) // 2)), BF16)
+    outs = (jax.ShapeDtypeStruct((height, order), BF16),) + (share,) * (lines - 1 if mirrored else 0)
+    whole, *shares = pl.pallas_call(
+        functools.partial(stage_kernel, tiles=tiles, lines=lines),
+        out_shape=outs,
+        in_specs=[SMEM] + vmem(1),
+        out_specs=tuple(vmem(len(outs))),
+        compiler_params=pltpu.CompilerParams(vmem_limit_bytes=8 << 20),
+        cost_estimate=pl.CostEstimate(flops=band * order * 20, bytes_accessed=band * order * 32, transcendentals=0),
+        name="stage_stats",
+    )(place, stats_old)
+    return whole, shares if mirrored else [whole] * (lines - 1)
+
+
+def whole_stats(place, whole, stats, order, band):
+    height = 2 * band + TILE
+    if stats and stats[0].shape[1] != order:
+        swapped = swap(jnp.concatenate([part[height:] for part in (whole, *stats)], axis=1), "grp", 1)
+        kernel, operands = mirror_kernel, [whole, swapped, *stats]
+    else:
+        swapped = swap(jnp.concatenate([part[height:] for part in (whole, *stats)], axis=0), "grp", 1)
+        kernel, operands = collect_kernel, []
+        for index, part in enumerate((whole, *stats)):
+            operands += [part[:height], swapped[index * height : (index + 1) * height]]
+    return pl.pallas_call(
+        functools.partial(kernel, rows=band),
+        out_shape=jax.ShapeDtypeStruct((2, order, order), F32),
+        in_specs=[SMEM] + vmem(len(operands)),
+        out_specs=vmem(1)[0],
+        compiler_params=pltpu.CompilerParams(vmem_limit_bytes=16 << 20),
+        cost_estimate=pl.CostEstimate(flops=order * order * 8, bytes_accessed=order * order * 12, transcendentals=0),
+        name="whole_stats",
+    )(place, *operands)
+
+
 def on_device(activations, out_grads, stats_old):
     order = activations.shape[1]
     tiles = out_grads.shape[1] // order
@@ -204,47 +298,29 @@
     along, rows = plan("grp", 1, lines, rows)
     steps = across + along
     here = jnp.int32(0)
-    for axis, shift, radix, splits in steps:
-        if splits:
+    for axis, shift, radix, halves in steps:
+        if halves:
             here = here * radix + ((lax.axis_index(axis) >> shift) & (radix - 1))
     place = jnp.stack([core, here, line, grp * band, (grp ^ 1) * band]).astype(jnp.int32)
 
     sent = gradient_term(place, out_grads, activations, 1, rows)
     sent = swap(sent, "grp", 1)
+    whole, shares = stage_stats(place, stats_old, tiles, lines)
+    place, *shares = lax.optimization_barrier((place, *shares))
+    stats = [swap(share, "grp", digit << 1) for digit, share in enumerate(shares, 1)]
     total = gradient_term(place, out_grads, activations, 0, rows)
 
-    packed = jax.ShapeDtypeStruct((2 * band + TILE, order), BF16)
-    keep, send = pl.pallas_call(
-        functools.partial(pack_kernel, tiles=tiles),
-        out_shape=(packed, packed),
-        in_specs=[SMEM] + vmem(1),
-        out_specs=tuple(vmem(2)),
-        compiler_params=pltpu.CompilerParams(vmem_limit_bytes=8 << 20),
-        cost_estimate=pl.CostEstimate(flops=band * order * 20, bytes_accessed=band * order * 32, transcendentals=0),
-        name="pack_stats",
-    )(place, stats_old)
-    packed = jnp.concatenate([keep, swap(send, "grp", 1)], axis=0)
-
     total = total + sent
-    for axis, shift, radix, splits in across + along:
+    for index, (axis, shift, radix, splits) in enumerate(steps):
+        if index == len(across):
+            total, *stats = lax.optimization_barrier((total, *stats))
         if splits:
             total = total.reshape(radix, -1, order)
             parts = [swap(total[digit], axis, digit << shift) for digit in range(1, radix)]
             total = sum(parts, total[0])
         else:
             total = total + swap(total, axis, 1 << shift)
-    stats = [packed]
-    for digit in range(1, lines):
-        stats.append(swap(packed, "grp", digit << 1))
-    damped = pl.pallas_call(
-        functools.partial(unpack_kernel, rows=band),
-        out_shape=jax.ShapeDtypeStruct((2, order, order), F32),
-        in_specs=[SMEM] + vmem(len(stats)),
-        out_specs=vmem(1)[0],
-        compiler_params=pltpu.CompilerParams(vmem_limit_bytes=16 << 20),
-        cost_estimate=pl.CostEstimate(flops=order * order * 8, bytes_accessed=order * order * 12, transcendentals=0),
-        name="unpack_stats",
-    )(place, *stats)
+    damped = whole_stats(place, whole, stats, order, band)
 
     pieces = [total.astype(BF16)]
     for axis, shift, radix, splits in reversed(steps):

time: 80.3 us -> 61.5 us (0.77)
  waiting for transfers between devices: 42.8 us -> 18.5 us
  starting transfers between devices: 23.4 us -> 27.7 us
  Pallas kernels: 8.63 us -> 9.71 us
    ppermute x18, waiting for transfers between devices: 42.8 us -> 18.5 us  [swap(): return lax.ppermute(array, axis, [(i, i ^ mask) for i in range(size)])]
    ppermute x18, starting transfers between devices: 23.4 us -> 27.7 us  [swap(): return lax.ppermute(array, axis, [(i, i ^ mask) for i in range(size)])]
    pallas_call x2, Pallas kernels: 1.63 us -> 2.72 us  [the longest x1 1.95 us: whole_stats(): pl.pallas_call(functools.partial(kernel, rows=band), out_shape=jax.ShapeD...]
    unnamed x7 -> x6, local copies, waits for them, and re-layouts: 2.28 us -> 2.27 us
  transfers between devices with their start and end apart: 18 -> 18, of which waited for: 11 -> 12; matrix products, arithmetic and copies ran while one was open for 0% -> 0% of each run, Pallas kernels for 3% -> 6%
where the time goes in v2:
time: 61.5 us; the launch traced here: 61.3 us
  starting transfers between devices  27.7 us (45%)
  waiting for transfers between devices  18.5 us (30%)
  Pallas kernels  9.71 us (16%)
  local copies, waits for them, and re-layouts  2.53 us (4%)
  other arithmetic  2.04 us (3%)
  between operations  0.79 us (1%)
    ppermute x18, starting transfers between devices, swap(): return lax.ppermute(array, axis, [(i, i ^ mask) for i in range(size)])  27.7 us
    ppermute x18, waiting for transfers between devices, swap(): return lax.ppermute(array, axis, [(i, i ^ mask) for i in range(size)])  18.5 us
    pallas_call x1, Pallas kernels, on_device(): pl.pallas_call(functools.partial(step_kernel, pieces=len(pieces), rows=ro...  4.97 us
    unnamed x6, local copies, waits for them, and re-layouts  2.27 us
    pallas_call x2, Pallas kernels, gradient_term(): pl.pallas_call(functools.partial(term_kernel, other=other, rows=rows), ou...  2.03 us
    pallas_call x1, Pallas kernels, whole_stats(): pl.pallas_call(functools.partial(kernel, rows=band), out_shape=jax.ShapeD...  1.95 us
  transfers between devices with their start and end apart: 18, of which 12 were waited for; matrix products, arithmetic and copies ran while one was open for 0% of the time, Pallas kernels for 6%

profile of v2, /device:TPU:0, one launch (start us, length us, event | category | flops | bytes accessed | tf_op | source)
XLA Modules:
  0.0 61.3 jit_solution(8243926223318913492)
XLA Ops:
  0.7 1.2 %copy-done = bf16[512,1024]{1,0:T(8,128)(2,1)S(1)} copy-done((bf16[512,1024]{1,0:T(8,128)(2,1)S(1)}, bf16[512,1024]{1,0:T(8,128)(2,1)}, u32[]{:S(2)}) %copy-start) | copy-done | bytes 1048600
  2.0 1.0 %copy-done.2 = bf16[512,512]{1,0:T(8,128)(2,1)S(1)} copy-done((bf16[512,512]{1,0:T(8,128)(2,1)S(1)}, bf16[512,512]{1,0:T(8,128)(2,1)}, u32[]{:S(2)}) %copy-start.2) | copy-done | bytes 524312
  3.0 1.0 %gradient_term.3 = f32[512,512]{1,0:T(8,128)S(1)} custom-call(s32[5]{0:T(128)S(1)} %stack.29.place, bf16[512,1024]{1,0:T(8,128)(2,1)S(1)} %copy-done, bf16[512,512]{1,0:T(8,128)(2,1)S(1)} %copy-done.2), custom_call_target="tpu_custom_call" | custom-call | flops 268435456 | bytes 1048576 | tf_op jit(solution)/shard_map/gradient_term/pallas_call | solution.py:64
  4.0 0.5 collective-permute-start
  4.5 0.8 %stage_stats.1 = (bf16[288,512]{1,0:T(8,128)(2,1)S(1)}, bf16[288,256]{1,0:T(8,128)(2,1)S(1)}, bf16[288,256]{1,0:T(8,128)(2,1)S(1)}, bf16[288,256]{1,0:T(8,128)(2,1)S(1)}) custom-call(s32[5]{0:T(128)S(1)} %stack.29.place, f32[4,64,512]{2,1,0:T(8,128)S(1)} %copy-done.1), custom_call_target="tpu_custom_call" | custom-call | flops 655360 | bytes 1048576 | tf_op jit(solution)/shard_map/stage_stats/pallas_call | solution.py:256
  5.3 1.0 %gradient_term.2 = f32[512,512]{1,0:T(8,128)S(1)} custom-call(s32[5]{0:T(128)S(1)} %stack.29.place, bf16[512,1024]{1,0:T(8,128)(2,1)S(1)} %copy-done, bf16[512,512]{1,0:T(8,128)(2,1)S(1)} %copy-done.2), custom_call_target="tpu_custom_call" | custom-call | flops 268435456 | bytes 1048576 | tf_op jit(solution)/shard_map/gradient_term/pallas_call | solution.py:64
  6.3 0.5 collective-permute-done
  7.1 3.9 %collective-permute-start.3 = (f32[128,512]{1,0:T(8,128)S(1)}, f32[128,512]{1,0:T(8,128)S(1)}, u32[]{:S(2)}, u32[]{:S(2)}) collective-permute-start(f32[128,512]{1,0:T(8,128)S(1)} %get-tuple-element.31), channel_id=1, source_target_pairs={{0,24},{8,16},{16,8},{24,0},{1,25},{9,17},{17,9},{25,1},{2,26},{10... | collective-permute-start | bytes 786440 | tf_op jit(solution)/shard_map/ppermute | solution.py:21
  11.0 0.5 collective-permute-start.2
  11.6 2.0 %collective-permute-start.4 = (bf16[288,256]{1,0:T(8,128)(2,1)S(1)}, bf16[288,256]{1,0:T(8,128)(2,1)S(1)}, u32[]{:S(2)}, u32[]{:S(2)}) collective-permute-start(bf16[288,256]{1,0:T(8,128)(2,1)S(1)} %get-tuple-element.21), channel_id=1, source_target_pairs={{0,2},{1,3},{2,0},{3,1},{4,6},{5,7},{6,4},{7,5},{8,10},{9,11},{10,... | collective-permute-start | bytes 442376 | tf_op jit(solution)/shard_map/ppermute | solution.py:21
  13.6 2.6 %collective-permute-start.5 = (bf16[288,256]{1,0:T(8,128)(2,1)S(1)}, bf16[288,256]{1,0:T(8,128)(2,1)S(1)}, u32[]{:S(2)}, u32[]{:S(2)}) collective-permute-start(bf16[288,256]{1,0:T(8,128)(2,1)S(1)} %get-tuple-element.22), channel_id=1, source_target_pairs={{0,4},{1,5},{2,6},{3,7},{4,0},{5,1},{6,2},{7,3},{8,12},{9,13},{10,... | collective-permute-start | bytes 442376 | tf_op jit(solution)/shard_map/ppermute | solution.py:21
  16.2 1.9 %collective-permute-done.3 = f32[128,512]{1,0:T(8,128)S(1)} collective-permute-done((f32[128,512]{1,0:T(8,128)S(1)}, f32[128,512]{1,0:T(8,128)S(1)}, u32[]{:S(2)}, u32[]{:S(2)}) %collective-permute-start.3) | collective-permute-done | bytes 262176 | tf_op jit(solution)/shard_map/ppermute | solution.py:21
  18.1 4.1 %collective-permute-start.6 = (bf16[288,256]{1,0:T(8,128)(2,1)S(1)}, bf16[288,256]{1,0:T(8,128)(2,1)S(1)}, u32[]{:S(2)}, u32[]{:S(2)}) collective-permute-start(bf16[288,256]{1,0:T(8,128)(2,1)S(1)} %get-tuple-element.23), channel_id=1, source_target_pairs={{0,6},{1,7},{2,4},{3,5},{4,2},{5,3},{6,0},{7,1},{8,14},{9,15},{10,... | collective-permute-start | bytes 442376 | tf_op jit(solution)/shard_map/ppermute | solution.py:21
  22.2 1.0 %collective-permute-done.2 = f32[128,512]{1,0:T(8,128)S(1)} collective-permute-done((f32[128,512]{1,0:T(8,128)S(1)}, f32[128,512]{1,0:T(8,128)S(1)}, u32[]{:S(2)}, u32[]{:S(2)}) %collective-permute-start.2) | collective-permute-done | bytes 262176 | tf_op jit(solution)/shard_map/ppermute | solution.py:21
  23.2 0.3 collective-permute-done.1
  23.6 2.2 %collective-permute-done.5.refs_1_ = bf16[288,256]{1,0:T(8,128)(2,1)S(1)} collective-permute-done((bf16[288,256]{1,0:T(8,128)(2,1)S(1)}, bf16[288,256]{1,0:T(8,128)(2,1)S(1)}, u32[]{:S(2)}, u32[]{:S(2)}) %collective-permute-start.5) | collective-permute-done | bytes 147488 | tf_op jit(solution)/shard_map/ppermute | solution.py:21
  25.8 3.6 %collective-permute-start.10 = (f32[32,512]{1,0:T(8,128)S(1)}, f32[32,512]{1,0:T(8,128)S(1)}, u32[]{:S(2)}, u32[]{:S(2)}) collective-permute-start(f32[32,512]{1,0:T(8,128)S(1)} %get-tuple-element.42), channel_id=1, source_target_pairs={{0,6},{1,7},{2,4},{3,5},{4,2},{5,3},{6,0},{7,1},{8,14},{9,15},{10,... | collective-permute-start | bytes 196616 | tf_op jit(solution)/shard_map/ppermute | solution.py:21
  29.5 2.2 %collective-permute-start.9 = (f32[32,512]{1,0:T(8,128)S(1)}, f32[32,512]{1,0:T(8,128)S(1)}, u32[]{:S(2)}, u32[]{:S(2)}) collective-permute-start(f32[32,512]{1,0:T(8,128)S(1)} %get-tuple-element.43), channel_id=1, source_target_pairs={{0,4},{1,5},{2,6},{3,7},{4,0},{5,1},{6,2},{7,3},{8,12},{9,13},{10,... | collective-permute-start | bytes 196616 | tf_op jit(solution)/shard_map/ppermute | solution.py:21
  32.0 4.5 %collective-permute-done.9 = f32[32,512]{1,0:T(8,128)S(1)} collective-permute-done((f32[32,512]{1,0:T(8,128)S(1)}, f32[32,512]{1,0:T(8,128)S(1)}, u32[]{:S(2)}, u32[]{:S(2)}) %collective-permute-start.9) | collective-permute-done | bytes 65568 | tf_op jit(solution)/shard_map/ppermute | solution.py:21
  36.6 1.9 %collective-permute-start.13 = (bf16[32,512]{1,0:T(8,128)(2,1)S(1)}, bf16[32,512]{1,0:T(8,128)(2,1)S(1)}, u32[]{:S(2)}, u32[]{:S(2)}) collective-permute-start(bf16[32,512]{1,0:T(8,128)(2,1)S(1)} %add_convert_fusion), channel_id=1, source_target_pairs={{0,6},{1,7},{2,4},{3,5},{4,2},{5,3},{6,0},{7,1},{8,14},{9,15},{10,... | collective-permute-start | bytes 98312 | tf_op jit(solution)/shard_map/ppermute | solution.py:21
  38.4 2.6 %collective-permute-start.11 = (bf16[32,512]{1,0:T(8,128)(2,1)S(1)}, bf16[32,512]{1,0:T(8,128)(2,1)S(1)}, u32[]{:S(2)}, u32[]{:S(2)}) collective-permute-start(bf16[32,512]{1,0:T(8,128)(2,1)S(1)} %add_convert_fusion), channel_id=1, source_target_pairs={{0,2},{1,3},{2,0},{3,1},{4,6},{5,7},{6,4},{7,5},{8,10},{9,11},{10,... | collective-permute-start | bytes 98312 | tf_op jit(solution)/shard_map/ppermute | solution.py:21
  41.0 1.3 %collective-permute-done.13 = bf16[32,512]{1,0:T(8,128)(2,1)S(1)} collective-permute-done((bf16[32,512]{1,0:T(8,128)(2,1)S(1)}, bf16[32,512]{1,0:T(8,128)(2,1)S(1)}, u32[]{:S(2)}, u32[]{:S(2)}) %collective-permute-start.13) | collective-permute-done | bytes 32800 | tf_op jit(solution)/shard_map/ppermute | solution.py:21
  42.3 0.9 %collective-permute-done.12 = bf16[32,512]{1,0:T(8,128)(2,1)S(1)} collective-permute-done((bf16[32,512]{1,0:T(8,128)(2,1)S(1)}, bf16[32,512]{1,0:T(8,128)(2,1)S(1)}, u32[]{:S(2)}, u32[]{:S(2)}) %collective-permute-start.12) | collective-permute-done | bytes 32800 | tf_op jit(solution)/shard_map/ppermute | solution.py:21
  43.3 1.6 %collective-permute-start.14 = (bf16[128,512]{1,0:T(8,128)(2,1)S(1)}, bf16[128,512]{1,0:T(8,128)(2,1)S(1)}, u32[]{:S(2)}, u32[]{:S(2)}) collective-permute-start(bf16[128,512]{1,0:T(8,128)(2,1)S(1)} %pad_maximum_fusion.2.refs_0_), channel_id=1, source_target_pairs={{0,8},{8,0},{16,24},{24,16},{1,9},{9,1},{17,25},{25,17},{2,10},{10... | collective-permute-start | bytes 393224 | tf_op jit(solution)/shard_map/ppermute | solution.py:21
  44.8 2.1 %collective-permute-start.15 = (bf16[128,512]{1,0:T(8,128)(2,1)S(1)}, bf16[128,512]{1,0:T(8,128)(2,1)S(1)}, u32[]{:S(2)}, u32[]{:S(2)}) collective-permute-start(bf16[128,512]{1,0:T(8,128)(2,1)S(1)} %pad_maximum_fusion.2.refs_0_), channel_id=1, source_target_pairs={{0,16},{8,24},{16,0},{24,8},{1,17},{9,25},{17,1},{25,9},{2,18},{10... | collective-permute-start | bytes 393224 | tf_op jit(solution)/shard_map/ppermute | solution.py:21
  46.9 2.0 %whole_stats.1.damped = f32[2,512,512]{2,1,0:T(8,128)S(1)} custom-call(s32[5]{0:T(128)S(1)} %stack.29.place, bf16[288,512]{1,0:T(8,128)(2,1)S(1)} %get-tuple-element.20.whole, bf16[144,1280]{1,0:T(8,128)(2,1)S(1)} %collective-permute-done.7.swapped, bf16[288,256]{1,0:T(8,128)(2,1)S(1)} %collective-permute-done.4.refs_0_, ...), custom_call_target="tpu_custom_call" | custom-call | flops 2097152 | bytes 3145728 | tf_op jit(solution)/shard_map/whole_stats/pallas_call | solution.py:278
  48.9 1.9 %collective-permute-done.15.refs_2_ = bf16[128,512]{1,0:T(8,128)(2,1)S(1)} collective-permute-done((bf16[128,512]{1,0:T(8,128)(2,1)S(1)}, bf16[128,512]{1,0:T(8,128)(2,1)S(1)}, u32[]{:S(2)}, u32[]{:S(2)}) %collective-permute-start.15) | collective-permute-done | bytes 131104 | tf_op jit(solution)/shard_map/ppermute | solution.py:21
  50.8 1.9 %collective-permute-done.16.refs_3_ = bf16[128,512]{1,0:T(8,128)(2,1)S(1)} collective-permute-done((bf16[128,512]{1,0:T(8,128)(2,1)S(1)}, bf16[128,512]{1,0:T(8,128)(2,1)S(1)}, u32[]{:S(2)}, u32[]{:S(2)}) %collective-permute-start.16) | collective-permute-done | bytes 131104 | tf_op jit(solution)/shard_map/ppermute | solution.py:21
  52.8 5.0 %precondition.1 = (f32[3,64,512]{2,1,0:T(8,128)S(1)}, f32[3,64,512]{2,1,0:T(8,128)S(1)}) custom-call(s32[5]{0:T(128)S(1)} %stack.29.place, f32[2,512,512]{2,1,0:T(8,128)S(1)} %whole_stats.1.damped, bf16[128,512]{1,0:T(8,128)(2,1)S(1)} %pad_maximum_fusion.2.refs_0_, bf16[128,512]{1,0:T(8,128)(2,1)S(1)} %collective-permute-done.14.refs_1_, ...), custom_call_target="tpu_custom_call" | custom-call | flops 2684354560 | bytes 4194304 | tf_op jit(solution)/shard_map/precondition/pallas_call | solution.py:333
  57.8 1.7 %collective-permute-done.17 = f32[3,64,512]{2,1,0:T(8,128)S(1)} collective-permute-done((f32[3,64,512]{2,1,0:T(8,128)S(1)}, f32[3,64,512]{2,1,0:T(8,128)S(1)}, u32[]{:S(2)}, u32[]{:S(2)}) %collective-permute-start.17) | collective-permute-done | bytes 393248 | tf_op jit(solution)/shard_map/ppermute | solution.py:21
  59.7 0.7 %pad_maximum_fusion.1 = f32[2,64,512]{2,1,0:T(8,128)} fusion(f32[1,64,512]{2,1,0:T(8,128)S(1)} %get-tuple-element.46, f32[1,64,512]{2,1,0:T(8,128)S(1)} %get-tuple-element.35), kind=kLoop, calls=%fused_computation.5 | loop fusion | flops 65536 | bytes 524288 | tf_op jit(solution)/shard_map/stack | solution.py:357
  60.4 0.9 %maximum_add_fusion = f32[4,64,512]{2,1,0:T(8,128)} fusion(f32[4,64,512]{2,1,0:T(8,128)S(1)} %copy-done.1, f32[1,64,512]{2,1,0:T(8,128)S(1)} %get-tuple-element.45, f32[1,64,512]{2,1,0:T(8,128)S(1)} %get-tuple-element.36, f32[1,64,512]{2,1,0:T(8,128)S(1)} %get-tuple-element.44, f32[1,64,512]{2,1,0:T(8,128)S(1)} %get-tuple-element.37), kind=kLoop, calls=%fused_computation | loop fusion | flops 524288 | bytes 1572864 | tf_op jit(solution)/shard_map/add | solution.py:356
  (31 shorter events, 1.3 us)
Async XLA Ops:
  0.7 1.2 %copy-start = (bf16[512,1024]{1,0:T(8,128)(2,1)S(1)}, bf16[512,1024]{1,0:T(8,128)(2,1)}, u32[]{:S(2)}) copy-start(bf16[512,1024]{1,0:T(8,128)(2,1)} %grads.3) | copy-start | bytes 3145732
  2.0 1.0 %copy-start.2 = (bf16[512,512]{1,0:T(8,128)(2,1)S(1)}, bf16[512,512]{1,0:T(8,128)(2,1)}, u32[]{:S(2)}) copy-start(bf16[512,512]{1,0:T(8,128)(2,1)} %acts.3) | copy-start | bytes 1572868
  3.0 1.5 %copy-start.1 = (f32[4,64,512]{2,1,0:T(8,128)S(1)}, f32[4,64,512]{2,1,0:T(8,128)}, u32[]{:S(2)}) copy-start(f32[4,64,512]{2,1,0:T(8,128)} %stats.1) | copy-start | bytes 1572868
  4.0 2.8 %collective-permute-start = (f32[512,512]{1,0:T(8,128)S(1)}, f32[512,512]{1,0:T(8,128)S(1)}, u32[]{:S(2)}, u32[]{:S(2)}) collective-permute-start(f32[512,512]{1,0:T(8,128)S(1)} %gradient_term.3), channel_id=1, source_target_pairs={{0,1},{1,0},{2,3},{3,2},{4,5},{5,4},{6,7},{7,6},{8,9},{9,8},{10,11... | collective-permute-start | bytes 3145736 | tf_op jit(solution)/shard_map/ppermute | solution.py:21
  7.1 11.0 %collective-permute-start.3 = (f32[128,512]{1,0:T(8,128)S(1)}, f32[128,512]{1,0:T(8,128)S(1)}, u32[]{:S(2)}, u32[]{:S(2)}) collective-permute-start(f32[128,512]{1,0:T(8,128)S(1)} %get-tuple-element.31), channel_id=1, source_target_pairs={{0,24},{8,16},{16,8},{24,0},{1,25},{9,17},{17,9},{25,1},{2,26},{10... | collective-permute-start | bytes 786440 | tf_op jit(solution)/shard_map/ppermute | solution.py:21
  11.0 12.2 %collective-permute-start.2 = (f32[128,512]{1,0:T(8,128)S(1)}, f32[128,512]{1,0:T(8,128)S(1)}, u32[]{:S(2)}, u32[]{:S(2)}) collective-permute-start(f32[128,512]{1,0:T(8,128)S(1)} %get-tuple-element.32), channel_id=1, source_target_pairs={{0,16},{8,24},{16,0},{24,8},{1,17},{9,25},{17,1},{25,9},{2,18},{10... | collective-permute-start | bytes 786440 | tf_op jit(solution)/shard_map/ppermute | solution.py:21
  11.5 12.0 %collective-permute-start.1 = (f32[128,512]{1,0:T(8,128)S(1)}, f32[128,512]{1,0:T(8,128)S(1)}, u32[]{:S(2)}, u32[]{:S(2)}) collective-permute-start(f32[128,512]{1,0:T(8,128)S(1)} %get-tuple-element.30), channel_id=1, source_target_pairs={{0,8},{8,0},{16,24},{24,16},{1,9},{9,1},{17,25},{25,17},{2,10},{10... | collective-permute-start | bytes 786440 | tf_op jit(solution)/shard_map/ppermute | solution.py:21
  11.6 12.0 %collective-permute-start.4 = (bf16[288,256]{1,0:T(8,128)(2,1)S(1)}, bf16[288,256]{1,0:T(8,128)(2,1)S(1)}, u32[]{:S(2)}, u32[]{:S(2)}) collective-permute-start(bf16[288,256]{1,0:T(8,128)(2,1)S(1)} %get-tuple-element.21), channel_id=1, source_target_pairs={{0,2},{1,3},{2,0},{3,1},{4,6},{5,7},{6,4},{7,5},{8,10},{9,11},{10,... | collective-permute-start | bytes 442376 | tf_op jit(solution)/shard_map/ppermute | solution.py:21
  13.6 12.2 %collective-permute-start.5 = (bf16[288,256]{1,0:T(8,128)(2,1)S(1)}, bf16[288,256]{1,0:T(8,128)(2,1)S(1)}, u32[]{:S(2)}, u32[]{:S(2)}) collective-permute-start(bf16[288,256]{1,0:T(8,128)(2,1)S(1)} %get-tuple-element.22), channel_id=1, source_target_pairs={{0,4},{1,5},{2,6},{3,7},{4,0},{5,1},{6,2},{7,3},{8,12},{9,13},{10,... | collective-permute-start | bytes 442376 | tf_op jit(solution)/shard_map/ppermute | solution.py:21
  18.1 7.7 %collective-permute-start.6 = (bf16[288,256]{1,0:T(8,128)(2,1)S(1)}, bf16[288,256]{1,0:T(8,128)(2,1)S(1)}, u32[]{:S(2)}, u32[]{:S(2)}) collective-permute-start(bf16[288,256]{1,0:T(8,128)(2,1)S(1)} %get-tuple-element.23), channel_id=1, source_target_pairs={{0,6},{1,7},{2,4},{3,5},{4,2},{5,3},{6,0},{7,1},{8,14},{9,15},{10,... | collective-permute-start | bytes 442376 | tf_op jit(solution)/shard_map/ppermute | solution.py:21
  25.8 6.1 %collective-permute-start.10 = (f32[32,512]{1,0:T(8,128)S(1)}, f32[32,512]{1,0:T(8,128)S(1)}, u32[]{:S(2)}, u32[]{:S(2)}) collective-permute-start(f32[32,512]{1,0:T(8,128)S(1)} %get-tuple-element.42), channel_id=1, source_target_pairs={{0,6},{1,7},{2,4},{3,5},{4,2},{5,3},{6,0},{7,1},{8,14},{9,15},{10,... | collective-permute-start | bytes 196616 | tf_op jit(solution)/shard_map/ppermute | solution.py:21
  29.5 7.0 %collective-permute-start.9 = (f32[32,512]{1,0:T(8,128)S(1)}, f32[32,512]{1,0:T(8,128)S(1)}, u32[]{:S(2)}, u32[]{:S(2)}) collective-permute-start(f32[32,512]{1,0:T(8,128)S(1)} %get-tuple-element.43), channel_id=1, source_target_pairs={{0,4},{1,5},{2,6},{3,7},{4,0},{5,1},{6,2},{7,3},{8,12},{9,13},{10,... | collective-permute-start | bytes 196616 | tf_op jit(solution)/shard_map/ppermute | solution.py:21
  31.6 4.9 %collective-permute-start.8 = (f32[32,512]{1,0:T(8,128)S(1)}, f32[32,512]{1,0:T(8,128)S(1)}, u32[]{:S(2)}, u32[]{:S(2)}) collective-permute-start(f32[32,512]{1,0:T(8,128)S(1)} %get-tuple-element.41), channel_id=1, source_target_pairs={{0,2},{1,3},{2,0},{3,1},{4,6},{5,7},{6,4},{7,5},{8,10},{9,11},{10,... | collective-permute-start | bytes 196616 | tf_op jit(solution)/shard_map/ppermute | solution.py:21
  31.7 15.2 %collective-permute-start.7 = (bf16[144,1280]{1,0:T(8,128)(2,1)S(1)}, bf16[144,1280]{1,0:T(8,128)(2,1)S(1)}, u32[]{:S(2)}, u32[]{:S(2)}) collective-permute-start(bf16[144,1280]{1,0:T(8,128)(2,1)S(1)} %pad_maximum_fusion), channel_id=1, source_target_pairs={{0,1},{1,0},{2,3},{3,2},{4,5},{5,4},{6,7},{7,6},{8,9},{9,8},{10,11... | collective-permute-start | bytes 1105928 | tf_op jit(solution)/shard_map/ppermute | solution.py:21
  36.6 5.8 %collective-permute-start.13 = (bf16[32,512]{1,0:T(8,128)(2,1)S(1)}, bf16[32,512]{1,0:T(8,128)(2,1)S(1)}, u32[]{:S(2)}, u32[]{:S(2)}) collective-permute-start(bf16[32,512]{1,0:T(8,128)(2,1)S(1)} %add_convert_fusion), channel_id=1, source_target_pairs={{0,6},{1,7},{2,4},{3,5},{4,2},{5,3},{6,0},{7,1},{8,14},{9,15},{10,... | collective-permute-start | bytes 98312 | tf_op jit(solution)/shard_map/ppermute | solution.py:21
  38.4 4.8 %collective-permute-start.12 = (bf16[32,512]{1,0:T(8,128)(2,1)S(1)}, bf16[32,512]{1,0:T(8,128)(2,1)S(1)}, u32[]{:S(2)}, u32[]{:S(2)}) collective-permute-start(bf16[32,512]{1,0:T(8,128)(2,1)S(1)} %add_convert_fusion), channel_id=1, source_target_pairs={{0,4},{1,5},{2,6},{3,7},{4,0},{5,1},{6,2},{7,3},{8,12},{9,13},{10,... | collective-permute-start | bytes 98312 | tf_op jit(solution)/shard_map/ppermute | solution.py:21
  38.4 4.8 %collective-permute-start.11 = (bf16[32,512]{1,0:T(8,128)(2,1)S(1)}, bf16[32,512]{1,0:T(8,128)(2,1)S(1)}, u32[]{:S(2)}, u32[]{:S(2)}) collective-permute-start(bf16[32,512]{1,0:T(8,128)(2,1)S(1)} %add_convert_fusion), channel_id=1, source_target_pairs={{0,2},{1,3},{2,0},{3,1},{4,6},{5,7},{6,4},{7,5},{8,10},{9,11},{10,... | collective-permute-start | bytes 98312 | tf_op jit(solution)/shard_map/ppermute | solution.py:21
  43.3 5.6 %collective-permute-start.14 = (bf16[128,512]{1,0:T(8,128)(2,1)S(1)}, bf16[128,512]{1,0:T(8,128)(2,1)S(1)}, u32[]{:S(2)}, u32[]{:S(2)}) collective-permute-start(bf16[128,512]{1,0:T(8,128)(2,1)S(1)} %pad_maximum_fusion.2.refs_0_), channel_id=1, source_target_pairs={{0,8},{8,0},{16,24},{24,16},{1,9},{9,1},{17,25},{25,17},{2,10},{10... | collective-permute-start | bytes 393224 | tf_op jit(solution)/shard_map/ppermute | solution.py:21
  44.8 6.0 %collective-permute-start.15 = (bf16[128,512]{1,0:T(8,128)(2,1)S(1)}, bf16[128,512]{1,0:T(8,128)(2,1)S(1)}, u32[]{:S(2)}, u32[]{:S(2)}) collective-permute-start(bf16[128,512]{1,0:T(8,128)(2,1)S(1)} %pad_maximum_fusion.2.refs_0_), channel_id=1, source_target_pairs={{0,16},{8,24},{16,0},{24,8},{1,17},{9,25},{17,1},{25,9},{2,18},{10... | collective-permute-start | bytes 393224 | tf_op jit(solution)/shard_map/ppermute | solution.py:21
  46.9 5.9 %collective-permute-start.16 = (bf16[128,512]{1,0:T(8,128)(2,1)S(1)}, bf16[128,512]{1,0:T(8,128)(2,1)S(1)}, u32[]{:S(2)}, u32[]{:S(2)}) collective-permute-start(bf16[128,512]{1,0:T(8,128)(2,1)S(1)} %pad_maximum_fusion.2.refs_0_), channel_id=1, source_target_pairs={{0,24},{8,16},{16,8},{24,0},{1,25},{9,17},{17,9},{25,1},{2,26},{10... | collective-permute-start | bytes 393224 | tf_op jit(solution)/shard_map/ppermute | solution.py:21
  57.8 1.8 %collective-permute-start.17 = (f32[3,64,512]{2,1,0:T(8,128)S(1)}, f32[3,64,512]{2,1,0:T(8,128)S(1)}, u32[]{:S(2)}, u32[]{:S(2)}) collective-permute-start(f32[3,64,512]{2,1,0:T(8,128)S(1)} %get-tuple-element.29), channel_id=1, source_target_pairs={{0,1},{1,0},{2,3},{3,2},{4,5},{5,4},{6,7},{7,6},{8,9},{9,8},{10,11... | collective-permute-start | bytes 1179656 | tf_op jit(solution)/shard_map/ppermute | solution.py:21

commit v3 on v2

v3 whole, which is shorter than its diff:
```python
import functools
import math

import jax
import jax.numpy as jnp
from jax import lax
from jax.experimental import pallas as pl
from jax.experimental.pallas import tpu as pltpu
from jax.sharding import PartitionSpec as P

F32 = jnp.float32
BF16 = jnp.bfloat16
DAMPING = 0.01
TILE = 16
LANES = 128


def swap(array, masks):
    reps, group = lax.axis_size("rep"), lax.axis_size("grp")
    pairs = []
    for rep in range(reps):
        for grp in range(group):
            over, along = masks[grp & 1]
            pairs.append((rep * group + grp, (rep ^ over) * group + (grp ^ along)))
    return lax.ppermute(array, ("rep", "grp"), pairs)


CORES = ((0, 1), (0, 1))


def both(first, second):
    return tuple((a[0] ^ b[0], a[1] ^ b[1]) for a, b in zip(first, second))


def plan(reps, lines, rows):
    over = [(1 << bit, 0) for bit in range(reps.bit_length() - 1)]
    along = [(0, 2 << bit) for bit in range(lines.bit_length() - 1)]
    phases = []
    for kind, bits in (("relay", list(zip(over, over[::-1]))), ("direct", list(zip(along, along)))):
        while bits:
            if len(bits) > 1 and rows // 4 >= TILE:
                phases.append((kind, bits[:2]))
                bits, rows = bits[2:], rows // 4
            elif rows // 2 >= TILE:
                phases.append(("halve", bits[:1]))
                bits, rows = bits[1:], rows // 2
            else:
                phases.append(("add", bits[:1]))
                bits = bits[1:]
    return phases, rows


def position(phases, core, rep, grp):
    here = jnp.int32(0)
    for kind, bits in phases:
        if kind != "add":
            for masks in bits:
                flags = [jnp.where((rep & over) | (grp & along), 1, 0) for over, along in masks]
                here = here * 2 + jnp.where(core == 0, flags[0], flags[1])
    return here


def reduce_phase(total, kind, bits, early=()):
    if kind == "add":
        return total + swap(total, bits[0])
    if kind == "halve":
        keep, send = jnp.split(total, 2)
        return keep + swap(send, bits[0])
    keep, second, first, last = jnp.split(total, 4)
    if kind == "relay":
        last = swap(last, bits[0])
        first = swap(first, bits[0])
        last = lax.optimization_barrier((last, *early))[0]
        second = swap(second + last, bits[1])
        return keep + first + second
    second, first, last = swap(second, bits[1]), swap(first, bits[0]), swap(last, both(*bits))
    return keep + second + first + last


def gather_phase(whole, kind, bits):
    if kind == "add":
        return [whole]
    if kind == "halve":
        return [whole, swap(whole, bits[0])]
    return [whole, swap(whole, bits[1]), swap(whole, bits[0]), swap(whole, both(*bits))]


def vmem(count):
    return [pl.BlockSpec(memory_space=pltpu.VMEM)] * count


SMEM = pl.BlockSpec(memory_space=pltpu.SMEM)


def dot(a, b, contract=(1, 0)):
    return lax.dot_general(
        a, b, (((contract[0],), (contract[1],)), ((), ())), preferred_element_type=F32
    )


def term_kernel(place, grads, acts, out, *, other, rows):
    order = acts.shape[1]
    columns = pl.ds(pl.multiple_of((place[0] ^ other) * order, order), order)
    term = dot(grads[:, columns], acts[...], (0, 0))
    for block in range(order // rows):
        there = pl.ds(pl.multiple_of((block ^ place[6 if other else 1]) * rows, rows), rows)
        out[there, :] = term[block * rows : (block + 1) * rows]


def gradient_term(place, grads, acts, other, rows):
    tokens, order = acts.shape
    return pl.pallas_call(
        functools.partial(term_kernel, other=other, rows=rows),
        out_shape=jax.ShapeDtypeStruct((order, order), F32),
        in_specs=[SMEM] + vmem(2),
        out_specs=vmem(1)[0],
        compiler_params=pltpu.CompilerParams(vmem_limit_bytes=16 << 20),
        cost_estimate=pl.CostEstimate(
            flops=2 * tokens * order * order, bytes_accessed=4 * tokens * order, transcendentals=0
        ),
        name="gradient_term",
    )(place, grads, acts)


def on_diagonal(rows, columns, start):
    row = lax.broadcasted_iota(jnp.int32, (rows, columns), 0) + start
    return lax.broadcasted_iota(jnp.int32, (rows, columns), 1) == row


def columns_for(digit, lines):
    return [0] + [digit ^ other for other in range(digit + 1, lines)]


def stage_kernel(place, stats, whole, *outs, tiles, lines):
    rows, order = stats.shape[1:]
    width = order // lines
    height = rows + TILE
    diagonal = on_diagonal(rows, order, place[3])
    row = lax.broadcasted_iota(jnp.int32, (TILE, order), 0)
    for other in range(2):
        for side in range(2):
            values = stats[(place[5] ^ side) * tiles + (place[0] ^ other)]
            high = values.astype(BF16)
            low = (2 * other + side) * height
            whole[low : low + rows, :] = high
            rest = values - high.astype(F32)
            rest = jnp.sum(jnp.where(diagonal, rest, 0.0), axis=0, keepdims=True)
            middle = rest.astype(BF16).astype(F32)
            tail = jnp.where(row == 0, middle, jnp.where(row == 1, rest - middle, 0.0))
            whole[low + rows : low + height, :] = tail.astype(BF16)
    for digit, out in enumerate(outs, 1):
        for index, column in enumerate(columns_for(digit, lines)):
            start = pl.multiple_of((place[2] ^ column) * width, width)
            for other in range(2):
                low = 2 * other * height
                values = whole[low : low + height, pl.ds(start, width)]
                out[other * height : (other + 1) * height, index * width : (index + 1) * width] = values


def mirror_kernel(place, whole, swapped, mine, turned, out, *, rows, lines):
    order = out.shape[2]
    width = order // lines
    height = rows + TILE
    diagonal = on_diagonal(width, width, 0)

    def at(digit):
        return pl.ds(pl.multiple_of((place[2] ^ digit) * width, width), width)

    def rows_of(digit, core):
        start = ((place[2] ^ digit) * 2 + (place[0] ^ core)) * rows
        return pl.ds(pl.multiple_of(start, rows), rows)

    for index, part in enumerate((mine, turned)):
        side = place[5] ^ index
        low = slice(index * height, index * height + rows)
        tail = slice(index * height + rows, (index + 1) * height)

        def damp(digit, tails):
            tails = [values.astype(F32) for values in tails]
            vector = sum((values[:1] + values[1:2] for values in tails), jnp.full((1, width), DAMPING, F32))
            out[side, at(digit), at(digit)] += jnp.where(diagonal, vector, 0.0)

        out[side, rows_of(0, 0), :] = whole[low, :].astype(F32)
        out[side, rows_of(0, 1), :] = swapped[low, :order].astype(F32)
        for digit in range(1, lines):
            out[side, at(digit), at(0)] = out[side, at(0), at(digit)].T
        damp(0, [whole[tail, at(0)], swapped[tail, at(0)]])
        start = 0
        for digit in range(1, lines):
            first = slice(start, start + width)
            for column in columns_for(digit, lines):
                other = digit ^ column
                lanes = slice(start, start + width)
                out[side, rows_of(digit, 0), at(other)] = part[:rows, lanes].astype(F32)
                lanes = slice(order + start, order + start + width)
                out[side, rows_of(digit, 1), at(other)] = swapped[low, lanes].astype(F32)
                if column:
                    out[side, at(other), at(digit)] = out[side, at(digit), at(other)].T
                start += width
            away = slice(order + first.start, order + first.stop)
            damp(digit, [part[rows:height, first], swapped[tail, away]])


def collect_kernel(place, *refs, rows):
    parts, out = refs[:-1], refs[-1]
    order = out.shape[2]
    height = rows + TILE
    for index in range(2):
        side = place[5] ^ index
        vector = jnp.full((1, order), DAMPING, F32)
        for part in parts:
            tail = part[index * height + rows : (index + 1) * height, :].astype(F32)
            vector += tail[:1] + tail[1:2]
        for number, part in enumerate(parts):
            start = ((place[2] ^ number // 2) * 2 + (place[0] ^ number % 2)) * rows
            start = pl.multiple_of(start, rows)
            values = part[index * height : index * height + rows, :].astype(F32)
            out[side, pl.ds(start, rows), :] = values + jnp.where(on_diagonal(rows, order, start), vector, 0.0)


def step_kernel(place, damped, *refs, pieces, rows, band):
    parts = refs[:pieces]
    own, sent, grad, gram, scaled, power, factors, offs, seconds, left_root, right_rows = refs[pieces:]
    order = grad.shape[0]
    for index, part in enumerate(parts):
        for low in range(0, part.shape[0], rows):
            block = (index * part.shape[0] + low) // rows
            start = pl.multiple_of((block ^ place[1]) * rows, rows)
            grad[pl.ds(start, rows), :] = part[low : low + rows, :]
    for side in range(2):
        gram[side] = dot(grad[...], grad[...], (side, side))
        own[side] = gram[side, pl.ds(pl.multiple_of(place[3], band), band), :]
        sent[side] = gram[side, pl.ds(pl.multiple_of(place[4], band), band), :]
    step = min(order, LANES)
    strips = [slice(low, low + step) for low in range(0, order, step)]
    eye = on_diagonal(step, step, 0)
    sides = range(2)

    def on_eye(block):
        return jnp.where(eye, block, 0.0)

    def beside(block):
        return jnp.sum(on_eye(block), axis=1, keepdims=True)

    def above(ref, side):
        blocks = [jnp.sum(on_eye(ref[side, strip, strip]), axis=0, keepdims=True) for strip in strips]
        return jnp.concatenate(blocks, axis=1)

    def off_eye(ref, side, strip, values):
        ref[side, strip, :] = values.astype(BF16)
        ref[side, strip, strip] = jnp.where(eye, 0.0, values[:, strip]).astype(BF16)

    scales = []
    for side in sides:
        total = jnp.zeros((8, order), F32)
        for strip in strips:
            value = gram[side, strip, :] + damped[side, strip, :]
            scaled[side, strip, :] = value
            total += jnp.sum((value * value).reshape(step // 8, 8, order), axis=0)
        scales.append(2.5 / jnp.sqrt(jnp.sum(total, keepdims=True)))

    def iterate(side, strip):
        return scaled[side, strip, :] * scales[side]

    for side in sides:
        for strip in strips:
            value = iterate(side, strip)
            factors[side, strip, :] = (value * -0.25).astype(BF16)
            block = (jnp.where(eye, 5.0, 0.0) - value[:, strip]) * 0.25
            factors[side, strip, strip] = block.astype(BF16)
    for side in sides:
        square = dot(factors[side], factors[side])
        for strip in strips:
            value = square[strip]
            power[side, strip, :] = value
            power[side, strip, strip] = value[:, strip] - jnp.where(eye, 1.5625, 0.0)
            off_eye(seconds, side, strip, value)
    for side in sides:
        square = dot(seconds[side], seconds[side])
        across = above(power, side) + 3.125
        for strip in strips:
            value = power[side, strip, :]
            down = beside(value[:, strip])
            value = square[strip] + value * (across + down)
            power[side, strip, :] = value
            power[side, strip, strip] = value[:, strip] - on_eye(down * down)
            off_eye(offs, side, strip, value)
            off_eye(seconds, side, strip, iterate(side, strip))
    for side in sides:
        product = dot(seconds[side], offs[side])
        across = above(power, side)
        for strip in strips:
            first, value = iterate(side, strip), power[side, strip, :]
            down = beside(first[:, strip])
            value = product[strip] + first * (across + 2.44140625) + down * value
            offs[side, strip, :] = (value * -0.25).astype(BF16)
            block = jnp.where(eye, 5.0 + down * across[:, strip], 0.0) - value[:, strip]
            offs[side, strip, strip] = (block * 0.25).astype(BF16)
    quarters = [jnp.sqrt(jnp.sqrt(scale)) for scale in scales]
    left_root[...] = (dot(factors[0], offs[0]) * quarters[0]).astype(BF16)
    right_rows[:band] = factors[1, pl.ds(pl.multiple_of(place[3], band), band), :]
    right_rows[band:] = factors[1, pl.ds(pl.multiple_of(place[4], band), band), :]
    right_root = (dot(right_rows[...], offs[1]) * quarters[1]).astype(BF16)
    inner = dot(right_root, grad[...])
    high = inner.astype(BF16)
    low = (inner - high.astype(F32)).astype(BF16)
    update = (dot(high, left_root[...]) + dot(low, left_root[...])) * math.sqrt(order)
    own[2] = update[:band]
    sent[2] = update[band:]


def stage_stats(place, stats_old, tiles, lines):
    band, order = stats_old.shape[1:]
    height, width = band + TILE, order // lines
    outs = [jax.ShapeDtypeStruct((4 * height, order), BF16)]
    for number in range(1, lines if width % LANES == 0 else 1):
        outs.append(jax.ShapeDtypeStruct((2 * height, width * len(columns_for(number, lines))), BF16))
    return pl.pallas_call(
        functools.partial(stage_kernel, tiles=tiles, lines=lines),
        out_shape=tuple(outs),
        in_specs=[SMEM] + vmem(1),
        out_specs=tuple(vmem(len(outs))),
        compiler_params=pltpu.CompilerParams(vmem_limit_bytes=8 << 20),
        cost_estimate=pl.CostEstimate(flops=band * order * 20, bytes_accessed=band * order * 32, transcendentals=0),
        name="stage_stats",
    )(place, stats_old)


def whole_stats(place, whole, stats, lines, order, band):
    height = band + TILE
    if order // lines % LANES == 0:
        mine = jnp.concatenate(stats, axis=1)
        turned = swap(mine, ((1, 0), (1, 0)))
        away = jnp.concatenate([mine[height:], turned[height:]], axis=0)
        swapped = swap(jnp.concatenate([whole[2 * height :], away], axis=1), CORES)
        kernel = functools.partial(mirror_kernel, rows=band, lines=lines)
        operands = [whole, swapped, mine, turned]
    else:
        swapped = swap(jnp.concatenate([part[2 * height :] for part in (whole, *stats)], axis=0), CORES)
        kernel, operands = functools.partial(collect_kernel, rows=band), []
        for index, part in enumerate((whole, *stats)):
            operands += [part[: 2 * height], swapped[index * 2 * height : (index + 1) * 2 * height]]
    return pl.pallas_call(
        kernel,
        out_shape=jax.ShapeDtypeStruct((2, order, order), F32),
        in_specs=[SMEM] + vmem(len(operands)),
        out_specs=vmem(1)[0],
        compiler_params=pltpu.CompilerParams(vmem_limit_bytes=16 << 20),
        cost_estimate=pl.CostEstimate(flops=order * order * 8, bytes_accessed=order * order * 12, transcendentals=0),
        name="whole_stats",
    )(place, *operands)


def on_device(activations, out_grads, stats_old):
    order = activations.shape[1]
    tiles = out_grads.shape[1] // order
    band = stats_old.shape[1]
    rep, grp = lax.axis_index("rep"), lax.axis_index("grp")
    reps, lines = lax.axis_size("rep"), lax.axis_size("grp") // 2
    core, line = grp & 1, grp >> 1

    phases, rows = plan(reps, lines, order)
    here, beside = (position(phases, core ^ other, rep, grp) for other in (0, 1))
    place = jnp.stack([core, here, line, grp * band, (grp ^ 1) * band, rep & 1, beside]).astype(jnp.int32)

    sent = swap(gradient_term(place, out_grads, activations, 1, rows), CORES)
    whole, *shares = stage_stats(place, stats_old, tiles, lines)
    place, *shares = lax.optimization_barrier((place, *shares))
    stats = [swap(share, ((0, 2 * step),) * 2) for step, share in enumerate(shares or [whole] * (lines - 1), 1)]
    total = gradient_term(place, out_grads, activations, 0, rows) + sent
    for index, (kind, bits) in enumerate(phases):
        if index == (reps > 1):
            total, *stats = lax.optimization_barrier((total, *stats))
        total = reduce_phase(total, kind, bits, [] if index else [stats[-1]])
    damped = whole_stats(place, whole, stats, lines, order, band)

    pieces = [total.astype(BF16)]
    for kind, bits in reversed(phases):
        joined = pieces[0] if len(pieces) == 1 else jnp.concatenate(pieces, axis=0)
        pieces = gather_phase(joined, kind, bits)

    result = jax.ShapeDtypeStruct((3, band, order), F32)
    square = (2, order, order)
    own, sent = pl.pallas_call(
        functools.partial(step_kernel, pieces=len(pieces), rows=rows, band=band),
        out_shape=(result, result),
        in_specs=[SMEM] + vmem(1 + len(pieces)),
        out_specs=tuple(vmem(2)),
        scratch_shapes=[
            pltpu.VMEM((order, order), BF16),
            pltpu.VMEM(square, F32),
            pltpu.VMEM(square, F32),
            pltpu.VMEM(square, F32),
            pltpu.VMEM(square, BF16),
            pltpu.VMEM(square, BF16),
            pltpu.VMEM(square, BF16),
            pltpu.VMEM((order, order), BF16),
            pltpu.VMEM((2 * band, order), BF16),
        ],
        compiler_params=pltpu.CompilerParams(vmem_limit_bytes=32 << 20),
        cost_estimate=pl.CostEstimate(flops=20 * order**3, bytes_accessed=order * order * 16, transcendentals=0),
        name="precondition",
    )(place, damped, *pieces)
    sent = swap(sent, CORES)
    own_tile = lax.broadcasted_iota(jnp.int32, (1, tiles, 1, 1), 1) == core
    moved = jnp.where(own_tile, own[:2, None], sent[:2, None]).reshape(stats_old.shape)
    return stats_old + moved, jnp.where(own_tile[0], own[2][None], sent[2][None])


def solution(mesh):
    in_specs = (P(("rep", "grp"), None), P(("rep", "grp"), None), P(None, "grp", None))
    out_specs = (P(None, "grp", None), P(None, "grp", None))
    return jax.shard_map(
        on_device, mesh=mesh, in_specs=in_specs, out_specs=out_specs, check_vma=False
    )
```

time: 61.5 us -> 56.7 us (0.922)
  waiting for transfers between devices: 18.5 us -> 14.8 us
  starting transfers between devices: 27.7 us -> 26.7 us
    ppermute x18 -> x19, waiting for transfers between devices: 18.5 us -> 14.8 us  [swap(): return lax.ppermute(array, ('rep', 'grp'), pairs)]
    ppermute x18 -> x19, starting transfers between devices: 27.7 us -> 26.7 us  [swap(): return lax.ppermute(array, ('rep', 'grp'), pairs)]
    another operation x1 -> x0, other arithmetic: 0.72 us -> none  [on_device(): return (stats_new, jnp.stack([low[2], high[2]]))]
    select_n x1, other arithmetic: 0.09 us -> 0.8 us  [on_device(): jnp.where(own_tile[0], own[2][None], sent[2][None])]
    add x3 -> x4, other arithmetic: 1.17 us -> 1.25 us  [the longest x1 0.95 us: on_device(): stats_old + moved]
    unnamed x6 -> x8, local copies, waits for them, and re-layouts: 2.27 us -> 2.29 us
  transfers between devices with their start and end apart: 18 -> 19, of which waited for: 12 -> 13; matrix products, arithmetic and copies ran while one was open for 0% -> 1% of each run, Pallas kernels for 6% -> 7%
where the time goes in v3:
time: 56.7 us; the launch traced here: 56.5 us
  starting transfers between devices  26.7 us (47%)
  waiting for transfers between devices  14.8 us (26%)
  Pallas kernels  9.41 us (17%)
  local copies, waits for them, and re-layouts  2.62 us (5%)
  other arithmetic  2.11 us (4%)
  between operations  0.85 us (1%)
    ppermute x19, starting transfers between devices, swap(): return lax.ppermute(array, ('rep', 'grp'), pairs)  26.7 us
    ppermute x19, waiting for transfers between devices, swap(): return lax.ppermute(array, ('rep', 'grp'), pairs)  14.8 us
    pallas_call x1, Pallas kernels, on_device(): pl.pallas_call(functools.partial(step_kernel, pieces=len(pieces), rows=ro...  4.7 us
    unnamed x8, local copies, waits for them, and re-layouts  2.29 us
    pallas_call x2, Pallas kernels, gradient_term(): pl.pallas_call(functools.partial(term_kernel, other=other, rows=rows), ou...  2.03 us
    pallas_call x1, Pallas kernels, whole_stats(): pl.pallas_call(kernel, out_shape=jax.ShapeDtypeStruct((2, order, order),...  1.95 us
  transfers between devices with their start and end apart: 19, of which 13 were waited for; matrix products, arithmetic and copies ran while one was open for 1% of the time, Pallas kernels for 7%

profile of v3, /device:TPU:0, one launch (start us, length us, event | category | flops | bytes accessed | tf_op | source)
XLA Modules:
  0.0 56.5 jit_solution(2040195665194357383)
XLA Ops:
  0.8 1.2 %copy-done = bf16[512,1024]{1,0:T(8,128)(2,1)S(1)} copy-done((bf16[512,1024]{1,0:T(8,128)(2,1)S(1)}, bf16[512,1024]{1,0:T(8,128)(2,1)}, u32[]{:S(2)}) %copy-start) | copy-done | bytes 1048600
  2.0 1.0 %copy-done.2 = bf16[512,512]{1,0:T(8,128)(2,1)S(1)} copy-done((bf16[512,512]{1,0:T(8,128)(2,1)S(1)}, bf16[512,512]{1,0:T(8,128)(2,1)}, u32[]{:S(2)}) %copy-start.2) | copy-done | bytes 524312
  3.0 1.0 %gradient_term.3 = f32[512,512]{1,0:T(8,128)S(1)} custom-call(s32[7]{0:T(128)S(1)} %stack.31.place, bf16[512,1024]{1,0:T(8,128)(2,1)S(1)} %copy-done, bf16[512,512]{1,0:T(8,128)(2,1)S(1)} %copy-done.2), custom_call_target="tpu_custom_call" | custom-call | flops 268435456 | bytes 1048576 | tf_op jit(solution)/shard_map/gradient_term/pallas_call | solution.py:112
  4.6 0.7 %stage_stats.1 = (bf16[320,512]{1,0:T(8,128)(2,1)S(1)}, bf16[160,384]{1,0:T(8,128)(2,1)S(1)}, bf16[160,256]{1,0:T(8,128)(2,1)S(1)}, bf16[160,128]{1,0:T(8,128)(2,1)S(1)}) custom-call(s32[7]{0:T(128)S(1)} %stack.31.place, f32[4,64,512]{2,1,0:T(8,128)S(1)} %copy-done.1), custom_call_target="tpu_custom_call" | custom-call | flops 655360 | bytes 1048576 | tf_op jit(solution)/shard_map/stage_stats/pallas_call | solution.py:318
  5.3 1.0 %gradient_term.2 = f32[512,512]{1,0:T(8,128)S(1)} custom-call(s32[7]{0:T(128)S(1)} %stack.31.place, bf16[512,1024]{1,0:T(8,128)(2,1)S(1)} %copy-done, bf16[512,512]{1,0:T(8,128)(2,1)S(1)} %copy-done.2), custom_call_target="tpu_custom_call" | custom-call | flops 268435456 | bytes 1048576 | tf_op jit(solution)/shard_map/gradient_term/pallas_call | solution.py:112
  7.1 2.9 %collective-permute-start.2 = (f32[128,512]{1,0:T(8,128)S(1)}, f32[128,512]{1,0:T(8,128)S(1)}, u32[]{:S(2)}, u32[]{:S(2)}) collective-permute-start(f32[128,512]{1,0:T(8,128)S(1)} %get-tuple-element.33), channel_id=1, source_target_pairs={{0,8},{1,17},{2,10},{3,19},{4,12},{5,21},{6,14},{7,23},{8,0},{9,25... | collective-permute-start | bytes 786440 | tf_op jit(solution)/shard_map/ppermute | solution.py:25
  10.0 3.6 %collective-permute-start.3 = (bf16[160,128]{1,0:T(8,128)(2,1)S(1)}, bf16[160,128]{1,0:T(8,128)(2,1)S(1)}, u32[]{:S(2)}, u32[]{:S(2)}) collective-permute-start(bf16[160,128]{1,0:T(8,128)(2,1)S(1)} %get-tuple-element.22), channel_id=1, source_target_pairs={{0,6},{1,7},{2,4},{3,5},{4,2},{5,3},{6,0},{7,1},{8,14},{9,15},{10,... | collective-permute-start | bytes 122888 | tf_op jit(solution)/shard_map/ppermute | solution.py:25
  14.2 1.7 %collective-permute-done.3 = bf16[160,128]{1,0:T(8,128)(2,1)S(1)} collective-permute-done((bf16[160,128]{1,0:T(8,128)(2,1)S(1)}, bf16[160,128]{1,0:T(8,128)(2,1)S(1)}, u32[]{:S(2)}, u32[]{:S(2)}) %collective-permute-start.3) | collective-permute-done | bytes 40992 | tf_op jit(solution)/shard_map/ppermute | solution.py:25
  15.9 1.6 %collective-permute-start.4 = (f32[128,512]{1,0:T(8,128)S(1)}, f32[128,512]{1,0:T(8,128)S(1)}, u32[]{:S(2)}, u32[]{:S(2)}) collective-permute-start(f32[128,512]{1,0:T(8,128)S(1)} %slice_add_fusion), channel_id=1, source_target_pairs={{0,16},{1,9},{2,18},{3,11},{4,20},{5,13},{6,22},{7,15},{8,24},{9,1... | collective-permute-start | bytes 786440 | tf_op jit(solution)/shard_map/ppermute | solution.py:25
  18.1 3.5 %collective-permute-start.6 = (bf16[160,256]{1,0:T(8,128)(2,1)S(1)}, bf16[160,256]{1,0:T(8,128)(2,1)S(1)}, u32[]{:S(2)}, u32[]{:S(2)}) collective-permute-start(bf16[160,256]{1,0:T(8,128)(2,1)S(1)} %get-tuple-element.25), channel_id=1, source_target_pairs={{0,4},{1,5},{2,6},{3,7},{4,0},{5,1},{6,2},{7,3},{8,12},{9,13},{10,... | collective-permute-start | bytes 245768 | tf_op jit(solution)/shard_map/ppermute | solution.py:25
  21.6 0.9 %collective-permute-done.1 = f32[128,512]{1,0:T(8,128)S(1)} collective-permute-done((f32[128,512]{1,0:T(8,128)S(1)}, f32[128,512]{1,0:T(8,128)S(1)}, u32[]{:S(2)}, u32[]{:S(2)}) %collective-permute-start.1) | collective-permute-done | bytes 262176 | tf_op jit(solution)/shard_map/ppermute | solution.py:25
  22.6 1.7 %collective-permute-done.6 = bf16[160,256]{1,0:T(8,128)(2,1)S(1)} collective-permute-done((bf16[160,256]{1,0:T(8,128)(2,1)S(1)}, bf16[160,256]{1,0:T(8,128)(2,1)S(1)}, u32[]{:S(2)}, u32[]{:S(2)}) %collective-permute-start.6) | collective-permute-done | bytes 81952 | tf_op jit(solution)/shard_map/ppermute | solution.py:25
  24.3 0.8 %collective-permute-start.7 = (bf16[160,768]{1,0:T(8,128)(2,1)S(1)}, bf16[160,768]{1,0:T(8,128)(2,1)S(1)}, u32[]{:S(2)}, u32[]{:S(2)}) collective-permute-start(bf16[160,768]{1,0:T(8,128)(2,1)S(1)} %constant_dynamic-update-slice_fusion.mine), channel_id=1, source_target_pairs={{0,8},{1,9},{2,10},{3,11},{4,12},{5,13},{6,14},{7,15},{8,0},{9,1},... | collective-permute-start | bytes 737288 | tf_op jit(solution)/shard_map/ppermute | solution.py:25
  25.1 2.7 %collective-permute-start.11 = (f32[32,512]{1,0:T(8,128)S(1)}, f32[32,512]{1,0:T(8,128)S(1)}, u32[]{:S(2)}, u32[]{:S(2)}) collective-permute-start(f32[32,512]{1,0:T(8,128)S(1)} %get-tuple-element.35), channel_id=1, source_target_pairs={{0,6},{1,7},{2,4},{3,5},{4,2},{5,3},{6,0},{7,1},{8,14},{9,15},{10,... | collective-permute-start | bytes 196616 | tf_op jit(solution)/shard_map/ppermute | solution.py:25
  28.4 1.2 %collective-permute-start.9 = (f32[32,512]{1,0:T(8,128)S(1)}, f32[32,512]{1,0:T(8,128)S(1)}, u32[]{:S(2)}, u32[]{:S(2)}) collective-permute-start(f32[32,512]{1,0:T(8,128)S(1)} %get-tuple-element.34), channel_id=1, source_target_pairs={{0,4},{1,5},{2,6},{3,7},{4,0},{5,1},{6,2},{7,3},{8,12},{9,13},{10,... | collective-permute-start | bytes 196616 | tf_op jit(solution)/shard_map/ppermute | solution.py:25
  29.6 1.4 %collective-permute-done.7.turned = bf16[160,768]{1,0:T(8,128)(2,1)S(1)} collective-permute-done((bf16[160,768]{1,0:T(8,128)(2,1)S(1)}, bf16[160,768]{1,0:T(8,128)(2,1)S(1)}, u32[]{:S(2)}, u32[]{:S(2)}) %collective-permute-start.7) | collective-permute-done | bytes 245792 | tf_op jit(solution)/shard_map/ppermute | solution.py:25
  31.1 0.7 %collective-permute-done.11 = f32[32,512]{1,0:T(8,128)S(1)} collective-permute-done((f32[32,512]{1,0:T(8,128)S(1)}, f32[32,512]{1,0:T(8,128)S(1)}, u32[]{:S(2)}, u32[]{:S(2)}) %collective-permute-start.11) | collective-permute-done | bytes 65568 | tf_op jit(solution)/shard_map/ppermute | solution.py:25
  32.4 1.1 %collective-permute-done.9 = f32[32,512]{1,0:T(8,128)S(1)} collective-permute-done((f32[32,512]{1,0:T(8,128)S(1)}, f32[32,512]{1,0:T(8,128)S(1)}, u32[]{:S(2)}, u32[]{:S(2)}) %collective-permute-start.9) | collective-permute-done | bytes 65568 | tf_op jit(solution)/shard_map/ppermute | solution.py:25
  33.6 1.3 %collective-permute-start.14 = (bf16[32,512]{1,0:T(8,128)(2,1)S(1)}, bf16[32,512]{1,0:T(8,128)(2,1)S(1)}, u32[]{:S(2)}, u32[]{:S(2)}) collective-permute-start(bf16[32,512]{1,0:T(8,128)(2,1)S(1)} %add_convert_fusion), channel_id=1, source_target_pairs={{0,6},{1,7},{2,4},{3,5},{4,2},{5,3},{6,0},{7,1},{8,14},{9,15},{10,... | collective-permute-start | bytes 98312 | tf_op jit(solution)/shard_map/ppermute | solution.py:25
  35.4 2.6 %collective-permute-start.12 = (bf16[32,512]{1,0:T(8,128)(2,1)S(1)}, bf16[32,512]{1,0:T(8,128)(2,1)S(1)}, u32[]{:S(2)}, u32[]{:S(2)}) collective-permute-start(bf16[32,512]{1,0:T(8,128)(2,1)S(1)} %add_convert_fusion), channel_id=1, source_target_pairs={{0,4},{1,5},{2,6},{3,7},{4,0},{5,1},{6,2},{7,3},{8,12},{9,13},{10,... | collective-permute-start | bytes 98312 | tf_op jit(solution)/shard_map/ppermute | solution.py:25
  38.0 1.3 %collective-permute-done.14 = bf16[32,512]{1,0:T(8,128)(2,1)S(1)} collective-permute-done((bf16[32,512]{1,0:T(8,128)(2,1)S(1)}, bf16[32,512]{1,0:T(8,128)(2,1)S(1)}, u32[]{:S(2)}, u32[]{:S(2)}) %collective-permute-start.14) | collective-permute-done | bytes 32800 | tf_op jit(solution)/shard_map/ppermute | solution.py:25
  39.4 0.9 %collective-permute-done.12 = bf16[32,512]{1,0:T(8,128)(2,1)S(1)} collective-permute-done((bf16[32,512]{1,0:T(8,128)(2,1)S(1)}, bf16[32,512]{1,0:T(8,128)(2,1)S(1)}, u32[]{:S(2)}, u32[]{:S(2)}) %collective-permute-start.12) | collective-permute-done | bytes 32800 | tf_op jit(solution)/shard_map/ppermute | solution.py:25
  40.2 1.4 %collective-permute-start.15 = (bf16[128,512]{1,0:T(8,128)(2,1)S(1)}, bf16[128,512]{1,0:T(8,128)(2,1)S(1)}, u32[]{:S(2)}, u32[]{:S(2)}) collective-permute-start(bf16[128,512]{1,0:T(8,128)(2,1)S(1)} %pad_maximum_fusion.refs_0_), channel_id=1, source_target_pairs={{0,16},{1,9},{2,18},{3,11},{4,20},{5,13},{6,22},{7,15},{8,24},{9,1... | collective-permute-start | bytes 393224 | tf_op jit(solution)/shard_map/ppermute | solution.py:25
  41.6 0.7 %collective-permute-start.16 = (bf16[128,512]{1,0:T(8,128)(2,1)S(1)}, bf16[128,512]{1,0:T(8,128)(2,1)S(1)}, u32[]{:S(2)}, u32[]{:S(2)}) collective-permute-start(bf16[128,512]{1,0:T(8,128)(2,1)S(1)} %pad_maximum_fusion.refs_0_), channel_id=1, source_target_pairs={{0,8},{1,17},{2,10},{3,19},{4,12},{5,21},{6,14},{7,23},{8,0},{9,25... | collective-permute-start | bytes 393224 | tf_op jit(solution)/shard_map/ppermute | solution.py:25
  42.4 1.4 %collective-permute-start.17 = (bf16[128,512]{1,0:T(8,128)(2,1)S(1)}, bf16[128,512]{1,0:T(8,128)(2,1)S(1)}, u32[]{:S(2)}, u32[]{:S(2)}) collective-permute-start(bf16[128,512]{1,0:T(8,128)(2,1)S(1)} %pad_maximum_fusion.refs_0_), channel_id=1, source_target_pairs={{0,24},{1,25},{2,26},{3,27},{4,28},{5,29},{6,30},{7,31},{8,16},{9,... | collective-permute-start | bytes 393224 | tf_op jit(solution)/shard_map/ppermute | solution.py:25
  43.8 1.9 %whole_stats.1.damped = f32[2,512,512]{2,1,0:T(8,128)S(1)} custom-call(s32[7]{0:T(128)S(1)} %stack.31.place, bf16[320,512]{1,0:T(8,128)(2,1)S(1)} %get-tuple-element.21.whole, bf16[160,1280]{1,0:T(8,128)(2,1)S(1)} %collective-permute-done.8.swapped, bf16[160,768]{1,0:T(8,128)(2,1)S(1)} %constant_dynamic-update-slice_fusion.mine, ...), custom_call_target="tpu_custom_call" | custom-call | flops 2097152 | bytes 3145728 | tf_op jit(solution)/shard_map/whole_stats/pallas_call | solution.py:343
  45.8 0.8 %collective-permute-done.16.refs_2_ = bf16[128,512]{1,0:T(8,128)(2,1)S(1)} collective-permute-done((bf16[128,512]{1,0:T(8,128)(2,1)S(1)}, bf16[128,512]{1,0:T(8,128)(2,1)S(1)}, u32[]{:S(2)}, u32[]{:S(2)}) %collective-permute-start.16) | collective-permute-done | bytes 131104 | tf_op jit(solution)/shard_map/ppermute | solution.py:25
  46.6 1.6 %collective-permute-done.17.refs_3_ = bf16[128,512]{1,0:T(8,128)(2,1)S(1)} collective-permute-done((bf16[128,512]{1,0:T(8,128)(2,1)S(1)}, bf16[128,512]{1,0:T(8,128)(2,1)S(1)}, u32[]{:S(2)}, u32[]{:S(2)}) %collective-permute-start.17) | collective-permute-done | bytes 131104 | tf_op jit(solution)/shard_map/ppermute | solution.py:25
  48.2 4.7 %precondition.1 = (f32[3,64,512]{2,1,0:T(8,128)S(1)}, f32[3,64,512]{2,1,0:T(8,128)S(1)}) custom-call(s32[7]{0:T(128)S(1)} %stack.31.place, f32[2,512,512]{2,1,0:T(8,128)S(1)} %whole_stats.1.damped, bf16[128,512]{1,0:T(8,128)(2,1)S(1)} %pad_maximum_fusion.refs_0_, bf16[128,512]{1,0:T(8,128)(2,1)S(1)} %collective-permute-done.15.refs_1_, ...), custom_call_target="tpu_custom_call" | custom-call | flops 2684354560 | bytes 4194304 | tf_op jit(solution)/shard_map/precondition/pallas_call | solution.py:384
  53.2 1.6 %collective-permute-done.18 = f32[3,64,512]{2,1,0:T(8,128)S(1)} collective-permute-done((f32[3,64,512]{2,1,0:T(8,128)S(1)}, f32[3,64,512]{2,1,0:T(8,128)S(1)}, u32[]{:S(2)}, u32[]{:S(2)}) %collective-permute-start.18) | collective-permute-done | bytes 393248 | tf_op jit(solution)/shard_map/ppermute | solution.py:25
  54.7 0.8 %broadcast_select_fusion = f32[2,64,512]{2,1,0:T(8,128)} fusion(f32[64,512]{1,0:T(8,128)S(1)} %slice_bitcast_fusion, f32[64,512]{1,0:T(8,128)S(1)} %slice_bitcast_fusion.1, pred[2]{0:T(512)(128)(4,1)S(1)} %iota_compare_fusion), kind=kLoop, calls=%fused_computation.8 | loop fusion | flops 65536 | bytes 524290 | tf_op jit(solution)/shard_map/jit(_where)/select_n | solution.py:407
  55.5 0.9 %fusion = f32[4,64,512]{2,1,0:T(8,128)} fusion(f32[4,64,512]{2,1,0:T(8,128)S(1)} %copy-done.1, f32[2,64,512]{2,1,0:T(8,128)S(1)} %slice.30, f32[2,64,512]{2,1,0:T(8,128)S(1)} %slice.24, pred[4]{0:T(512)(128)(4,1)S(1)} %broadcast_in_dim.63), kind=kLoop, calls=%fused_computation.1 | loop fusion | flops 262144 | bytes 1572868 | tf_op jit(solution)/shard_map/add | solution.py:407
  (41 shorter events, 4.8 us)
Async XLA Ops:
  0.8 1.2 %copy-start = (bf16[512,1024]{1,0:T(8,128)(2,1)S(1)}, bf16[512,1024]{1,0:T(8,128)(2,1)}, u32[]{:S(2)}) copy-start(bf16[512,1024]{1,0:T(8,128)(2,1)} %grads.3) | copy-start | bytes 3145732
  2.0 1.0 %copy-start.2 = (bf16[512,512]{1,0:T(8,128)(2,1)S(1)}, bf16[512,512]{1,0:T(8,128)(2,1)}, u32[]{:S(2)}) copy-start(bf16[512,512]{1,0:T(8,128)(2,1)} %acts.3) | copy-start | bytes 1572868
  3.0 1.5 %copy-start.1 = (f32[4,64,512]{2,1,0:T(8,128)S(1)}, f32[4,64,512]{2,1,0:T(8,128)}, u32[]{:S(2)}) copy-start(f32[4,64,512]{2,1,0:T(8,128)} %stats.1) | copy-start | bytes 1572868
  4.1 2.8 %collective-permute-start = (f32[512,512]{1,0:T(8,128)S(1)}, f32[512,512]{1,0:T(8,128)S(1)}, u32[]{:S(2)}, u32[]{:S(2)}) collective-permute-start(f32[512,512]{1,0:T(8,128)S(1)} %gradient_term.3), channel_id=1, source_target_pairs={{0,1},{1,0},{2,3},{3,2},{4,5},{5,4},{6,7},{7,6},{8,9},{9,8},{10,11... | collective-permute-start | bytes 3145736 | tf_op jit(solution)/shard_map/ppermute | solution.py:25
  7.1 8.7 %collective-permute-start.2 = (f32[128,512]{1,0:T(8,128)S(1)}, f32[128,512]{1,0:T(8,128)S(1)}, u32[]{:S(2)}, u32[]{:S(2)}) collective-permute-start(f32[128,512]{1,0:T(8,128)S(1)} %get-tuple-element.33), channel_id=1, source_target_pairs={{0,8},{1,17},{2,10},{3,19},{4,12},{5,21},{6,14},{7,23},{8,0},{9,25... | collective-permute-start | bytes 786440 | tf_op jit(solution)/shard_map/ppermute | solution.py:25
  10.0 5.8 %collective-permute-start.3 = (bf16[160,128]{1,0:T(8,128)(2,1)S(1)}, bf16[160,128]{1,0:T(8,128)(2,1)S(1)}, u32[]{:S(2)}, u32[]{:S(2)}) collective-permute-start(bf16[160,128]{1,0:T(8,128)(2,1)S(1)} %get-tuple-element.22), channel_id=1, source_target_pairs={{0,6},{1,7},{2,4},{3,5},{4,2},{5,3},{6,0},{7,1},{8,14},{9,15},{10,... | collective-permute-start | bytes 122888 | tf_op jit(solution)/shard_map/ppermute | solution.py:25
  13.6 8.9 %collective-permute-start.1 = (f32[128,512]{1,0:T(8,128)S(1)}, f32[128,512]{1,0:T(8,128)S(1)}, u32[]{:S(2)}, u32[]{:S(2)}) collective-permute-start(f32[128,512]{1,0:T(8,128)S(1)} %get-tuple-element.32), channel_id=1, source_target_pairs={{0,8},{1,17},{2,10},{3,19},{4,12},{5,21},{6,14},{7,23},{8,0},{9,25... | collective-permute-start | bytes 786440 | tf_op jit(solution)/shard_map/ppermute | solution.py:25
  15.9 6.6 %collective-permute-start.4 = (f32[128,512]{1,0:T(8,128)S(1)}, f32[128,512]{1,0:T(8,128)S(1)}, u32[]{:S(2)}, u32[]{:S(2)}) collective-permute-start(f32[128,512]{1,0:T(8,128)S(1)} %slice_add_fusion), channel_id=1, source_target_pairs={{0,16},{1,9},{2,18},{3,11},{4,20},{5,13},{6,22},{7,15},{8,24},{9,1... | collective-permute-start | bytes 786440 | tf_op jit(solution)/shard_map/ppermute | solution.py:25
  17.5 6.8 %collective-permute-start.5 = (bf16[160,384]{1,0:T(8,128)(2,1)S(1)}, bf16[160,384]{1,0:T(8,128)(2,1)S(1)}, u32[]{:S(2)}, u32[]{:S(2)}) collective-permute-start(bf16[160,384]{1,0:T(8,128)(2,1)S(1)} %get-tuple-element.24), channel_id=1, source_target_pairs={{0,2},{1,3},{2,0},{3,1},{4,6},{5,7},{6,4},{7,5},{8,10},{9,11},{10,... | collective-permute-start | bytes 368648 | tf_op jit(solution)/shard_map/ppermute | solution.py:25
  18.1 6.1 %collective-permute-start.6 = (bf16[160,256]{1,0:T(8,128)(2,1)S(1)}, bf16[160,256]{1,0:T(8,128)(2,1)S(1)}, u32[]{:S(2)}, u32[]{:S(2)}) collective-permute-start(bf16[160,256]{1,0:T(8,128)(2,1)S(1)} %get-tuple-element.25), channel_id=1, source_target_pairs={{0,4},{1,5},{2,6},{3,7},{4,0},{5,1},{6,2},{7,3},{8,12},{9,13},{10,... | collective-permute-start | bytes 245768 | tf_op jit(solution)/shard_map/ppermute | solution.py:25
  24.3 6.7 %collective-permute-start.7 = (bf16[160,768]{1,0:T(8,128)(2,1)S(1)}, bf16[160,768]{1,0:T(8,128)(2,1)S(1)}, u32[]{:S(2)}, u32[]{:S(2)}) collective-permute-start(bf16[160,768]{1,0:T(8,128)(2,1)S(1)} %constant_dynamic-update-slice_fusion.mine), channel_id=1, source_target_pairs={{0,8},{1,9},{2,10},{3,11},{4,12},{5,13},{6,14},{7,15},{8,0},{9,1},... | collective-permute-start | bytes 737288 | tf_op jit(solution)/shard_map/ppermute | solution.py:25
  25.1 6.7 %collective-permute-start.11 = (f32[32,512]{1,0:T(8,128)S(1)}, f32[32,512]{1,0:T(8,128)S(1)}, u32[]{:S(2)}, u32[]{:S(2)}) collective-permute-start(f32[32,512]{1,0:T(8,128)S(1)} %get-tuple-element.35), channel_id=1, source_target_pairs={{0,6},{1,7},{2,4},{3,5},{4,2},{5,3},{6,0},{7,1},{8,14},{9,15},{10,... | collective-permute-start | bytes 196616 | tf_op jit(solution)/shard_map/ppermute | solution.py:25
  27.8 4.6 %collective-permute-start.10 = (f32[32,512]{1,0:T(8,128)S(1)}, f32[32,512]{1,0:T(8,128)S(1)}, u32[]{:S(2)}, u32[]{:S(2)}) collective-permute-start(f32[32,512]{1,0:T(8,128)S(1)} %get-tuple-element.36), channel_id=1, source_target_pairs={{0,2},{1,3},{2,0},{3,1},{4,6},{5,7},{6,4},{7,5},{8,10},{9,11},{10,... | collective-permute-start | bytes 196616 | tf_op jit(solution)/shard_map/ppermute | solution.py:25
  28.4 5.2 %collective-permute-start.9 = (f32[32,512]{1,0:T(8,128)S(1)}, f32[32,512]{1,0:T(8,128)S(1)}, u32[]{:S(2)}, u32[]{:S(2)}) collective-permute-start(f32[32,512]{1,0:T(8,128)S(1)} %get-tuple-element.34), channel_id=1, source_target_pairs={{0,4},{1,5},{2,6},{3,7},{4,0},{5,1},{6,2},{7,3},{8,12},{9,13},{10,... | collective-permute-start | bytes 196616 | tf_op jit(solution)/shard_map/ppermute | solution.py:25
  31.0 12.8 %collective-permute-start.8 = (bf16[160,1280]{1,0:T(8,128)(2,1)S(1)}, bf16[160,1280]{1,0:T(8,128)(2,1)S(1)}, u32[]{:S(2)}, u32[]{:S(2)}) collective-permute-start(bf16[160,1280]{1,0:T(8,128)(2,1)S(1)} %maximum_maximum_fusion), channel_id=1, source_target_pairs={{0,1},{1,0},{2,3},{3,2},{4,5},{5,4},{6,7},{7,6},{8,9},{9,8},{10,11... | collective-permute-start | bytes 1228808 | tf_op jit(solution)/shard_map/ppermute | solution.py:25
  33.6 5.8 %collective-permute-start.14 = (bf16[32,512]{1,0:T(8,128)(2,1)S(1)}, bf16[32,512]{1,0:T(8,128)(2,1)S(1)}, u32[]{:S(2)}, u32[]{:S(2)}) collective-permute-start(bf16[32,512]{1,0:T(8,128)(2,1)S(1)} %add_convert_fusion), channel_id=1, source_target_pairs={{0,6},{1,7},{2,4},{3,5},{4,2},{5,3},{6,0},{7,1},{8,14},{9,15},{10,... | collective-permute-start | bytes 98312 | tf_op jit(solution)/shard_map/ppermute | solution.py:25
  34.8 4.5 %collective-permute-start.13 = (bf16[32,512]{1,0:T(8,128)(2,1)S(1)}, bf16[32,512]{1,0:T(8,128)(2,1)S(1)}, u32[]{:S(2)}, u32[]{:S(2)}) collective-permute-start(bf16[32,512]{1,0:T(8,128)(2,1)S(1)} %add_convert_fusion), channel_id=1, source_target_pairs={{0,2},{1,3},{2,0},{3,1},{4,6},{5,7},{6,4},{7,5},{8,10},{9,11},{10,... | collective-permute-start | bytes 98312 | tf_op jit(solution)/shard_map/ppermute | solution.py:25
  35.4 4.8 %collective-permute-start.12 = (bf16[32,512]{1,0:T(8,128)(2,1)S(1)}, bf16[32,512]{1,0:T(8,128)(2,1)S(1)}, u32[]{:S(2)}, u32[]{:S(2)}) collective-permute-start(bf16[32,512]{1,0:T(8,128)(2,1)S(1)} %add_convert_fusion), channel_id=1, source_target_pairs={{0,4},{1,5},{2,6},{3,7},{4,0},{5,1},{6,2},{7,3},{8,12},{9,13},{10,... | collective-permute-start | bytes 98312 | tf_op jit(solution)/shard_map/ppermute | solution.py:25
  40.2 5.5 %collective-permute-start.15 = (bf16[128,512]{1,0:T(8,128)(2,1)S(1)}, bf16[128,512]{1,0:T(8,128)(2,1)S(1)}, u32[]{:S(2)}, u32[]{:S(2)}) collective-permute-start(bf16[128,512]{1,0:T(8,128)(2,1)S(1)} %pad_maximum_fusion.refs_0_), channel_id=1, source_target_pairs={{0,16},{1,9},{2,18},{3,11},{4,20},{5,13},{6,22},{7,15},{8,24},{9,1... | collective-permute-start | bytes 393224 | tf_op jit(solution)/shard_map/ppermute | solution.py:25
  41.6 5.0 %collective-permute-start.16 = (bf16[128,512]{1,0:T(8,128)(2,1)S(1)}, bf16[128,512]{1,0:T(8,128)(2,1)S(1)}, u32[]{:S(2)}, u32[]{:S(2)}) collective-permute-start(bf16[128,512]{1,0:T(8,128)(2,1)S(1)} %pad_maximum_fusion.refs_0_), channel_id=1, source_target_pairs={{0,8},{1,17},{2,10},{3,19},{4,12},{5,21},{6,14},{7,23},{8,0},{9,25... | collective-permute-start | bytes 393224 | tf_op jit(solution)/shard_map/ppermute | solution.py:25
  42.4 5.9 %collective-permute-start.17 = (bf16[128,512]{1,0:T(8,128)(2,1)S(1)}, bf16[128,512]{1,0:T(8,128)(2,1)S(1)}, u32[]{:S(2)}, u32[]{:S(2)}) collective-permute-start(bf16[128,512]{1,0:T(8,128)(2,1)S(1)} %pad_maximum_fusion.refs_0_), channel_id=1, source_target_pairs={{0,24},{1,25},{2,26},{3,27},{4,28},{5,29},{6,30},{7,31},{8,16},{9,... | collective-permute-start | bytes 393224 | tf_op jit(solution)/shard_map/ppermute | solution.py:25
  52.9 1.8 %collective-permute-start.18 = (f32[3,64,512]{2,1,0:T(8,128)S(1)}, f32[3,64,512]{2,1,0:T(8,128)S(1)}, u32[]{:S(2)}, u32[]{:S(2)}) collective-permute-start(f32[3,64,512]{2,1,0:T(8,128)S(1)} %get-tuple-element.31), channel_id=1, source_target_pairs={{0,1},{1,0},{2,3},{3,2},{4,5},{5,4},{6,7},{7,6},{8,9},{9,8},{10,11... | collective-permute-start | bytes 1179656 | tf_op jit(solution)/shard_map/ppermute | solution.py:25

commit v4 on v3

--- a/solution.py
+++ b/solution.py
@@ -218,18 +218,23 @@
             out[side, pl.ds(start, rows), :] = values + jnp.where(on_diagonal(rows, order, start), vector, 0.0)
 
 
-def step_kernel(place, damped, *refs, pieces, rows, band):
+def step_kernel(place, damped, stats, *refs, pieces, rows, band):
     parts = refs[:pieces]
-    own, sent, grad, gram, scaled, power, factors, offs, seconds, left_root, right_rows = refs[pieces:]
+    fresh, own, sent, grad, gram, scaled, power, factors, offs, seconds, left_root, right_rows, added, sems = refs[pieces:]
+    tiles = stats.shape[0] // 2
     order = grad.shape[0]
     for index, part in enumerate(parts):
         for low in range(0, part.shape[0], rows):
             block = (index * part.shape[0] + low) // rows
             start = pl.multiple_of((block ^ place[1]) * rows, rows)
             grad[pl.ds(start, rows), :] = part[low : low + rows, :]
+    copies = []
     for side in range(2):
         gram[side] = dot(grad[...], grad[...], (side, side))
-        own[side] = gram[side, pl.ds(pl.multiple_of(place[3], band), band), :]
+        chain = side * tiles + place[0]
+        added[side] = stats[chain] + gram[side, pl.ds(pl.multiple_of(place[3], band), band), :]
+        copies.append(pltpu.make_async_copy(added.at[side], fresh.at[chain], sems.at[side]))
+        copies[side].start()
         sent[side] = gram[side, pl.ds(pl.multiple_of(place[4], band), band), :]
     step = min(order, LANES)
     strips = [slice(low, low + step) for low in range(0, order, step)]
@@ -305,8 +310,27 @@
     high = inner.astype(BF16)
     low = (inner - high.astype(F32)).astype(BF16)
     update = (dot(high, left_root[...]) + dot(low, left_root[...])) * math.sqrt(order)
-    own[2] = update[:band]
+    own[...] = update[:band]
     sent[2] = update[band:]
+    for copy in copies:
+        copy.wait()
+
+
+def finish_kernel(place, fresh, stats, own, sent, out, update, added, sems):
+    tiles = update.shape[0]
+    other = 1 - place[0]
+    copies = [
+        pltpu.make_async_copy(own, update.at[place[0]], sems.at[0]),
+        pltpu.make_async_copy(sent.at[2], update.at[other], sems.at[1]),
+    ]
+    for side in range(2):
+        chain = side * tiles + other
+        added[side] = stats[chain] + sent[side]
+        copies.append(pltpu.make_async_copy(added.at[side], out.at[chain], sems.at[2 + side]))
+    for copy in copies:
+        copy.start()
+    for copy in copies:
+        copy.wait()
 
 
 def stage_stats(place, stats_old, tiles, lines):
@@ -379,13 +403,19 @@
         joined = pieces[0] if len(pieces) == 1 else jnp.concatenate(pieces, axis=0)
         pieces = gather_phase(joined, kind, bits)
 
-    result = jax.ShapeDtypeStruct((3, band, order), F32)
+    rows_pair = (2, band, order)
     square = (2, order, order)
-    own, sent = pl.pallas_call(
+    anywhere = pl.BlockSpec(memory_space=pl.ANY)
+    new_shape = jax.ShapeDtypeStruct(stats_old.shape, F32)
+    fresh, own, sent = pl.pallas_call(
         functools.partial(step_kernel, pieces=len(pieces), rows=rows, band=band),
-        out_shape=(result, result),
-        in_specs=[SMEM] + vmem(1 + len(pieces)),
-        out_specs=tuple(vmem(2)),
+        out_shape=(
+            new_shape,
+            jax.ShapeDtypeStruct((band, order), F32),
+            jax.ShapeDtypeStruct((3, band, order), F32),
+        ),
+        in_specs=[SMEM] + vmem(2 + len(pieces)),
+        out_specs=(anywhere, *vmem(2)),
         scratch_shapes=[
             pltpu.VMEM((order, order), BF16),
             pltpu.VMEM(square, F32),
@@ -396,15 +426,25 @@
             pltpu.VMEM(square, BF16),
             pltpu.VMEM((order, order), BF16),
             pltpu.VMEM((2 * band, order), BF16),
+            pltpu.VMEM(rows_pair, F32),
+            pltpu.SemaphoreType.DMA((2,)),
         ],
         compiler_params=pltpu.CompilerParams(vmem_limit_bytes=32 << 20),
         cost_estimate=pl.CostEstimate(flops=20 * order**3, bytes_accessed=order * order * 16, transcendentals=0),
         name="precondition",
-    )(place, damped, *pieces)
+    )(place, damped, stats_old, *pieces)
     sent = swap(sent, CORES)
-    own_tile = lax.broadcasted_iota(jnp.int32, (1, tiles, 1, 1), 1) == core
-    moved = jnp.where(own_tile, own[:2, None], sent[:2, None]).reshape(stats_old.shape)
-    return stats_old + moved, jnp.where(own_tile[0], own[2][None], sent[2][None])
+    return pl.pallas_call(
+        finish_kernel,
+        out_shape=(new_shape, jax.ShapeDtypeStruct((tiles, band, order), F32)),
+        in_specs=[SMEM, anywhere] + vmem(3),
+        out_specs=(anywhere, anywhere),
+        scratch_shapes=[pltpu.VMEM(rows_pair, F32), pltpu.SemaphoreType.DMA((4,))],
+        input_output_aliases={1: 0},
+        compiler_params=pltpu.CompilerParams(vmem_limit_bytes=8 << 20),
+        cost_estimate=pl.CostEstimate(flops=band * order * 4, bytes_accessed=band * order * 32, transcendentals=0),
+        name="finish",
+    )(place, fresh, stats_old, own, sent)
 
 
 def solution(mesh):

time: 56.7 us -> 56.3 us (level)
  other arithmetic: 2.11 us -> 0.37 us
  Pallas kernels: 9.41 us -> 10.8 us
    pallas_call x0 -> x1, Pallas kernels: none -> 1.36 us  [on_device(): pl.pallas_call(finish_kernel, out_shape=(new_shape, jax.ShapeDtypeStruct(...]
    add x1 -> x0, other arithmetic: 0.95 us -> none  [on_device(): stats_old + moved]
    select_n x1 -> x0, other arithmetic: 0.8 us -> none  [on_device(): jnp.where(own_tile[0], own[2][None], sent[2][None])]
  transfers between devices with their start and end apart: 19 -> 19, of which waited for: 13 -> 13; matrix products, arithmetic and copies ran while one was open for 1% -> 0% of each run, Pallas kernels for 7% -> 7%
where the time goes in v4:
time: 56.3 us; the launch traced here: 56.1 us
  starting transfers between devices  26.7 us (47%)
  waiting for transfers between devices  14.9 us (26%)
  Pallas kernels  10.8 us (19%)
  local copies, waits for them, and re-layouts  2.47 us (4%)
  between operations  0.81 us (1%)
    ppermute x19, starting transfers between devices, swap(): return lax.ppermute(array, ('rep', 'grp'), pairs)  26.7 us
    ppermute x19, waiting for transfers between devices, swap(): return lax.ppermute(array, ('rep', 'grp'), pairs)  14.9 us
    pallas_call x1, Pallas kernels, on_device(): pl.pallas_call(functools.partial(step_kernel, pieces=len(pieces), rows=ro...  4.74 us
    unnamed x8, local copies, waits for them, and re-layouts  2.29 us
    pallas_call x2, Pallas kernels, gradient_term(): pl.pallas_call(functools.partial(term_kernel, other=other, rows=rows), ou...  2.04 us
    pallas_call x1, Pallas kernels, whole_stats(): pl.pallas_call(kernel, out_shape=jax.ShapeDtypeStruct((2, order, order),...  1.95 us
    pallas_call x1, Pallas kernels, on_device(): pl.pallas_call(finish_kernel, out_shape=(new_shape, jax.ShapeDtypeStruct(...  1.36 us
  transfers between devices with their start and end apart: 19, of which 13 were waited for; matrix products, arithmetic and copies ran while one was open for 0% of the time, Pallas kernels for 7%

profile of v4, /device:TPU:0, one launch (start us, length us, event | category | flops | bytes accessed | tf_op | source)
XLA Modules:
  0.0 56.1 jit_solution(1791011738885245135)
XLA Ops:
  0.8 1.2 %copy-done = bf16[512,1024]{1,0:T(8,128)(2,1)S(1)} copy-done((bf16[512,1024]{1,0:T(8,128)(2,1)S(1)}, bf16[512,1024]{1,0:T(8,128)(2,1)}, u32[]{:S(2)}) %copy-start) | copy-done | bytes 1048600
  2.0 1.0 %copy-done.2 = bf16[512,512]{1,0:T(8,128)(2,1)S(1)} copy-done((bf16[512,512]{1,0:T(8,128)(2,1)S(1)}, bf16[512,512]{1,0:T(8,128)(2,1)}, u32[]{:S(2)}) %copy-start.2) | copy-done | bytes 524312
  3.0 1.0 %gradient_term.3 = f32[512,512]{1,0:T(8,128)S(1)} custom-call(s32[7]{0:T(128)S(1)} %stack.31.place, bf16[512,1024]{1,0:T(8,128)(2,1)S(1)} %copy-done, bf16[512,512]{1,0:T(8,128)(2,1)S(1)} %copy-done.2), custom_call_target="tpu_custom_call" | custom-call | flops 268435456 | bytes 1048576 | tf_op jit(solution)/shard_map/gradient_term/pallas_call | solution.py:112
  4.6 0.7 %stage_stats.1 = (bf16[320,512]{1,0:T(8,128)(2,1)S(1)}, bf16[160,384]{1,0:T(8,128)(2,1)S(1)}, bf16[160,256]{1,0:T(8,128)(2,1)S(1)}, bf16[160,128]{1,0:T(8,128)(2,1)S(1)}) custom-call(s32[7]{0:T(128)S(1)} %stack.31.place, f32[4,64,512]{2,1,0:T(8,128)S(1)} %copy-done.1), custom_call_target="tpu_custom_call" | custom-call | flops 655360 | bytes 1048576 | tf_op jit(solution)/shard_map/stage_stats/pallas_call | solution.py:342
  5.3 1.0 %gradient_term.2 = f32[512,512]{1,0:T(8,128)S(1)} custom-call(s32[7]{0:T(128)S(1)} %stack.31.place, bf16[512,1024]{1,0:T(8,128)(2,1)S(1)} %copy-done, bf16[512,512]{1,0:T(8,128)(2,1)S(1)} %copy-done.2), custom_call_target="tpu_custom_call" | custom-call | flops 268435456 | bytes 1048576 | tf_op jit(solution)/shard_map/gradient_term/pallas_call | solution.py:112
  7.1 2.9 %collective-permute-start.2 = (f32[128,512]{1,0:T(8,128)S(1)}, f32[128,512]{1,0:T(8,128)S(1)}, u32[]{:S(2)}, u32[]{:S(2)}) collective-permute-start(f32[128,512]{1,0:T(8,128)S(1)} %get-tuple-element.35), channel_id=1, source_target_pairs={{0,8},{1,17},{2,10},{3,19},{4,12},{5,21},{6,14},{7,23},{8,0},{9,25... | collective-permute-start | bytes 786440 | tf_op jit(solution)/shard_map/ppermute | solution.py:25
  10.0 3.6 %collective-permute-start.3 = (bf16[160,128]{1,0:T(8,128)(2,1)S(1)}, bf16[160,128]{1,0:T(8,128)(2,1)S(1)}, u32[]{:S(2)}, u32[]{:S(2)}) collective-permute-start(bf16[160,128]{1,0:T(8,128)(2,1)S(1)} %get-tuple-element.23), channel_id=1, source_target_pairs={{0,6},{1,7},{2,4},{3,5},{4,2},{5,3},{6,0},{7,1},{8,14},{9,15},{10,... | collective-permute-start | bytes 122888 | tf_op jit(solution)/shard_map/ppermute | solution.py:25
  14.2 1.7 %collective-permute-done.3 = bf16[160,128]{1,0:T(8,128)(2,1)S(1)} collective-permute-done((bf16[160,128]{1,0:T(8,128)(2,1)S(1)}, bf16[160,128]{1,0:T(8,128)(2,1)S(1)}, u32[]{:S(2)}, u32[]{:S(2)}) %collective-permute-start.3) | collective-permute-done | bytes 40992 | tf_op jit(solution)/shard_map/ppermute | solution.py:25
  15.9 1.6 %collective-permute-start.4 = (f32[128,512]{1,0:T(8,128)S(1)}, f32[128,512]{1,0:T(8,128)S(1)}, u32[]{:S(2)}, u32[]{:S(2)}) collective-permute-start(f32[128,512]{1,0:T(8,128)S(1)} %slice_add_fusion), channel_id=1, source_target_pairs={{0,16},{1,9},{2,18},{3,11},{4,20},{5,13},{6,22},{7,15},{8,24},{9,1... | collective-permute-start | bytes 786440 | tf_op jit(solution)/shard_map/ppermute | solution.py:25
  17.5 0.7 %collective-permute-start.5 = (bf16[160,384]{1,0:T(8,128)(2,1)S(1)}, bf16[160,384]{1,0:T(8,128)(2,1)S(1)}, u32[]{:S(2)}, u32[]{:S(2)}) collective-permute-start(bf16[160,384]{1,0:T(8,128)(2,1)S(1)} %get-tuple-element.25), channel_id=1, source_target_pairs={{0,2},{1,3},{2,0},{3,1},{4,6},{5,7},{6,4},{7,5},{8,10},{9,11},{10,... | collective-permute-start | bytes 368648 | tf_op jit(solution)/shard_map/ppermute | solution.py:25
  18.1 3.5 %collective-permute-start.6 = (bf16[160,256]{1,0:T(8,128)(2,1)S(1)}, bf16[160,256]{1,0:T(8,128)(2,1)S(1)}, u32[]{:S(2)}, u32[]{:S(2)}) collective-permute-start(bf16[160,256]{1,0:T(8,128)(2,1)S(1)} %get-tuple-element.26), channel_id=1, source_target_pairs={{0,4},{1,5},{2,6},{3,7},{4,0},{5,1},{6,2},{7,3},{8,12},{9,13},{10,... | collective-permute-start | bytes 245768 | tf_op jit(solution)/shard_map/ppermute | solution.py:25
  21.6 0.8 %collective-permute-done.1 = f32[128,512]{1,0:T(8,128)S(1)} collective-permute-done((f32[128,512]{1,0:T(8,128)S(1)}, f32[128,512]{1,0:T(8,128)S(1)}, u32[]{:S(2)}, u32[]{:S(2)}) %collective-permute-start.1) | collective-permute-done | bytes 262176 | tf_op jit(solution)/shard_map/ppermute | solution.py:25
  22.5 1.7 %collective-permute-done.6 = bf16[160,256]{1,0:T(8,128)(2,1)S(1)} collective-permute-done((bf16[160,256]{1,0:T(8,128)(2,1)S(1)}, bf16[160,256]{1,0:T(8,128)(2,1)S(1)}, u32[]{:S(2)}, u32[]{:S(2)}) %collective-permute-start.6) | collective-permute-done | bytes 81952 | tf_op jit(solution)/shard_map/ppermute | solution.py:25
  24.3 0.8 %collective-permute-start.7 = (bf16[160,768]{1,0:T(8,128)(2,1)S(1)}, bf16[160,768]{1,0:T(8,128)(2,1)S(1)}, u32[]{:S(2)}, u32[]{:S(2)}) collective-permute-start(bf16[160,768]{1,0:T(8,128)(2,1)S(1)} %constant_dynamic-update-slice_fusion.mine), channel_id=1, source_target_pairs={{0,8},{1,9},{2,10},{3,11},{4,12},{5,13},{6,14},{7,15},{8,0},{9,1},... | collective-permute-start | bytes 737288 | tf_op jit(solution)/shard_map/ppermute | solution.py:25
  25.1 2.7 %collective-permute-start.11 = (f32[32,512]{1,0:T(8,128)S(1)}, f32[32,512]{1,0:T(8,128)S(1)}, u32[]{:S(2)}, u32[]{:S(2)}) collective-permute-start(f32[32,512]{1,0:T(8,128)S(1)} %get-tuple-element.37), channel_id=1, source_target_pairs={{0,6},{1,7},{2,4},{3,5},{4,2},{5,3},{6,0},{7,1},{8,14},{9,15},{10,... | collective-permute-start | bytes 196616 | tf_op jit(solution)/shard_map/ppermute | solution.py:25
  28.4 1.2 %collective-permute-start.9 = (f32[32,512]{1,0:T(8,128)S(1)}, f32[32,512]{1,0:T(8,128)S(1)}, u32[]{:S(2)}, u32[]{:S(2)}) collective-permute-start(f32[32,512]{1,0:T(8,128)S(1)} %get-tuple-element.36), channel_id=1, source_target_pairs={{0,4},{1,5},{2,6},{3,7},{4,0},{5,1},{6,2},{7,3},{8,12},{9,13},{10,... | collective-permute-start | bytes 196616 | tf_op jit(solution)/shard_map/ppermute | solution.py:25
  29.6 1.4 %collective-permute-done.7.turned = bf16[160,768]{1,0:T(8,128)(2,1)S(1)} collective-permute-done((bf16[160,768]{1,0:T(8,128)(2,1)S(1)}, bf16[160,768]{1,0:T(8,128)(2,1)S(1)}, u32[]{:S(2)}, u32[]{:S(2)}) %collective-permute-start.7) | collective-permute-done | bytes 245792 | tf_op jit(solution)/shard_map/ppermute | solution.py:25
  31.1 0.7 %collective-permute-done.11 = f32[32,512]{1,0:T(8,128)S(1)} collective-permute-done((f32[32,512]{1,0:T(8,128)S(1)}, f32[32,512]{1,0:T(8,128)S(1)}, u32[]{:S(2)}, u32[]{:S(2)}) %collective-permute-start.11) | collective-permute-done | bytes 65568 | tf_op jit(solution)/shard_map/ppermute | solution.py:25
  32.4 1.1 %collective-permute-done.9 = f32[32,512]{1,0:T(8,128)S(1)} collective-permute-done((f32[32,512]{1,0:T(8,128)S(1)}, f32[32,512]{1,0:T(8,128)S(1)}, u32[]{:S(2)}, u32[]{:S(2)}) %collective-permute-start.9) | collective-permute-done | bytes 65568 | tf_op jit(solution)/shard_map/ppermute | solution.py:25
  33.6 1.2 %collective-permute-start.14 = (bf16[32,512]{1,0:T(8,128)(2,1)S(1)}, bf16[32,512]{1,0:T(8,128)(2,1)S(1)}, u32[]{:S(2)}, u32[]{:S(2)}) collective-permute-start(bf16[32,512]{1,0:T(8,128)(2,1)S(1)} %add_convert_fusion), channel_id=1, source_target_pairs={{0,6},{1,7},{2,4},{3,5},{4,2},{5,3},{6,0},{7,1},{8,14},{9,15},{10,... | collective-permute-start | bytes 98312 | tf_op jit(solution)/shard_map/ppermute | solution.py:25
  35.4 2.6 %collective-permute-start.12 = (bf16[32,512]{1,0:T(8,128)(2,1)S(1)}, bf16[32,512]{1,0:T(8,128)(2,1)S(1)}, u32[]{:S(2)}, u32[]{:S(2)}) collective-permute-start(bf16[32,512]{1,0:T(8,128)(2,1)S(1)} %add_convert_fusion), channel_id=1, source_target_pairs={{0,4},{1,5},{2,6},{3,7},{4,0},{5,1},{6,2},{7,3},{8,12},{9,13},{10,... | collective-permute-start | bytes 98312 | tf_op jit(solution)/shard_map/ppermute | solution.py:25
  38.0 1.3 %collective-permute-done.14 = bf16[32,512]{1,0:T(8,128)(2,1)S(1)} collective-permute-done((bf16[32,512]{1,0:T(8,128)(2,1)S(1)}, bf16[32,512]{1,0:T(8,128)(2,1)S(1)}, u32[]{:S(2)}, u32[]{:S(2)}) %collective-permute-start.14) | collective-permute-done | bytes 32800 | tf_op jit(solution)/shard_map/ppermute | solution.py:25
  39.4 0.9 %collective-permute-done.12 = bf16[32,512]{1,0:T(8,128)(2,1)S(1)} collective-permute-done((bf16[32,512]{1,0:T(8,128)(2,1)S(1)}, bf16[32,512]{1,0:T(8,128)(2,1)S(1)}, u32[]{:S(2)}, u32[]{:S(2)}) %collective-permute-start.12) | collective-permute-done | bytes 32800 | tf_op jit(solution)/shard_map/ppermute | solution.py:25
  40.2 1.4 %collective-permute-start.15 = (bf16[128,512]{1,0:T(8,128)(2,1)S(1)}, bf16[128,512]{1,0:T(8,128)(2,1)S(1)}, u32[]{:S(2)}, u32[]{:S(2)}) collective-permute-start(bf16[128,512]{1,0:T(8,128)(2,1)S(1)} %pad_maximum_fusion.refs_0_), channel_id=1, source_target_pairs={{0,16},{1,9},{2,18},{3,11},{4,20},{5,13},{6,22},{7,15},{8,24},{9,1... | collective-permute-start | bytes 393224 | tf_op jit(solution)/shard_map/ppermute | solution.py:25
  41.6 0.7 %collective-permute-start.16 = (bf16[128,512]{1,0:T(8,128)(2,1)S(1)}, bf16[128,512]{1,0:T(8,128)(2,1)S(1)}, u32[]{:S(2)}, u32[]{:S(2)}) collective-permute-start(bf16[128,512]{1,0:T(8,128)(2,1)S(1)} %pad_maximum_fusion.refs_0_), channel_id=1, source_target_pairs={{0,8},{1,17},{2,10},{3,19},{4,12},{5,21},{6,14},{7,23},{8,0},{9,25... | collective-permute-start | bytes 393224 | tf_op jit(solution)/shard_map/ppermute | solution.py:25
  42.4 1.4 %collective-permute-start.17 = (bf16[128,512]{1,0:T(8,128)(2,1)S(1)}, bf16[128,512]{1,0:T(8,128)(2,1)S(1)}, u32[]{:S(2)}, u32[]{:S(2)}) collective-permute-start(bf16[128,512]{1,0:T(8,128)(2,1)S(1)} %pad_maximum_fusion.refs_0_), channel_id=1, source_target_pairs={{0,24},{1,25},{2,26},{3,27},{4,28},{5,29},{6,30},{7,31},{8,16},{9,... | collective-permute-start | bytes 393224 | tf_op jit(solution)/shard_map/ppermute | solution.py:25
  43.8 1.9 %whole_stats.1.damped = f32[2,512,512]{2,1,0:T(8,128)S(1)} custom-call(s32[7]{0:T(128)S(1)} %stack.31.place, bf16[320,512]{1,0:T(8,128)(2,1)S(1)} %get-tuple-element.22.whole, bf16[160,1280]{1,0:T(8,128)(2,1)S(1)} %collective-permute-done.8.swapped, bf16[160,768]{1,0:T(8,128)(2,1)S(1)} %constant_dynamic-update-slice_fusion.mine, ...), custom_call_target="tpu_custom_call" | custom-call | flops 2097152 | bytes 3145728 | tf_op jit(solution)/shard_map/whole_stats/pallas_call | solution.py:367
  45.8 0.8 %collective-permute-done.16.refs_2_ = bf16[128,512]{1,0:T(8,128)(2,1)S(1)} collective-permute-done((bf16[128,512]{1,0:T(8,128)(2,1)S(1)}, bf16[128,512]{1,0:T(8,128)(2,1)S(1)}, u32[]{:S(2)}, u32[]{:S(2)}) %collective-permute-start.16) | collective-permute-done | bytes 131104 | tf_op jit(solution)/shard_map/ppermute | solution.py:25
  46.6 1.6 %collective-permute-done.17.refs_3_ = bf16[128,512]{1,0:T(8,128)(2,1)S(1)} collective-permute-done((bf16[128,512]{1,0:T(8,128)(2,1)S(1)}, bf16[128,512]{1,0:T(8,128)(2,1)S(1)}, u32[]{:S(2)}, u32[]{:S(2)}) %collective-permute-start.17) | collective-permute-done | bytes 131104 | tf_op jit(solution)/shard_map/ppermute | solution.py:25
  48.2 4.7 %precondition.1 = (f32[4,64,512]{2,1,0:T(8,128)}, f32[64,512]{1,0:T(8,128)S(1)}, f32[3,64,512]{2,1,0:T(8,128)S(1)}) custom-call(s32[7]{0:T(128)S(1)} %stack.31.place, f32[2,512,512]{2,1,0:T(8,128)S(1)} %whole_stats.1.damped, f32[4,64,512]{2,1,0:T(8,128)S(1)} %copy-done.1, bf16[128,512]{1,0:T(8,128)(2,1)S(1)} %pad_maximum_fusion.refs_0_, ...), custom_call_target="tpu_custom_call" | custom-call | flops 2684354560 | bytes 4194304 | tf_op jit(solution)/shard_map/precondition/pallas_call | solution.py:410
  53.0 1.7 %collective-permute-done.18.sent = f32[3,64,512]{2,1,0:T(8,128)S(1)} collective-permute-done((f32[3,64,512]{2,1,0:T(8,128)S(1)}, f32[3,64,512]{2,1,0:T(8,128)S(1)}, u32[]{:S(2)}, u32[]{:S(2)}) %collective-permute-start.18) | collective-permute-done | bytes 393248 | tf_op jit(solution)/shard_map/ppermute | solution.py:25
  54.8 1.4 %finish.1 = (f32[4,64,512]{2,1,0:T(8,128)}, f32[2,64,512]{2,1,0:T(8,128)}) custom-call(s32[7]{0:T(128)S(1)} %stack.31.place, f32[4,64,512]{2,1,0:T(8,128)} %get-tuple-element.31.fresh, f32[4,64,512]{2,1,0:T(8,128)S(1)} %copy-done.1, f32[64,512]{1,0:T(8,128)S(1)} %get-tuple-element.32.own, ...), custom_call_target="tpu_custom_call", output_to_operand_aliasing={{0}: (1, {})} | custom-call | flops 131072 | bytes 1048576 | tf_op jit(solution)/shard_map/finish/pallas_call | solution.py:437
  (33 shorter events, 4.0 us)
Async XLA Ops:
  0.8 1.2 %copy-start = (bf16[512,1024]{1,0:T(8,128)(2,1)S(1)}, bf16[512,1024]{1,0:T(8,128)(2,1)}, u32[]{:S(2)}) copy-start(bf16[512,1024]{1,0:T(8,128)(2,1)} %grads.3) | copy-start | bytes 3145732
  2.0 1.0 %copy-start.2 = (bf16[512,512]{1,0:T(8,128)(2,1)S(1)}, bf16[512,512]{1,0:T(8,128)(2,1)}, u32[]{:S(2)}) copy-start(bf16[512,512]{1,0:T(8,128)(2,1)} %acts.3) | copy-start | bytes 1572868
  3.0 1.5 %copy-start.1 = (f32[4,64,512]{2,1,0:T(8,128)S(1)}, f32[4,64,512]{2,1,0:T(8,128)}, u32[]{:S(2)}) copy-start(f32[4,64,512]{2,1,0:T(8,128)} %stats.5) | copy-start | bytes 1572868
  4.0 2.8 %collective-permute-start = (f32[512,512]{1,0:T(8,128)S(1)}, f32[512,512]{1,0:T(8,128)S(1)}, u32[]{:S(2)}, u32[]{:S(2)}) collective-permute-start(f32[512,512]{1,0:T(8,128)S(1)} %gradient_term.3), channel_id=1, source_target_pairs={{0,1},{1,0},{2,3},{3,2},{4,5},{5,4},{6,7},{7,6},{8,9},{9,8},{10,11... | collective-permute-start | bytes 3145736 | tf_op jit(solution)/shard_map/ppermute | solution.py:25
  7.1 8.7 %collective-permute-start.2 = (f32[128,512]{1,0:T(8,128)S(1)}, f32[128,512]{1,0:T(8,128)S(1)}, u32[]{:S(2)}, u32[]{:S(2)}) collective-permute-start(f32[128,512]{1,0:T(8,128)S(1)} %get-tuple-element.35), channel_id=1, source_target_pairs={{0,8},{1,17},{2,10},{3,19},{4,12},{5,21},{6,14},{7,23},{8,0},{9,25... | collective-permute-start | bytes 786440 | tf_op jit(solution)/shard_map/ppermute | solution.py:25
  10.0 5.8 %collective-permute-start.3 = (bf16[160,128]{1,0:T(8,128)(2,1)S(1)}, bf16[160,128]{1,0:T(8,128)(2,1)S(1)}, u32[]{:S(2)}, u32[]{:S(2)}) collective-permute-start(bf16[160,128]{1,0:T(8,128)(2,1)S(1)} %get-tuple-element.23), channel_id=1, source_target_pairs={{0,6},{1,7},{2,4},{3,5},{4,2},{5,3},{6,0},{7,1},{8,14},{9,15},{10,... | collective-permute-start | bytes 122888 | tf_op jit(solution)/shard_map/ppermute | solution.py:25
  13.6 8.8 %collective-permute-start.1 = (f32[128,512]{1,0:T(8,128)S(1)}, f32[128,512]{1,0:T(8,128)S(1)}, u32[]{:S(2)}, u32[]{:S(2)}) collective-permute-start(f32[128,512]{1,0:T(8,128)S(1)} %get-tuple-element.34), channel_id=1, source_target_pairs={{0,8},{1,17},{2,10},{3,19},{4,12},{5,21},{6,14},{7,23},{8,0},{9,25... | collective-permute-start | bytes 786440 | tf_op jit(solution)/shard_map/ppermute | solution.py:25
  15.9 6.6 %collective-permute-start.4 = (f32[128,512]{1,0:T(8,128)S(1)}, f32[128,512]{1,0:T(8,128)S(1)}, u32[]{:S(2)}, u32[]{:S(2)}) collective-permute-start(f32[128,512]{1,0:T(8,128)S(1)} %slice_add_fusion), channel_id=1, source_target_pairs={{0,16},{1,9},{2,18},{3,11},{4,20},{5,13},{6,22},{7,15},{8,24},{9,1... | collective-permute-start | bytes 786440 | tf_op jit(solution)/shard_map/ppermute | solution.py:25
  17.5 6.8 %collective-permute-start.5 = (bf16[160,384]{1,0:T(8,128)(2,1)S(1)}, bf16[160,384]{1,0:T(8,128)(2,1)S(1)}, u32[]{:S(2)}, u32[]{:S(2)}) collective-permute-start(bf16[160,384]{1,0:T(8,128)(2,1)S(1)} %get-tuple-element.25), channel_id=1, source_target_pairs={{0,2},{1,3},{2,0},{3,1},{4,6},{5,7},{6,4},{7,5},{8,10},{9,11},{10,... | collective-permute-start | bytes 368648 | tf_op jit(solution)/shard_map/ppermute | solution.py:25
  18.1 6.1 %collective-permute-start.6 = (bf16[160,256]{1,0:T(8,128)(2,1)S(1)}, bf16[160,256]{1,0:T(8,128)(2,1)S(1)}, u32[]{:S(2)}, u32[]{:S(2)}) collective-permute-start(bf16[160,256]{1,0:T(8,128)(2,1)S(1)} %get-tuple-element.26), channel_id=1, source_target_pairs={{0,4},{1,5},{2,6},{3,7},{4,0},{5,1},{6,2},{7,3},{8,12},{9,13},{10,... | collective-permute-start | bytes 245768 | tf_op jit(solution)/shard_map/ppermute | solution.py:25
  24.3 6.7 %collective-permute-start.7 = (bf16[160,768]{1,0:T(8,128)(2,1)S(1)}, bf16[160,768]{1,0:T(8,128)(2,1)S(1)}, u32[]{:S(2)}, u32[]{:S(2)}) collective-permute-start(bf16[160,768]{1,0:T(8,128)(2,1)S(1)} %constant_dynamic-update-slice_fusion.mine), channel_id=1, source_target_pairs={{0,8},{1,9},{2,10},{3,11},{4,12},{5,13},{6,14},{7,15},{8,0},{9,1},... | collective-permute-start | bytes 737288 | tf_op jit(solution)/shard_map/ppermute | solution.py:25
  25.1 6.7 %collective-permute-start.11 = (f32[32,512]{1,0:T(8,128)S(1)}, f32[32,512]{1,0:T(8,128)S(1)}, u32[]{:S(2)}, u32[]{:S(2)}) collective-permute-start(f32[32,512]{1,0:T(8,128)S(1)} %get-tuple-element.37), channel_id=1, source_target_pairs={{0,6},{1,7},{2,4},{3,5},{4,2},{5,3},{6,0},{7,1},{8,14},{9,15},{10,... | collective-permute-start | bytes 196616 | tf_op jit(solution)/shard_map/ppermute | solution.py:25
  27.9 4.6 %collective-permute-start.10 = (f32[32,512]{1,0:T(8,128)S(1)}, f32[32,512]{1,0:T(8,128)S(1)}, u32[]{:S(2)}, u32[]{:S(2)}) collective-permute-start(f32[32,512]{1,0:T(8,128)S(1)} %get-tuple-element.38), channel_id=1, source_target_pairs={{0,2},{1,3},{2,0},{3,1},{4,6},{5,7},{6,4},{7,5},{8,10},{9,11},{10,... | collective-permute-start | bytes 196616 | tf_op jit(solution)/shard_map/ppermute | solution.py:25
  28.4 5.2 %collective-permute-start.9 = (f32[32,512]{1,0:T(8,128)S(1)}, f32[32,512]{1,0:T(8,128)S(1)}, u32[]{:S(2)}, u32[]{:S(2)}) collective-permute-start(f32[32,512]{1,0:T(8,128)S(1)} %get-tuple-element.36), channel_id=1, source_target_pairs={{0,4},{1,5},{2,6},{3,7},{4,0},{5,1},{6,2},{7,3},{8,12},{9,13},{10,... | collective-permute-start | bytes 196616 | tf_op jit(solution)/shard_map/ppermute | solution.py:25
  31.0 12.8 %collective-permute-start.8 = (bf16[160,1280]{1,0:T(8,128)(2,1)S(1)}, bf16[160,1280]{1,0:T(8,128)(2,1)S(1)}, u32[]{:S(2)}, u32[]{:S(2)}) collective-permute-start(bf16[160,1280]{1,0:T(8,128)(2,1)S(1)} %maximum_maximum_fusion), channel_id=1, source_target_pairs={{0,1},{1,0},{2,3},{3,2},{4,5},{5,4},{6,7},{7,6},{8,9},{9,8},{10,11... | collective-permute-start | bytes 1228808 | tf_op jit(solution)/shard_map/ppermute | solution.py:25
  33.6 5.8 %collective-permute-start.14 = (bf16[32,512]{1,0:T(8,128)(2,1)S(1)}, bf16[32,512]{1,0:T(8,128)(2,1)S(1)}, u32[]{:S(2)}, u32[]{:S(2)}) collective-permute-start(bf16[32,512]{1,0:T(8,128)(2,1)S(1)} %add_convert_fusion), channel_id=1, source_target_pairs={{0,6},{1,7},{2,4},{3,5},{4,2},{5,3},{6,0},{7,1},{8,14},{9,15},{10,... | collective-permute-start | bytes 98312 | tf_op jit(solution)/shard_map/ppermute | solution.py:25
  34.8 4.5 %collective-permute-start.13 = (bf16[32,512]{1,0:T(8,128)(2,1)S(1)}, bf16[32,512]{1,0:T(8,128)(2,1)S(1)}, u32[]{:S(2)}, u32[]{:S(2)}) collective-permute-start(bf16[32,512]{1,0:T(8,128)(2,1)S(1)} %add_convert_fusion), channel_id=1, source_target_pairs={{0,2},{1,3},{2,0},{3,1},{4,6},{5,7},{6,4},{7,5},{8,10},{9,11},{10,... | collective-permute-start | bytes 98312 | tf_op jit(solution)/shard_map/ppermute | solution.py:25
  35.4 4.8 %collective-permute-start.12 = (bf16[32,512]{1,0:T(8,128)(2,1)S(1)}, bf16[32,512]{1,0:T(8,128)(2,1)S(1)}, u32[]{:S(2)}, u32[]{:S(2)}) collective-permute-start(bf16[32,512]{1,0:T(8,128)(2,1)S(1)} %add_convert_fusion), channel_id=1, source_target_pairs={{0,4},{1,5},{2,6},{3,7},{4,0},{5,1},{6,2},{7,3},{8,12},{9,13},{10,... | collective-permute-start | bytes 98312 | tf_op jit(solution)/shard_map/ppermute | solution.py:25
  40.2 5.5 %collective-permute-start.15 = (bf16[128,512]{1,0:T(8,128)(2,1)S(1)}, bf16[128,512]{1,0:T(8,128)(2,1)S(1)}, u32[]{:S(2)}, u32[]{:S(2)}) collective-permute-start(bf16[128,512]{1,0:T(8,128)(2,1)S(1)} %pad_maximum_fusion.refs_0_), channel_id=1, source_target_pairs={{0,16},{1,9},{2,18},{3,11},{4,20},{5,13},{6,22},{7,15},{8,24},{9,1... | collective-permute-start | bytes 393224 | tf_op jit(solution)/shard_map/ppermute | solution.py:25
  41.6 5.0 %collective-permute-start.16 = (bf16[128,512]{1,0:T(8,128)(2,1)S(1)}, bf16[128,512]{1,0:T(8,128)(2,1)S(1)}, u32[]{:S(2)}, u32[]{:S(2)}) collective-permute-start(bf16[128,512]{1,0:T(8,128)(2,1)S(1)} %pad_maximum_fusion.refs_0_), channel_id=1, source_target_pairs={{0,8},{1,17},{2,10},{3,19},{4,12},{5,21},{6,14},{7,23},{8,0},{9,25... | collective-permute-start | bytes 393224 | tf_op jit(solution)/shard_map/ppermute | solution.py:25
  42.4 5.9 %collective-permute-start.17 = (bf16[128,512]{1,0:T(8,128)(2,1)S(1)}, bf16[128,512]{1,0:T(8,128)(2,1)S(1)}, u32[]{:S(2)}, u32[]{:S(2)}) collective-permute-start(bf16[128,512]{1,0:T(8,128)(2,1)S(1)} %pad_maximum_fusion.refs_0_), channel_id=1, source_target_pairs={{0,24},{1,25},{2,26},{3,27},{4,28},{5,29},{6,30},{7,31},{8,16},{9,... | collective-permute-start | bytes 393224 | tf_op jit(solution)/shard_map/ppermute | solution.py:25
  53.0 1.8 %collective-permute-start.18 = (f32[3,64,512]{2,1,0:T(8,128)S(1)}, f32[3,64,512]{2,1,0:T(8,128)S(1)}, u32[]{:S(2)}, u32[]{:S(2)}) collective-permute-start(f32[3,64,512]{2,1,0:T(8,128)S(1)} %get-tuple-element.33), channel_id=1, source_target_pairs={{0,1},{1,0},{2,3},{3,2},{4,5},{5,4},{6,7},{7,6},{8,9},{9,8},{10,11... | collective-permute-start | bytes 1179656 | tf_op jit(solution)/shard_map/ppermute | solution.py:25

commit v5 on v4

--- a/solution.py
+++ b/solution.py
@@ -13,6 +13,7 @@
 DAMPING = 0.01
 TILE = 16
 LANES = 128
+CORE, LINE, HERE, BESIDE, OWN, SENT, ASKED = range(7)
 
 
 def swap(array, masks):
@@ -50,17 +51,17 @@
     return phases, rows
 
 
-def position(phases, core, rep, grp):
+def position(phases, tile, rep, grp):
     here = jnp.int32(0)
     for kind, bits in phases:
         if kind != "add":
             for masks in bits:
                 flags = [jnp.where((rep & over) | (grp & along), 1, 0) for over, along in masks]
-                here = here * 2 + jnp.where(core == 0, flags[0], flags[1])
+                here = here * 2 + jnp.where(tile == 0, flags[0], flags[1])
     return here
 
 
-def reduce_phase(total, kind, bits, early=()):
+def reduce_phase(total, kind, bits, after_all):
     if kind == "add":
         return total + swap(total, bits[0])
     if kind == "halve":
@@ -70,19 +71,21 @@
     if kind == "relay":
         last = swap(last, bits[0])
         first = swap(first, bits[0])
-        last = lax.optimization_barrier((last, *early))[0]
-        second = swap(second + last, bits[1])
+        second = second + last
+        after_all.append(second)
+        second = swap(second, bits[1])
         return keep + first + second
     second, first, last = swap(second, bits[1]), swap(first, bits[0]), swap(last, both(*bits))
-    return keep + second + first + last
+    return keep + last + first + second
 
 
 def gather_phase(whole, kind, bits):
     if kind == "add":
-        return [whole]
+        return {0: whole}
     if kind == "halve":
-        return [whole, swap(whole, bits[0])]
-    return [whole, swap(whole, bits[1]), swap(whole, bits[0]), swap(whole, both(*bits))]
+        return {0: whole, 1: swap(whole, bits[0])}
+    last, first, second = swap(whole, both(*bits)), swap(whole, bits[0]), swap(whole, bits[1])
+    return {0: whole, 2: first, 1: second, 3: last}
 
 
 def vmem(count):
@@ -100,10 +103,10 @@
 
 def term_kernel(place, grads, acts, out, *, other, rows):
     order = acts.shape[1]
-    columns = pl.ds(pl.multiple_of((place[0] ^ other) * order, order), order)
+    columns = pl.ds(pl.multiple_of((place[CORE] ^ other) * order, order), order)
     term = dot(grads[:, columns], acts[...], (0, 0))
     for block in range(order // rows):
-        there = pl.ds(pl.multiple_of((block ^ place[6 if other else 1]) * rows, rows), rows)
+        there = pl.ds(pl.multiple_of((block ^ place[BESIDE if other else HERE]) * rows, rows), rows)
         out[there, :] = term[block * rows : (block + 1) * rows]
 
 
@@ -135,11 +138,11 @@
     rows, order = stats.shape[1:]
     width = order // lines
     height = rows + TILE
-    diagonal = on_diagonal(rows, order, place[3])
+    diagonal = on_diagonal(rows, order, place[OWN])
     row = lax.broadcasted_iota(jnp.int32, (TILE, order), 0)
     for other in range(2):
         for side in range(2):
-            values = stats[(place[5] ^ side) * tiles + (place[0] ^ other)]
+            values = stats[(place[ASKED] ^ side) * tiles + (place[CORE] ^ other)]
             high = values.astype(BF16)
             low = (2 * other + side) * height
             whole[low : low + rows, :] = high
@@ -150,55 +153,54 @@
             whole[low + rows : low + height, :] = tail.astype(BF16)
     for digit, out in enumerate(outs, 1):
         for index, column in enumerate(columns_for(digit, lines)):
-            start = pl.multiple_of((place[2] ^ column) * width, width)
+            start = pl.multiple_of((place[LINE] ^ column) * width, width)
             for other in range(2):
                 low = 2 * other * height
                 values = whole[low : low + height, pl.ds(start, width)]
                 out[other * height : (other + 1) * height, index * width : (index + 1) * width] = values
 
 
-def mirror_kernel(place, whole, swapped, mine, turned, out, *, rows, lines):
+def mirror_kernel(place, whole, received, mine, turned, out, *, rows, lines):
     order = out.shape[2]
     width = order // lines
     height = rows + TILE
+    wide = mine.shape[1]
     diagonal = on_diagonal(width, width, 0)
 
     def at(digit):
-        return pl.ds(pl.multiple_of((place[2] ^ digit) * width, width), width)
+        return pl.ds(pl.multiple_of((place[LINE] ^ digit) * width, width), width)
 
     def rows_of(digit, core):
-        start = ((place[2] ^ digit) * 2 + (place[0] ^ core)) * rows
+        start = ((place[LINE] ^ digit) * 2 + (place[CORE] ^ core)) * rows
         return pl.ds(pl.multiple_of(start, rows), rows)
 
     for index, part in enumerate((mine, turned)):
-        side = place[5] ^ index
-        low = slice(index * height, index * height + rows)
-        tail = slice(index * height + rows, (index + 1) * height)
+        side = place[ASKED] ^ index
+        low, first = index * height, wide + index * order
 
         def damp(digit, tails):
             tails = [values.astype(F32) for values in tails]
             vector = sum((values[:1] + values[1:2] for values in tails), jnp.full((1, width), DAMPING, F32))
             out[side, at(digit), at(digit)] += jnp.where(diagonal, vector, 0.0)
 
-        out[side, rows_of(0, 0), :] = whole[low, :].astype(F32)
-        out[side, rows_of(0, 1), :] = swapped[low, :order].astype(F32)
+        out[side, rows_of(0, 0), :] = whole[low : low + rows, :].astype(F32)
+        out[side, rows_of(0, 1), :] = received[:rows, first : first + order].astype(F32)
         for digit in range(1, lines):
             out[side, at(digit), at(0)] = out[side, at(0), at(digit)].T
-        damp(0, [whole[tail, at(0)], swapped[tail, at(0)]])
+        lanes = pl.ds(pl.multiple_of(first + place[LINE] * width, width), width)
+        damp(0, [whole[low + rows : low + height, at(0)], received[rows:height, lanes]])
         start = 0
         for digit in range(1, lines):
-            first = slice(start, start + width)
+            tails = [part[core * height + rows : (core + 1) * height, start : start + width] for core in range(2)]
             for column in columns_for(digit, lines):
                 other = digit ^ column
-                lanes = slice(start, start + width)
-                out[side, rows_of(digit, 0), at(other)] = part[:rows, lanes].astype(F32)
-                lanes = slice(order + start, order + start + width)
-                out[side, rows_of(digit, 1), at(other)] = swapped[low, lanes].astype(F32)
+                for core in range(2):
+                    values = part[core * height : core * height + rows, start : start + width]
+                    out[side, rows_of(digit, core), at(other)] = values.astype(F32)
                 if column:
                     out[side, at(other), at(digit)] = out[side, at(digit), at(other)].T
                 start += width
-            away = slice(order + first.start, order + first.stop)
-            damp(digit, [part[rows:height, first], swapped[tail, away]])
+            damp(digit, tails)
 
 
 def collect_kernel(place, *refs, rows):
@@ -206,36 +208,35 @@
     order = out.shape[2]
     height = rows + TILE
     for index in range(2):
-        side = place[5] ^ index
+        side = place[ASKED] ^ index
         vector = jnp.full((1, order), DAMPING, F32)
         for part in parts:
             tail = part[index * height + rows : (index + 1) * height, :].astype(F32)
             vector += tail[:1] + tail[1:2]
         for number, part in enumerate(parts):
-            start = ((place[2] ^ number // 2) * 2 + (place[0] ^ number % 2)) * rows
+            start = ((place[LINE] ^ number // 2) * 2 + (place[CORE] ^ number % 2)) * rows
             start = pl.multiple_of(start, rows)
             values = part[index * height : index * height + rows, :].astype(F32)
             out[side, pl.ds(start, rows), :] = values + jnp.where(on_diagonal(rows, order, start), vector, 0.0)
 
 
-def step_kernel(place, damped, stats, *refs, pieces, rows, band):
-    parts = refs[:pieces]
-    fresh, own, sent, grad, gram, scaled, power, factors, offs, seconds, left_root, right_rows, added, sems = refs[pieces:]
+def step_kernel(place, damped, stats, *refs, numbers, rows, band):
+    parts = refs[: len(numbers)]
+    fresh, own, sent, grad, gram, scaled, power, factors, offs, seconds, left_root, right_rows, added, sems = refs[len(numbers) :]
     tiles = stats.shape[0] // 2
     order = grad.shape[0]
-    for index, part in enumerate(parts):
-        for low in range(0, part.shape[0], rows):
-            block = (index * part.shape[0] + low) // rows
-            start = pl.multiple_of((block ^ place[1]) * rows, rows)
-            grad[pl.ds(start, rows), :] = part[low : low + rows, :]
+    for part, blocks in zip(parts, numbers):
+        for index, block in enumerate(blocks):
+            start = pl.multiple_of((block ^ place[HERE]) * rows, rows)
+            grad[pl.ds(start, rows), :] = part[index * rows : (index + 1) * rows, :]
     copies = []
     for side in range(2):
         gram[side] = dot(grad[...], grad[...], (side, side))
-        chain = side * tiles + place[0]
-        added[side] = stats[chain] + gram[side, pl.ds(pl.multiple_of(place[3], band), band), :]
+        chain = side * tiles + place[CORE]
+        added[side] = stats[chain] + gram[side, pl.ds(pl.multiple_of(place[OWN], band), band), :]
         copies.append(pltpu.make_async_copy(added.at[side], fresh.at[chain], sems.at[side]))
         copies[side].start()
-        sent[side] = gram[side, pl.ds(pl.multiple_of(place[4], band), band), :]
+        sent[side] = gram[side, pl.ds(pl.multiple_of(place[SENT], band), band), :]
     step = min(order, LANES)
     strips = [slice(low, low + step) for low in range(0, order, step)]
     eye = on_diagonal(step, step, 0)
@@ -303,8 +304,8 @@
             offs[side, strip, strip] = (block * 0.25).astype(BF16)
     quarters = [jnp.sqrt(jnp.sqrt(scale)) for scale in scales]
     left_root[...] = (dot(factors[0], offs[0]) * quarters[0]).astype(BF16)
-    right_rows[:band] = factors[1, pl.ds(pl.multiple_of(place[3], band), band), :]
-    right_rows[band:] = factors[1, pl.ds(pl.multiple_of(place[4], band), band), :]
+    right_rows[:band] = factors[1, pl.ds(pl.multiple_of(place[OWN], band), band), :]
+    right_rows[band:] = factors[1, pl.ds(pl.multiple_of(place[SENT], band), band), :]
     right_root = (dot(right_rows[...], offs[1]) * quarters[1]).astype(BF16)
     inner = dot(right_root, grad[...])
     high = inner.astype(BF16)
@@ -318,9 +319,9 @@
 
 def finish_kernel(place, fresh, stats, own, sent, out, update, added, sems):
     tiles = update.shape[0]
-    other = 1 - place[0]
+    other = 1 - place[CORE]
     copies = [
-        pltpu.make_async_copy(own, update.at[place[0]], sems.at[0]),
+        pltpu.make_async_copy(own, update.at[place[CORE]], sems.at[0]),
         pltpu.make_async_copy(sent.at[2], update.at[other], sems.at[1]),
     ]
     for side in range(2):
@@ -350,20 +351,45 @@
     )(place, stats_old)
 
 
-def whole_stats(place, whole, stats, lines, order, band):
-    height = band + TILE
+def join_kernel(whole, *refs, half):
+    parts, out = refs[:-1], refs[-1]
+    height = half // 2
+    start = 0
+    for part in parts:
+        out[:, start : start + part.shape[1]] = part[height:, :]
+        start += part.shape[1]
+    for side in range(2):
+        out[:, start : start + whole.shape[1]] = whole[half + side * height : half + (side + 1) * height, :]
+        start += whole.shape[1]
+
+
+def join_stats(whole, stats):
+    half, order = whole.shape[0] // 2, whole.shape[1]
+    wide = 2 * order + sum(part.shape[1] for part in stats)
+    return pl.pallas_call(
+        functools.partial(join_kernel, half=half),
+        out_shape=jax.ShapeDtypeStruct((half // 2, wide), BF16),
+        in_specs=vmem(1 + len(stats)),
+        out_specs=vmem(1)[0],
+        compiler_params=pltpu.CompilerParams(vmem_limit_bytes=8 << 20),
+        cost_estimate=pl.CostEstimate(flops=10**10, bytes_accessed=2 * half * wide, transcendentals=0),
+        name="join_stats",
+    )(whole, *stats)
+
+
+def after(array, *others):
+    return lax.optimization_barrier((array, *others))[0]
+
+
+def whole_stats(place, whole, received, stats, lines, order, band):
+    half = 2 * (band + TILE)
     if order // lines % LANES == 0:
-        mine = jnp.concatenate(stats, axis=1)
-        turned = swap(mine, ((1, 0), (1, 0)))
-        away = jnp.concatenate([mine[height:], turned[height:]], axis=0)
-        swapped = swap(jnp.concatenate([whole[2 * height :], away], axis=1), CORES)
         kernel = functools.partial(mirror_kernel, rows=band, lines=lines)
-        operands = [whole, swapped, mine, turned]
+        operands = [whole, received, *stats]
     else:
-        swapped = swap(jnp.concatenate([part[2 * height :] for part in (whole, *stats)], axis=0), CORES)
         kernel, operands = functools.partial(collect_kernel, rows=band), []
         for index, part in enumerate((whole, *stats)):
-            operands += [part[: 2 * height], swapped[index * 2 * height : (index + 1) * 2 * height]]
+            operands += [part[:half], received[index * half : (index + 1) * half]]
     return pl.pallas_call(
         kernel,
         out_shape=jax.ShapeDtypeStruct((2, order, order), F32),
@@ -385,30 +411,50 @@
 
     phases, rows = plan(reps, lines, order)
     here, beside = (position(phases, core ^ other, rep, grp) for other in (0, 1))
-    place = jnp.stack([core, here, line, grp * band, (grp ^ 1) * band, rep & 1, beside]).astype(jnp.int32)
+    place = jnp.stack([core, line, here, beside, grp * band, (grp ^ 1) * band, rep & 1]).astype(jnp.int32)
 
     sent = swap(gradient_term(place, out_grads, activations, 1, rows), CORES)
     whole, *shares = stage_stats(place, stats_old, tiles, lines)
     place, *shares = lax.optimization_barrier((place, *shares))
     stats = [swap(share, ((0, 2 * step),) * 2) for step, share in enumerate(shares or [whole] * (lines - 1), 1)]
     total = gradient_term(place, out_grads, activations, 0, rows) + sent
+    mirrored = order // lines % LANES == 0
+    relayed = []
     for index, (kind, bits) in enumerate(phases):
         if index == (reps > 1):
-            total, *stats = lax.optimization_barrier((total, *stats))
-        total = reduce_phase(total, kind, bits, [] if index else [stats[-1]])
-    damped = whole_stats(place, whole, stats, lines, order, band)
-
-    pieces = [total.astype(BF16)]
-    for kind, bits in reversed(phases):
+            if mirrored:
+                stats = [after(part, *relayed) for part in stats]
+                others = join_stats(whole, stats)
+                received = swap(others, CORES)
+                wide = sum(part.shape[1] for part in stats)
+                own = jnp.concatenate([part[: band + TILE] for part in stats], axis=1)
+                mine = jnp.concatenate([own, received[:, :wide]], axis=0)
+                stats = [mine, swap(mine, ((1, 0), (1, 0)))]
+                total, others = lax.optimization_barrier((total, others))
+            else:
+                half = 2 * (band + TILE)
+                received = swap(jnp.concatenate([part[half:] for part in (whole, *stats)], axis=0), CORES)
+                total, *stats = lax.optimization_barrier((total, *stats))
+        total = reduce_phase(total, kind, bits, relayed)
+    pieces, numbers, count = [total.astype(BF16)], [[0]], 1
+    for index, (kind, bits) in enumerate(reversed(phases)):
+        if index == len(phases) - 1:
+            damped = whole_stats(place, whole, received, stats, lines, order, band)
         joined = pieces[0] if len(pieces) == 1 else jnp.concatenate(pieces, axis=0)
-        pieces = gather_phase(joined, kind, bits)
+        if index == len(phases) - 1 and mirrored:
+            joined = after(joined, stats[1])
+        inner = sum(numbers, [])
+        parts = gather_phase(joined, kind, bits)
+        pieces = list(parts.values())
+        numbers = [[digit * count + number for number in inner] for digit in parts]
+        count *= len(parts)
 
     rows_pair = (2, band, order)
     square = (2, order, order)
     anywhere = pl.BlockSpec(memory_space=pl.ANY)
     new_shape = jax.ShapeDtypeStruct(stats_old.shape, F32)
     fresh, own, sent = pl.pallas_call(
-        functools.partial(step_kernel, pieces=len(pieces), rows=rows, band=band),
+        functools.partial(step_kernel, numbers=numbers, rows=rows, band=band),
         out_shape=(
             new_shape,
             jax.ShapeDtypeStruct((band, order), F32),

time: 56.3 us -> 55.2 us (0.980)
  starting transfers between devices: 26.7 us -> 24.2 us
  waiting for transfers between devices: 14.9 us -> 16.3 us
    ppermute x19, starting transfers between devices: 26.7 us -> 24.2 us  [swap(): return lax.ppermute(array, ('rep', 'grp'), pairs)]
    ppermute x19, waiting for transfers between devices: 14.9 us -> 16.3 us  [swap(): return lax.ppermute(array, ('rep', 'grp'), pairs)]
    pallas_call x1 -> x2, Pallas kernels: 4.74 us -> 4.76 us  [the longest x1 4.74 us: on_device(): pl.pallas_call(functools.partial(step_kernel, numbers=numbers, rows=rows,...]
    unnamed x8 -> x6, local copies, waits for them, and re-layouts: 2.29 us -> 2.27 us
  transfers between devices with their start and end apart: 19 -> 19, of which waited for: 13 -> 12; matrix products, arithmetic and copies ran while one was open for 0% -> 0% of each run, Pallas kernels for 7% -> 7%
where the time goes in v5:
time: 55.2 us; the launch traced here: 55 us
  starting transfers between devices  24.2 us (44%)
  waiting for transfers between devices  16.3 us (30%)
  Pallas kernels  10.8 us (20%)
  local copies, waits for them, and re-layouts  2.43 us (4%)
  between operations  0.81 us (1%)
    ppermute x19, starting transfers between devices, swap(): return lax.ppermute(array, ('rep', 'grp'), pairs)  24.2 us
    ppermute x19, waiting for transfers between devices, swap(): return lax.ppermute(array, ('rep', 'grp'), pairs)  16.3 us
    pallas_call x1, Pallas kernels, on_device(): pl.pallas_call(functools.partial(step_kernel, numbers=numbers, rows=rows,...  4.74 us
    unnamed x6, local copies, waits for them, and re-layouts  2.27 us
    pallas_call x2, Pallas kernels, gradient_term(): pl.pallas_call(functools.partial(term_kernel, other=other, rows=rows), ou...  2.04 us
    pallas_call x1, Pallas kernels, whole_stats(): pl.pallas_call(kernel, out_shape=jax.ShapeDtypeStruct((2, order, order),...  1.95 us
    pallas_call x1, Pallas kernels, on_device(): pl.pallas_call(finish_kernel, out_shape=(new_shape, jax.ShapeDtypeStruct(...  1.36 us
  transfers between devices with their start and end apart: 19, of which 12 were waited for; matrix products, arithmetic and copies ran while one was open for 0% of the time, Pallas kernels for 7%

profile of v5, /device:TPU:0, one launch (start us, length us, event | category | flops | bytes accessed | tf_op | source)
XLA Modules:
  0.0 55.0 jit_solution(13353940851200034821)
XLA Ops:
  0.8 1.2 %copy-done = bf16[512,1024]{1,0:T(8,128)(2,1)S(1)} copy-done((bf16[512,1024]{1,0:T(8,128)(2,1)S(1)}, bf16[512,1024]{1,0:T(8,128)(2,1)}, u32[]{:S(2)}) %copy-start) | copy-done | bytes 1048600
  2.0 1.0 %copy-done.2 = bf16[512,512]{1,0:T(8,128)(2,1)S(1)} copy-done((bf16[512,512]{1,0:T(8,128)(2,1)S(1)}, bf16[512,512]{1,0:T(8,128)(2,1)}, u32[]{:S(2)}) %copy-start.2) | copy-done | bytes 524312
  3.0 1.0 %gradient_term.3 = f32[512,512]{1,0:T(8,128)S(1)} custom-call(s32[7]{0:T(128)S(1)} %stack.31.place, bf16[512,1024]{1,0:T(8,128)(2,1)S(1)} %copy-done, bf16[512,512]{1,0:T(8,128)(2,1)S(1)} %copy-done.2), custom_call_target="tpu_custom_call" | custom-call | flops 268435456 | bytes 1048576 | tf_op jit(solution)/shard_map/gradient_term/pallas_call | solution.py:115
  4.0 0.5 collective-permute-start.1
  4.6 0.7 %stage_stats.1 = (bf16[320,512]{1,0:T(8,128)(2,1)S(1)}, bf16[160,384]{1,0:T(8,128)(2,1)S(1)}, bf16[160,256]{1,0:T(8,128)(2,1)S(1)}, bf16[160,128]{1,0:T(8,128)(2,1)S(1)}) custom-call(s32[7]{0:T(128)S(1)} %stack.31.place, f32[4,64,512]{2,1,0:T(8,128)S(1)} %copy-done.1), custom_call_target="tpu_custom_call" | custom-call | flops 655360 | bytes 1048576 | tf_op jit(solution)/shard_map/stage_stats/pallas_call | solution.py:343
  5.3 1.0 %gradient_term.2 = f32[512,512]{1,0:T(8,128)S(1)} custom-call(s32[7]{0:T(128)S(1)} %stack.31.place, bf16[512,1024]{1,0:T(8,128)(2,1)S(1)} %copy-done, bf16[512,512]{1,0:T(8,128)(2,1)S(1)} %copy-done.2), custom_call_target="tpu_custom_call" | custom-call | flops 268435456 | bytes 1048576 | tf_op jit(solution)/shard_map/gradient_term/pallas_call | solution.py:115
  6.3 0.5 collective-permute-done.1
  7.1 2.9 %collective-permute-start.2 = (f32[128,512]{1,0:T(8,128)S(1)}, f32[128,512]{1,0:T(8,128)S(1)}, u32[]{:S(2)}, u32[]{:S(2)}) collective-permute-start(f32[128,512]{1,0:T(8,128)S(1)} %get-tuple-element.35), channel_id=1, source_target_pairs={{0,8},{1,17},{2,10},{3,19},{4,12},{5,21},{6,14},{7,23},{8,0},{9,25... | collective-permute-start | bytes 786440 | tf_op jit(solution)/shard_map/ppermute | solution.py:26
  10.0 3.6 %collective-permute-start.4 = (bf16[160,128]{1,0:T(8,128)(2,1)S(1)}, bf16[160,128]{1,0:T(8,128)(2,1)S(1)}, u32[]{:S(2)}, u32[]{:S(2)}) collective-permute-start(bf16[160,128]{1,0:T(8,128)(2,1)S(1)} %get-tuple-element.27), channel_id=1, source_target_pairs={{0,6},{1,7},{2,4},{3,5},{4,2},{5,3},{6,0},{7,1},{8,14},{9,15},{10,... | collective-permute-start | bytes 122888 | tf_op jit(solution)/shard_map/ppermute | solution.py:26
  13.6 0.8 %collective-permute-start = (bf16[160,384]{1,0:T(8,128)(2,1)S(1)}, bf16[160,384]{1,0:T(8,128)(2,1)S(1)}, u32[]{:S(2)}, u32[]{:S(2)}) collective-permute-start(bf16[160,384]{1,0:T(8,128)(2,1)S(1)} %get-tuple-element.23), channel_id=1, source_target_pairs={{0,2},{1,3},{2,0},{3,1},{4,6},{5,7},{6,4},{7,5},{8,10},{9,11},{10,... | collective-permute-start | bytes 368648 | tf_op jit(solution)/shard_map/ppermute | solution.py:26
  14.8 1.8 %collective-permute-start.8 = (f32[128,512]{1,0:T(8,128)S(1)}, f32[128,512]{1,0:T(8,128)S(1)}, u32[]{:S(2)}, u32[]{:S(2)}) collective-permute-start(f32[128,512]{1,0:T(8,128)S(1)} %slice_add_fusion.1), channel_id=1, source_target_pairs={{0,16},{1,9},{2,18},{3,11},{4,20},{5,13},{6,22},{7,15},{8,24},{9,1... | collective-permute-start | bytes 786440 | tf_op jit(solution)/shard_map/ppermute | solution.py:26
  16.6 2.9 %collective-permute-done.3.refs_1_ = bf16[160,256]{1,0:T(8,128)(2,1)S(1)} collective-permute-done((bf16[160,256]{1,0:T(8,128)(2,1)S(1)}, bf16[160,256]{1,0:T(8,128)(2,1)S(1)}, u32[]{:S(2)}, u32[]{:S(2)}) %collective-permute-start.3) | collective-permute-done | bytes 81952 | tf_op jit(solution)/shard_map/ppermute | solution.py:26
  19.5 0.8 %collective-permute-done.refs_0_ = bf16[160,384]{1,0:T(8,128)(2,1)S(1)} collective-permute-done((bf16[160,384]{1,0:T(8,128)(2,1)S(1)}, bf16[160,384]{1,0:T(8,128)(2,1)S(1)}, u32[]{:S(2)}, u32[]{:S(2)}) %collective-permute-start) | collective-permute-done | bytes 122912 | tf_op jit(solution)/shard_map/ppermute | solution.py:26
  20.4 1.9 %collective-permute-done.7 = f32[128,512]{1,0:T(8,128)S(1)} collective-permute-done((f32[128,512]{1,0:T(8,128)S(1)}, f32[128,512]{1,0:T(8,128)S(1)}, u32[]{:S(2)}, u32[]{:S(2)}) %collective-permute-start.7) | collective-permute-done | bytes 262176 | tf_op jit(solution)/shard_map/ppermute | solution.py:26
  22.4 3.9 %collective-permute-start.9 = (f32[32,512]{1,0:T(8,128)S(1)}, f32[32,512]{1,0:T(8,128)S(1)}, u32[]{:S(2)}, u32[]{:S(2)}) collective-permute-start(f32[32,512]{1,0:T(8,128)S(1)} %get-tuple-element.36), channel_id=1, source_target_pairs={{0,6},{1,7},{2,4},{3,5},{4,2},{5,3},{6,0},{7,1},{8,14},{9,15},{10,... | collective-permute-start | bytes 196616 | tf_op jit(solution)/shard_map/ppermute | solution.py:26
  26.3 0.6 %collective-permute-start.10 = (f32[32,512]{1,0:T(8,128)S(1)}, f32[32,512]{1,0:T(8,128)S(1)}, u32[]{:S(2)}, u32[]{:S(2)}) collective-permute-start(f32[32,512]{1,0:T(8,128)S(1)} %get-tuple-element.38), channel_id=1, source_target_pairs={{0,2},{1,3},{2,0},{3,1},{4,6},{5,7},{6,4},{7,5},{8,10},{9,11},{10,... | collective-permute-start | bytes 196616 | tf_op jit(solution)/shard_map/ppermute | solution.py:26
  26.9 1.6 %collective-permute-start.6 = (bf16[160,768]{1,0:T(8,128)(2,1)S(1)}, bf16[160,768]{1,0:T(8,128)(2,1)S(1)}, u32[]{:S(2)}, u32[]{:S(2)}) collective-permute-start(bf16[160,768]{1,0:T(8,128)(2,1)S(1)} %pad_maximum_fusion.mine), channel_id=1, source_target_pairs={{0,8},{1,9},{2,10},{3,11},{4,12},{5,13},{6,14},{7,15},{8,0},{9,1},... | collective-permute-start | bytes 737288 | tf_op jit(solution)/shard_map/ppermute | solution.py:26
  28.5 0.6 %collective-permute-done.9 = f32[32,512]{1,0:T(8,128)S(1)} collective-permute-done((f32[32,512]{1,0:T(8,128)S(1)}, f32[32,512]{1,0:T(8,128)S(1)}, u32[]{:S(2)}, u32[]{:S(2)}) %collective-permute-start.9) | collective-permute-done | bytes 65568 | tf_op jit(solution)/shard_map/ppermute | solution.py:26
  29.1 2.5 %collective-permute-done.11 = f32[32,512]{1,0:T(8,128)S(1)} collective-permute-done((f32[32,512]{1,0:T(8,128)S(1)}, f32[32,512]{1,0:T(8,128)S(1)}, u32[]{:S(2)}, u32[]{:S(2)}) %collective-permute-start.11) | collective-permute-done | bytes 65568 | tf_op jit(solution)/shard_map/ppermute | solution.py:26
  31.6 2.3 %collective-permute-start.14 = (bf16[32,512]{1,0:T(8,128)(2,1)S(1)}, bf16[32,512]{1,0:T(8,128)(2,1)S(1)}, u32[]{:S(2)}, u32[]{:S(2)}) collective-permute-start(bf16[32,512]{1,0:T(8,128)(2,1)S(1)} %add_convert_fusion), channel_id=1, source_target_pairs={{0,6},{1,7},{2,4},{3,5},{4,2},{5,3},{6,0},{7,1},{8,14},{9,15},{10,... | collective-permute-start | bytes 98312 | tf_op jit(solution)/shard_map/ppermute | solution.py:26
  34.0 2.1 %collective-permute-start.12 = (bf16[32,512]{1,0:T(8,128)(2,1)S(1)}, bf16[32,512]{1,0:T(8,128)(2,1)S(1)}, u32[]{:S(2)}, u32[]{:S(2)}) collective-permute-start(bf16[32,512]{1,0:T(8,128)(2,1)S(1)} %add_convert_fusion), channel_id=1, source_target_pairs={{0,2},{1,3},{2,0},{3,1},{4,6},{5,7},{6,4},{7,5},{8,10},{9,11},{10,... | collective-permute-start | bytes 98312 | tf_op jit(solution)/shard_map/ppermute | solution.py:26
  36.1 1.3 %collective-permute-done.14 = bf16[32,512]{1,0:T(8,128)(2,1)S(1)} collective-permute-done((bf16[32,512]{1,0:T(8,128)(2,1)S(1)}, bf16[32,512]{1,0:T(8,128)(2,1)S(1)}, u32[]{:S(2)}, u32[]{:S(2)}) %collective-permute-start.14) | collective-permute-done | bytes 32800 | tf_op jit(solution)/shard_map/ppermute | solution.py:26
  37.4 1.4 %collective-permute-done.13 = bf16[32,512]{1,0:T(8,128)(2,1)S(1)} collective-permute-done((bf16[32,512]{1,0:T(8,128)(2,1)S(1)}, bf16[32,512]{1,0:T(8,128)(2,1)S(1)}, u32[]{:S(2)}, u32[]{:S(2)}) %collective-permute-start.13) | collective-permute-done | bytes 32800 | tf_op jit(solution)/shard_map/ppermute | solution.py:26
  38.8 2.8 %collective-permute-start.17 = (bf16[128,512]{1,0:T(8,128)(2,1)S(1)}, bf16[128,512]{1,0:T(8,128)(2,1)S(1)}, u32[]{:S(2)}, u32[]{:S(2)}) collective-permute-start(bf16[128,512]{1,0:T(8,128)(2,1)S(1)} %pad_maximum_fusion.1.refs_0_), channel_id=1, source_target_pairs={{0,24},{1,25},{2,26},{3,27},{4,28},{5,29},{6,30},{7,31},{8,16},{9,... | collective-permute-start | bytes 393224 | tf_op jit(solution)/shard_map/ppermute | solution.py:26
  41.6 0.5 collective-permute-start.16
  42.4 1.9 %whole_stats.1.damped = f32[2,512,512]{2,1,0:T(8,128)S(1)} custom-call(s32[7]{0:T(128)S(1)} %stack.31.place, bf16[320,512]{1,0:T(8,128)(2,1)S(1)} %get-tuple-element.22.whole, bf16[80,1792]{1,0:T(8,128)(2,1)S(1)} %collective-permute-done.5.received, bf16[160,768]{1,0:T(8,128)(2,1)S(1)} %pad_maximum_fusion.mine, ...), custom_call_target="tpu_custom_call" | custom-call | flops 2097152 | bytes 3145728 | tf_op jit(solution)/shard_map/whole_stats/pallas_call | solution.py:393
  44.3 0.8 %collective-permute-done.17.refs_3_ = bf16[128,512]{1,0:T(8,128)(2,1)S(1)} collective-permute-done((bf16[128,512]{1,0:T(8,128)(2,1)S(1)}, bf16[128,512]{1,0:T(8,128)(2,1)S(1)}, u32[]{:S(2)}, u32[]{:S(2)}) %collective-permute-start.17) | collective-permute-done | bytes 131104 | tf_op jit(solution)/shard_map/ppermute | solution.py:26
  45.1 1.4 %collective-permute-done.16.refs_2_ = bf16[128,512]{1,0:T(8,128)(2,1)S(1)} collective-permute-done((bf16[128,512]{1,0:T(8,128)(2,1)S(1)}, bf16[128,512]{1,0:T(8,128)(2,1)S(1)}, u32[]{:S(2)}, u32[]{:S(2)}) %collective-permute-start.16) | collective-permute-done | bytes 131104 | tf_op jit(solution)/shard_map/ppermute | solution.py:26
  46.5 0.5 collective-permute-done.15.refs_1_
  47.1 4.7 %precondition.1 = (f32[4,64,512]{2,1,0:T(8,128)}, f32[64,512]{1,0:T(8,128)S(1)}, f32[3,64,512]{2,1,0:T(8,128)S(1)}) custom-call(s32[7]{0:T(128)S(1)} %stack.31.place, f32[2,512,512]{2,1,0:T(8,128)S(1)} %whole_stats.1.damped, f32[4,64,512]{2,1,0:T(8,128)S(1)} %copy-done.1, bf16[128,512]{1,0:T(8,128)(2,1)S(1)} %pad_maximum_fusion.1.refs_0_, ...), custom_call_target="tpu_custom_call" | custom-call | flops 2684354560 | bytes 4194304 | tf_op jit(solution)/shard_map/precondition/pallas_call | solution.py:456
  51.9 1.7 %collective-permute-done.18.sent = f32[3,64,512]{2,1,0:T(8,128)S(1)} collective-permute-done((f32[3,64,512]{2,1,0:T(8,128)S(1)}, f32[3,64,512]{2,1,0:T(8,128)S(1)}, u32[]{:S(2)}, u32[]{:S(2)}) %collective-permute-start.18) | collective-permute-done | bytes 393248 | tf_op jit(solution)/shard_map/ppermute | solution.py:26
  53.6 1.4 %finish.1 = (f32[4,64,512]{2,1,0:T(8,128)}, f32[2,64,512]{2,1,0:T(8,128)}) custom-call(s32[7]{0:T(128)S(1)} %stack.31.place, f32[4,64,512]{2,1,0:T(8,128)} %get-tuple-element.31.fresh, f32[4,64,512]{2,1,0:T(8,128)S(1)} %copy-done.1, f32[64,512]{1,0:T(8,128)S(1)} %get-tuple-element.32.own, ...), custom_call_target="tpu_custom_call", output_to_operand_aliasing={{0}: (1, {})} | custom-call | flops 131072 | bytes 1048576 | tf_op jit(solution)/shard_map/finish/pallas_call | solution.py:483
  (32 shorter events, 1.3 us)
Async XLA Ops:
  0.8 1.2 %copy-start = (bf16[512,1024]{1,0:T(8,128)(2,1)S(1)}, bf16[512,1024]{1,0:T(8,128)(2,1)}, u32[]{:S(2)}) copy-start(bf16[512,1024]{1,0:T(8,128)(2,1)} %grads.3) | copy-start | bytes 3145732
  2.0 1.0 %copy-start.2 = (bf16[512,512]{1,0:T(8,128)(2,1)S(1)}, bf16[512,512]{1,0:T(8,128)(2,1)}, u32[]{:S(2)}) copy-start(bf16[512,512]{1,0:T(8,128)(2,1)} %acts.3) | copy-start | bytes 1572868
  3.0 1.5 %copy-start.1 = (f32[4,64,512]{2,1,0:T(8,128)S(1)}, f32[4,64,512]{2,1,0:T(8,128)}, u32[]{:S(2)}) copy-start(f32[4,64,512]{2,1,0:T(8,128)} %stats.5) | copy-start | bytes 1572868
  4.0 2.8 %collective-permute-start.1 = (f32[512,512]{1,0:T(8,128)S(1)}, f32[512,512]{1,0:T(8,128)S(1)}, u32[]{:S(2)}, u32[]{:S(2)}) collective-permute-start(f32[512,512]{1,0:T(8,128)S(1)} %gradient_term.3), channel_id=1, source_target_pairs={{0,1},{1,0},{2,3},{3,2},{4,5},{5,4},{6,7},{7,6},{8,9},{9,8},{10,11... | collective-permute-start | bytes 3145736 | tf_op jit(solution)/shard_map/ppermute | solution.py:26
  7.1 7.6 %collective-permute-start.2 = (f32[128,512]{1,0:T(8,128)S(1)}, f32[128,512]{1,0:T(8,128)S(1)}, u32[]{:S(2)}, u32[]{:S(2)}) collective-permute-start(f32[128,512]{1,0:T(8,128)S(1)} %get-tuple-element.35), channel_id=1, source_target_pairs={{0,8},{1,17},{2,10},{3,19},{4,12},{5,21},{6,14},{7,23},{8,0},{9,25... | collective-permute-start | bytes 786440 | tf_op jit(solution)/shard_map/ppermute | solution.py:26
  10.0 6.6 %collective-permute-start.4 = (bf16[160,128]{1,0:T(8,128)(2,1)S(1)}, bf16[160,128]{1,0:T(8,128)(2,1)S(1)}, u32[]{:S(2)}, u32[]{:S(2)}) collective-permute-start(bf16[160,128]{1,0:T(8,128)(2,1)S(1)} %get-tuple-element.27), channel_id=1, source_target_pairs={{0,6},{1,7},{2,4},{3,5},{4,2},{5,3},{6,0},{7,1},{8,14},{9,15},{10,... | collective-permute-start | bytes 122888 | tf_op jit(solution)/shard_map/ppermute | solution.py:26
  13.6 5.8 %collective-permute-start.3 = (bf16[160,256]{1,0:T(8,128)(2,1)S(1)}, bf16[160,256]{1,0:T(8,128)(2,1)S(1)}, u32[]{:S(2)}, u32[]{:S(2)}) collective-permute-start(bf16[160,256]{1,0:T(8,128)(2,1)S(1)} %get-tuple-element.25), channel_id=1, source_target_pairs={{0,4},{1,5},{2,6},{3,7},{4,0},{5,1},{6,2},{7,3},{8,12},{9,13},{10,... | collective-permute-start | bytes 245768 | tf_op jit(solution)/shard_map/ppermute | solution.py:26
  13.6 6.6 %collective-permute-start = (bf16[160,384]{1,0:T(8,128)(2,1)S(1)}, bf16[160,384]{1,0:T(8,128)(2,1)S(1)}, u32[]{:S(2)}, u32[]{:S(2)}) collective-permute-start(bf16[160,384]{1,0:T(8,128)(2,1)S(1)} %get-tuple-element.23), channel_id=1, source_target_pairs={{0,2},{1,3},{2,0},{3,1},{4,6},{5,7},{6,4},{7,5},{8,10},{9,11},{10,... | collective-permute-start | bytes 368648 | tf_op jit(solution)/shard_map/ppermute | solution.py:26
  14.4 7.9 %collective-permute-start.7 = (f32[128,512]{1,0:T(8,128)S(1)}, f32[128,512]{1,0:T(8,128)S(1)}, u32[]{:S(2)}, u32[]{:S(2)}) collective-permute-start(f32[128,512]{1,0:T(8,128)S(1)} %get-tuple-element.34), channel_id=1, source_target_pairs={{0,8},{1,17},{2,10},{3,19},{4,12},{5,21},{6,14},{7,23},{8,0},{9,25... | collective-permute-start | bytes 786440 | tf_op jit(solution)/shard_map/ppermute | solution.py:26
  14.8 7.5 %collective-permute-start.8 = (f32[128,512]{1,0:T(8,128)S(1)}, f32[128,512]{1,0:T(8,128)S(1)}, u32[]{:S(2)}, u32[]{:S(2)}) collective-permute-start(f32[128,512]{1,0:T(8,128)S(1)} %slice_add_fusion.1), channel_id=1, source_target_pairs={{0,16},{1,9},{2,18},{3,11},{4,20},{5,13},{6,22},{7,15},{8,24},{9,1... | collective-permute-start | bytes 786440 | tf_op jit(solution)/shard_map/ppermute | solution.py:26
  20.3 6.6 %collective-permute-start.5 = (bf16[80,1792]{1,0:T(8,128)(2,1)S(1)}, bf16[80,1792]{1,0:T(8,128)(2,1)S(1)}, u32[]{:S(2)}, u32[]{:S(2)}) collective-permute-start(bf16[80,1792]{1,0:T(8,128)(2,1)S(1)} %join_stats.1), channel_id=1, source_target_pairs={{0,1},{1,0},{2,3},{3,2},{4,5},{5,4},{6,7},{7,6},{8,9},{9,8},{10,11... | collective-permute-start | bytes 860168 | tf_op jit(solution)/shard_map/ppermute | solution.py:26
  22.4 6.8 %collective-permute-start.9 = (f32[32,512]{1,0:T(8,128)S(1)}, f32[32,512]{1,0:T(8,128)S(1)}, u32[]{:S(2)}, u32[]{:S(2)}) collective-permute-start(f32[32,512]{1,0:T(8,128)S(1)} %get-tuple-element.36), channel_id=1, source_target_pairs={{0,6},{1,7},{2,4},{3,5},{4,2},{5,3},{6,0},{7,1},{8,14},{9,15},{10,... | collective-permute-start | bytes 196616 | tf_op jit(solution)/shard_map/ppermute | solution.py:26
  26.3 5.4 %collective-permute-start.11 = (f32[32,512]{1,0:T(8,128)S(1)}, f32[32,512]{1,0:T(8,128)S(1)}, u32[]{:S(2)}, u32[]{:S(2)}) collective-permute-start(f32[32,512]{1,0:T(8,128)S(1)} %get-tuple-element.37), channel_id=1, source_target_pairs={{0,4},{1,5},{2,6},{3,7},{4,0},{5,1},{6,2},{7,3},{8,12},{9,13},{10,... | collective-permute-start | bytes 196616 | tf_op jit(solution)/shard_map/ppermute | solution.py:26
  26.3 5.4 %collective-permute-start.10 = (f32[32,512]{1,0:T(8,128)S(1)}, f32[32,512]{1,0:T(8,128)S(1)}, u32[]{:S(2)}, u32[]{:S(2)}) collective-permute-start(f32[32,512]{1,0:T(8,128)S(1)} %get-tuple-element.38), channel_id=1, source_target_pairs={{0,2},{1,3},{2,0},{3,1},{4,6},{5,7},{6,4},{7,5},{8,10},{9,11},{10,... | collective-permute-start | bytes 196616 | tf_op jit(solution)/shard_map/ppermute | solution.py:26
  26.9 11.9 %collective-permute-start.6 = (bf16[160,768]{1,0:T(8,128)(2,1)S(1)}, bf16[160,768]{1,0:T(8,128)(2,1)S(1)}, u32[]{:S(2)}, u32[]{:S(2)}) collective-permute-start(bf16[160,768]{1,0:T(8,128)(2,1)S(1)} %pad_maximum_fusion.mine), channel_id=1, source_target_pairs={{0,8},{1,9},{2,10},{3,11},{4,12},{5,13},{6,14},{7,15},{8,0},{9,1},... | collective-permute-start | bytes 737288 | tf_op jit(solution)/shard_map/ppermute | solution.py:26
  31.6 5.8 %collective-permute-start.14 = (bf16[32,512]{1,0:T(8,128)(2,1)S(1)}, bf16[32,512]{1,0:T(8,128)(2,1)S(1)}, u32[]{:S(2)}, u32[]{:S(2)}) collective-permute-start(bf16[32,512]{1,0:T(8,128)(2,1)S(1)} %add_convert_fusion), channel_id=1, source_target_pairs={{0,6},{1,7},{2,4},{3,5},{4,2},{5,3},{6,0},{7,1},{8,14},{9,15},{10,... | collective-permute-start | bytes 98312 | tf_op jit(solution)/shard_map/ppermute | solution.py:26
  34.0 4.8 %collective-permute-start.13 = (bf16[32,512]{1,0:T(8,128)(2,1)S(1)}, bf16[32,512]{1,0:T(8,128)(2,1)S(1)}, u32[]{:S(2)}, u32[]{:S(2)}) collective-permute-start(bf16[32,512]{1,0:T(8,128)(2,1)S(1)} %add_convert_fusion), channel_id=1, source_target_pairs={{0,4},{1,5},{2,6},{3,7},{4,0},{5,1},{6,2},{7,3},{8,12},{9,13},{10,... | collective-permute-start | bytes 98312 | tf_op jit(solution)/shard_map/ppermute | solution.py:26
  34.0 4.8 %collective-permute-start.12 = (bf16[32,512]{1,0:T(8,128)(2,1)S(1)}, bf16[32,512]{1,0:T(8,128)(2,1)S(1)}, u32[]{:S(2)}, u32[]{:S(2)}) collective-permute-start(bf16[32,512]{1,0:T(8,128)(2,1)S(1)} %add_convert_fusion), channel_id=1, source_target_pairs={{0,2},{1,3},{2,0},{3,1},{4,6},{5,7},{6,4},{7,5},{8,10},{9,11},{10,... | collective-permute-start | bytes 98312 | tf_op jit(solution)/shard_map/ppermute | solution.py:26
  38.8 6.3 %collective-permute-start.17 = (bf16[128,512]{1,0:T(8,128)(2,1)S(1)}, bf16[128,512]{1,0:T(8,128)(2,1)S(1)}, u32[]{:S(2)}, u32[]{:S(2)}) collective-permute-start(bf16[128,512]{1,0:T(8,128)(2,1)S(1)} %pad_maximum_fusion.1.refs_0_), channel_id=1, source_target_pairs={{0,24},{1,25},{2,26},{3,27},{4,28},{5,29},{6,30},{7,31},{8,16},{9,... | collective-permute-start | bytes 393224 | tf_op jit(solution)/shard_map/ppermute | solution.py:26
  41.6 5.0 %collective-permute-start.16 = (bf16[128,512]{1,0:T(8,128)(2,1)S(1)}, bf16[128,512]{1,0:T(8,128)(2,1)S(1)}, u32[]{:S(2)}, u32[]{:S(2)}) collective-permute-start(bf16[128,512]{1,0:T(8,128)(2,1)S(1)} %pad_maximum_fusion.1.refs_0_), channel_id=1, source_target_pairs={{0,16},{1,9},{2,18},{3,11},{4,20},{5,13},{6,22},{7,15},{8,24},{9,1... | collective-permute-start | bytes 393224 | tf_op jit(solution)/shard_map/ppermute | solution.py:26
  42.1 5.0 %collective-permute-start.15 = (bf16[128,512]{1,0:T(8,128)(2,1)S(1)}, bf16[128,512]{1,0:T(8,128)(2,1)S(1)}, u32[]{:S(2)}, u32[]{:S(2)}) collective-permute-start(bf16[128,512]{1,0:T(8,128)(2,1)S(1)} %pad_maximum_fusion.1.refs_0_), channel_id=1, source_target_pairs={{0,8},{1,17},{2,10},{3,19},{4,12},{5,21},{6,14},{7,23},{8,0},{9,25... | collective-permute-start | bytes 393224 | tf_op jit(solution)/shard_map/ppermute | solution.py:26
  51.8 1.8 %collective-permute-start.18 = (f32[3,64,512]{2,1,0:T(8,128)S(1)}, f32[3,64,512]{2,1,0:T(8,128)S(1)}, u32[]{:S(2)}, u32[]{:S(2)}) collective-permute-start(f32[3,64,512]{2,1,0:T(8,128)S(1)} %get-tuple-element.33), channel_id=1, source_target_pairs={{0,1},{1,0},{2,3},{3,2},{4,5},{5,4},{6,7},{7,6},{8,9},{9,8},{10,11... | collective-permute-start | bytes 1179656 | tf_op jit(solution)/shard_map/ppermute | solution.py:26

commit v6 on v5

--- a/solution.py
+++ b/solution.py
@@ -222,7 +222,7 @@
 
 def step_kernel(place, damped, stats, *refs, numbers, rows, band):
     parts = refs[: len(numbers)]
-    fresh, own, sent, grad, gram, scaled, power, factors, offs, seconds, left_root, right_rows, added, sems = refs[len(numbers) :]
+    fresh, own, sent, sent_update, grad, gram, scaled, power, factors, offs, seconds, left_root, right_rows, added, sems = refs[len(numbers) :]
     tiles = stats.shape[0] // 2
     order = grad.shape[0]
     for part, blocks in zip(parts, numbers):
@@ -312,17 +312,17 @@
     low = (inner - high.astype(F32)).astype(BF16)
     update = (dot(high, left_root[...]) + dot(low, left_root[...])) * math.sqrt(order)
     own[...] = update[:band]
-    sent[2] = update[band:]
+    sent_update[...] = update[band:]
     for copy in copies:
         copy.wait()
 
 
-def finish_kernel(place, fresh, stats, own, sent, out, update, added, sems):
+def finish_kernel(place, fresh, stats, own, sent, sent_update, out, update, added, sems):
     tiles = update.shape[0]
     other = 1 - place[CORE]
     copies = [
         pltpu.make_async_copy(own, update.at[place[CORE]], sems.at[0]),
-        pltpu.make_async_copy(sent.at[2], update.at[other], sems.at[1]),
+        pltpu.make_async_copy(sent_update, update.at[other], sems.at[1]),
     ]
     for side in range(2):
         chain = side * tiles + other
@@ -453,15 +453,16 @@
     square = (2, order, order)
     anywhere = pl.BlockSpec(memory_space=pl.ANY)
     new_shape = jax.ShapeDtypeStruct(stats_old.shape, F32)
-    fresh, own, sent = pl.pallas_call(
+    fresh, own, sent, sent_update = pl.pallas_call(
         functools.partial(step_kernel, numbers=numbers, rows=rows, band=band),
         out_shape=(
             new_shape,
             jax.ShapeDtypeStruct((band, order), F32),
-            jax.ShapeDtypeStruct((3, band, order), F32),
+            jax.ShapeDtypeStruct(rows_pair, F32),
+            jax.ShapeDtypeStruct((band, order), F32),
         ),
         in_specs=[SMEM] + vmem(2 + len(pieces)),
-        out_specs=(anywhere, *vmem(2)),
+        out_specs=(anywhere, *vmem(3)),
         scratch_shapes=[
             pltpu.VMEM((order, order), BF16),
             pltpu.VMEM(square, F32),
@@ -479,18 +480,18 @@
         cost_estimate=pl.CostEstimate(flops=20 * order**3, bytes_accessed=order * order * 16, transcendentals=0),
         name="precondition",
     )(place, damped, stats_old, *pieces)
-    sent = swap(sent, CORES)
+    sent, sent_update = swap(sent, CORES), swap(sent_update, CORES)
     return pl.pallas_call(
         finish_kernel,
         out_shape=(new_shape, jax.ShapeDtypeStruct((tiles, band, order), F32)),
-        in_specs=[SMEM, anywhere] + vmem(3),
+        in_specs=[SMEM, anywhere] + vmem(4),
         out_specs=(anywhere, anywhere),
         scratch_shapes=[pltpu.VMEM(rows_pair, F32), pltpu.SemaphoreType.DMA((4,))],
         input_output_aliases={1: 0},
         compiler_params=pltpu.CompilerParams(vmem_limit_bytes=8 << 20),
         cost_estimate=pl.CostEstimate(flops=band * order * 4, bytes_accessed=band * order * 32, transcendentals=0),
         name="finish",
-    )(place, fresh, stats_old, own, sent)
+    )(place, fresh, stats_old, own, sent, sent_update)
 
 
 def solution(mesh):

time: 55.2 us -> 55.2 us (level)
    ppermute x19 -> x20, waiting for transfers between devices: 16.3 us -> 15.8 us  [swap(): return lax.ppermute(array, ('rep', 'grp'), pairs)]
    ppermute x19 -> x20, starting transfers between devices: 24.2 us -> 24.7 us  [swap(): return lax.ppermute(array, ('rep', 'grp'), pairs)]
  transfers between devices with their start and end apart: 19 -> 20, of which waited for: 12 -> 12; matrix products, arithmetic and copies ran while one was open for 0% -> 0% of each run, Pallas kernels for 7% -> 7%
where the time goes in v6:
time: 55.2 us; the launch traced here: 55 us
  starting transfers between devices  24.7 us (45%)
  waiting for transfers between devices  15.8 us (29%)
  Pallas kernels  10.8 us (20%)
  local copies, waits for them, and re-layouts  2.43 us (4%)
  between operations  0.82 us (1%)
    ppermute x20, starting transfers between devices, swap(): return lax.ppermute(array, ('rep', 'grp'), pairs)  24.7 us
    ppermute x20, waiting for transfers between devices, swap(): return lax.ppermute(array, ('rep', 'grp'), pairs)  15.8 us
    pallas_call x1, Pallas kernels, on_device(): pl.pallas_call(functools.partial(step_kernel, numbers=numbers, rows=rows,...  4.74 us
    unnamed x6, local copies, waits for them, and re-layouts  2.27 us
    pallas_call x2, Pallas kernels, gradient_term(): pl.pallas_call(functools.partial(term_kernel, other=other, rows=rows), ou...  2.04 us
    pallas_call x1, Pallas kernels, whole_stats(): pl.pallas_call(kernel, out_shape=jax.ShapeDtypeStruct((2, order, order),...  1.95 us
    pallas_call x1, Pallas kernels, on_device(): pl.pallas_call(finish_kernel, out_shape=(new_shape, jax.ShapeDtypeStruct(...  1.36 us
  transfers between devices with their start and end apart: 20, of which 12 were waited for; matrix products, arithmetic and copies ran while one was open for 0% of the time, Pallas kernels for 7%

profile of v6, /device:TPU:0, one launch (start us, length us, event | category | flops | bytes accessed | tf_op | source)
XLA Modules:
  0.0 55.0 jit_solution(13762312520372448758)
XLA Ops:
  0.8 1.2 %copy-done = bf16[512,1024]{1,0:T(8,128)(2,1)S(1)} copy-done((bf16[512,1024]{1,0:T(8,128)(2,1)S(1)}, bf16[512,1024]{1,0:T(8,128)(2,1)}, u32[]{:S(2)}) %copy-start) | copy-done | bytes 1048600
  2.0 1.0 %copy-done.2 = bf16[512,512]{1,0:T(8,128)(2,1)S(1)} copy-done((bf16[512,512]{1,0:T(8,128)(2,1)S(1)}, bf16[512,512]{1,0:T(8,128)(2,1)}, u32[]{:S(2)}) %copy-start.2) | copy-done | bytes 524312
  3.0 1.0 %gradient_term.3 = f32[512,512]{1,0:T(8,128)S(1)} custom-call(s32[7]{0:T(128)S(1)} %stack.31.place, bf16[512,1024]{1,0:T(8,128)(2,1)S(1)} %copy-done, bf16[512,512]{1,0:T(8,128)(2,1)S(1)} %copy-done.2), custom_call_target="tpu_custom_call" | custom-call | flops 268435456 | bytes 1048576 | tf_op jit(solution)/shard_map/gradient_term/pallas_call | solution.py:115
  4.0 0.5 collective-permute-start.1
  4.6 0.7 %stage_stats.1 = (bf16[320,512]{1,0:T(8,128)(2,1)S(1)}, bf16[160,384]{1,0:T(8,128)(2,1)S(1)}, bf16[160,256]{1,0:T(8,128)(2,1)S(1)}, bf16[160,128]{1,0:T(8,128)(2,1)S(1)}) custom-call(s32[7]{0:T(128)S(1)} %stack.31.place, f32[4,64,512]{2,1,0:T(8,128)S(1)} %copy-done.1), custom_call_target="tpu_custom_call" | custom-call | flops 655360 | bytes 1048576 | tf_op jit(solution)/shard_map/stage_stats/pallas_call | solution.py:343
  5.3 1.0 %gradient_term.2 = f32[512,512]{1,0:T(8,128)S(1)} custom-call(s32[7]{0:T(128)S(1)} %stack.31.place, bf16[512,1024]{1,0:T(8,128)(2,1)S(1)} %copy-done, bf16[512,512]{1,0:T(8,128)(2,1)S(1)} %copy-done.2), custom_call_target="tpu_custom_call" | custom-call | flops 268435456 | bytes 1048576 | tf_op jit(solution)/shard_map/gradient_term/pallas_call | solution.py:115
  6.3 0.5 collective-permute-done.1
  7.1 2.9 %collective-permute-start.2 = (f32[128,512]{1,0:T(8,128)S(1)}, f32[128,512]{1,0:T(8,128)S(1)}, u32[]{:S(2)}, u32[]{:S(2)}) collective-permute-start(f32[128,512]{1,0:T(8,128)S(1)} %get-tuple-element.37), channel_id=1, source_target_pairs={{0,8},{1,17},{2,10},{3,19},{4,12},{5,21},{6,14},{7,23},{8,0},{9,25... | collective-permute-start | bytes 786440 | tf_op jit(solution)/shard_map/ppermute | solution.py:26
  10.0 3.6 %collective-permute-start.4 = (bf16[160,128]{1,0:T(8,128)(2,1)S(1)}, bf16[160,128]{1,0:T(8,128)(2,1)S(1)}, u32[]{:S(2)}, u32[]{:S(2)}) collective-permute-start(bf16[160,128]{1,0:T(8,128)(2,1)S(1)} %get-tuple-element.28), channel_id=1, source_target_pairs={{0,6},{1,7},{2,4},{3,5},{4,2},{5,3},{6,0},{7,1},{8,14},{9,15},{10,... | collective-permute-start | bytes 122888 | tf_op jit(solution)/shard_map/ppermute | solution.py:26
  13.6 0.8 %collective-permute-start = (bf16[160,384]{1,0:T(8,128)(2,1)S(1)}, bf16[160,384]{1,0:T(8,128)(2,1)S(1)}, u32[]{:S(2)}, u32[]{:S(2)}) collective-permute-start(bf16[160,384]{1,0:T(8,128)(2,1)S(1)} %get-tuple-element.24), channel_id=1, source_target_pairs={{0,2},{1,3},{2,0},{3,1},{4,6},{5,7},{6,4},{7,5},{8,10},{9,11},{10,... | collective-permute-start | bytes 368648 | tf_op jit(solution)/shard_map/ppermute | solution.py:26
  14.8 1.8 %collective-permute-start.8 = (f32[128,512]{1,0:T(8,128)S(1)}, f32[128,512]{1,0:T(8,128)S(1)}, u32[]{:S(2)}, u32[]{:S(2)}) collective-permute-start(f32[128,512]{1,0:T(8,128)S(1)} %slice_add_fusion.1), channel_id=1, source_target_pairs={{0,16},{1,9},{2,18},{3,11},{4,20},{5,13},{6,22},{7,15},{8,24},{9,1... | collective-permute-start | bytes 786440 | tf_op jit(solution)/shard_map/ppermute | solution.py:26
  16.6 2.9 %collective-permute-done.3.refs_1_ = bf16[160,256]{1,0:T(8,128)(2,1)S(1)} collective-permute-done((bf16[160,256]{1,0:T(8,128)(2,1)S(1)}, bf16[160,256]{1,0:T(8,128)(2,1)S(1)}, u32[]{:S(2)}, u32[]{:S(2)}) %collective-permute-start.3) | collective-permute-done | bytes 81952 | tf_op jit(solution)/shard_map/ppermute | solution.py:26
  19.5 0.8 %collective-permute-done.refs_0_ = bf16[160,384]{1,0:T(8,128)(2,1)S(1)} collective-permute-done((bf16[160,384]{1,0:T(8,128)(2,1)S(1)}, bf16[160,384]{1,0:T(8,128)(2,1)S(1)}, u32[]{:S(2)}, u32[]{:S(2)}) %collective-permute-start) | collective-permute-done | bytes 122912 | tf_op jit(solution)/shard_map/ppermute | solution.py:26
  20.4 1.9 %collective-permute-done.7 = f32[128,512]{1,0:T(8,128)S(1)} collective-permute-done((f32[128,512]{1,0:T(8,128)S(1)}, f32[128,512]{1,0:T(8,128)S(1)}, u32[]{:S(2)}, u32[]{:S(2)}) %collective-permute-start.7) | collective-permute-done | bytes 262176 | tf_op jit(solution)/shard_map/ppermute | solution.py:26
  22.4 3.9 %collective-permute-start.9 = (f32[32,512]{1,0:T(8,128)S(1)}, f32[32,512]{1,0:T(8,128)S(1)}, u32[]{:S(2)}, u32[]{:S(2)}) collective-permute-start(f32[32,512]{1,0:T(8,128)S(1)} %get-tuple-element.38), channel_id=1, source_target_pairs={{0,6},{1,7},{2,4},{3,5},{4,2},{5,3},{6,0},{7,1},{8,14},{9,15},{10,... | collective-permute-start | bytes 196616 | tf_op jit(solution)/shard_map/ppermute | solution.py:26
  26.3 0.6 %collective-permute-start.10 = (f32[32,512]{1,0:T(8,128)S(1)}, f32[32,512]{1,0:T(8,128)S(1)}, u32[]{:S(2)}, u32[]{:S(2)}) collective-permute-start(f32[32,512]{1,0:T(8,128)S(1)} %get-tuple-element.40), channel_id=1, source_target_pairs={{0,2},{1,3},{2,0},{3,1},{4,6},{5,7},{6,4},{7,5},{8,10},{9,11},{10,... | collective-permute-start | bytes 196616 | tf_op jit(solution)/shard_map/ppermute | solution.py:26
  27.0 1.6 %collective-permute-start.6 = (bf16[160,768]{1,0:T(8,128)(2,1)S(1)}, bf16[160,768]{1,0:T(8,128)(2,1)S(1)}, u32[]{:S(2)}, u32[]{:S(2)}) collective-permute-start(bf16[160,768]{1,0:T(8,128)(2,1)S(1)} %pad_maximum_fusion.mine), channel_id=1, source_target_pairs={{0,8},{1,9},{2,10},{3,11},{4,12},{5,13},{6,14},{7,15},{8,0},{9,1},... | collective-permute-start | bytes 737288 | tf_op jit(solution)/shard_map/ppermute | solution.py:26
  28.5 0.6 %collective-permute-done.9 = f32[32,512]{1,0:T(8,128)S(1)} collective-permute-done((f32[32,512]{1,0:T(8,128)S(1)}, f32[32,512]{1,0:T(8,128)S(1)}, u32[]{:S(2)}, u32[]{:S(2)}) %collective-permute-start.9) | collective-permute-done | bytes 65568 | tf_op jit(solution)/shard_map/ppermute | solution.py:26
  29.1 2.5 %collective-permute-done.11 = f32[32,512]{1,0:T(8,128)S(1)} collective-permute-done((f32[32,512]{1,0:T(8,128)S(1)}, f32[32,512]{1,0:T(8,128)S(1)}, u32[]{:S(2)}, u32[]{:S(2)}) %collective-permute-start.11) | collective-permute-done | bytes 65568 | tf_op jit(solution)/shard_map/ppermute | solution.py:26
  31.7 2.3 %collective-permute-start.14 = (bf16[32,512]{1,0:T(8,128)(2,1)S(1)}, bf16[32,512]{1,0:T(8,128)(2,1)S(1)}, u32[]{:S(2)}, u32[]{:S(2)}) collective-permute-start(bf16[32,512]{1,0:T(8,128)(2,1)S(1)} %add_convert_fusion), channel_id=1, source_target_pairs={{0,6},{1,7},{2,4},{3,5},{4,2},{5,3},{6,0},{7,1},{8,14},{9,15},{10,... | collective-permute-start | bytes 98312 | tf_op jit(solution)/shard_map/ppermute | solution.py:26
  34.0 2.1 %collective-permute-start.12 = (bf16[32,512]{1,0:T(8,128)(2,1)S(1)}, bf16[32,512]{1,0:T(8,128)(2,1)S(1)}, u32[]{:S(2)}, u32[]{:S(2)}) collective-permute-start(bf16[32,512]{1,0:T(8,128)(2,1)S(1)} %add_convert_fusion), channel_id=1, source_target_pairs={{0,2},{1,3},{2,0},{3,1},{4,6},{5,7},{6,4},{7,5},{8,10},{9,11},{10,... | collective-permute-start | bytes 98312 | tf_op jit(solution)/shard_map/ppermute | solution.py:26
  36.1 1.3 %collective-permute-done.14 = bf16[32,512]{1,0:T(8,128)(2,1)S(1)} collective-permute-done((bf16[32,512]{1,0:T(8,128)(2,1)S(1)}, bf16[32,512]{1,0:T(8,128)(2,1)S(1)}, u32[]{:S(2)}, u32[]{:S(2)}) %collective-permute-start.14) | collective-permute-done | bytes 32800 | tf_op jit(solution)/shard_map/ppermute | solution.py:26
  37.4 1.4 %collective-permute-done.13 = bf16[32,512]{1,0:T(8,128)(2,1)S(1)} collective-permute-done((bf16[32,512]{1,0:T(8,128)(2,1)S(1)}, bf16[32,512]{1,0:T(8,128)(2,1)S(1)}, u32[]{:S(2)}, u32[]{:S(2)}) %collective-permute-start.13) | collective-permute-done | bytes 32800 | tf_op jit(solution)/shard_map/ppermute | solution.py:26
  38.8 2.8 %collective-permute-start.17 = (bf16[128,512]{1,0:T(8,128)(2,1)S(1)}, bf16[128,512]{1,0:T(8,128)(2,1)S(1)}, u32[]{:S(2)}, u32[]{:S(2)}) collective-permute-start(bf16[128,512]{1,0:T(8,128)(2,1)S(1)} %pad_maximum_fusion.1.refs_0_), channel_id=1, source_target_pairs={{0,24},{1,25},{2,26},{3,27},{4,28},{5,29},{6,30},{7,31},{8,16},{9,... | collective-permute-start | bytes 393224 | tf_op jit(solution)/shard_map/ppermute | solution.py:26
  41.6 0.5 collective-permute-start.16
  42.4 1.9 %whole_stats.1.damped = f32[2,512,512]{2,1,0:T(8,128)S(1)} custom-call(s32[7]{0:T(128)S(1)} %stack.31.place, bf16[320,512]{1,0:T(8,128)(2,1)S(1)} %get-tuple-element.23.whole, bf16[80,1792]{1,0:T(8,128)(2,1)S(1)} %collective-permute-done.5.received, bf16[160,768]{1,0:T(8,128)(2,1)S(1)} %pad_maximum_fusion.mine, ...), custom_call_target="tpu_custom_call" | custom-call | flops 2097152 | bytes 3145728 | tf_op jit(solution)/shard_map/whole_stats/pallas_call | solution.py:393
  44.3 0.8 %collective-permute-done.17.refs_3_ = bf16[128,512]{1,0:T(8,128)(2,1)S(1)} collective-permute-done((bf16[128,512]{1,0:T(8,128)(2,1)S(1)}, bf16[128,512]{1,0:T(8,128)(2,1)S(1)}, u32[]{:S(2)}, u32[]{:S(2)}) %collective-permute-start.17) | collective-permute-done | bytes 131104 | tf_op jit(solution)/shard_map/ppermute | solution.py:26
  45.1 1.4 %collective-permute-done.16.refs_2_ = bf16[128,512]{1,0:T(8,128)(2,1)S(1)} collective-permute-done((bf16[128,512]{1,0:T(8,128)(2,1)S(1)}, bf16[128,512]{1,0:T(8,128)(2,1)S(1)}, u32[]{:S(2)}, u32[]{:S(2)}) %collective-permute-start.16) | collective-permute-done | bytes 131104 | tf_op jit(solution)/shard_map/ppermute | solution.py:26
  47.0 4.7 %precondition.1 = (f32[4,64,512]{2,1,0:T(8,128)}, f32[64,512]{1,0:T(8,128)S(1)}, f32[2,64,512]{2,1,0:T(8,128)S(1)}, f32[64,512]{1,0:T(8,128)S(1)}) custom-call(s32[7]{0:T(128)S(1)} %stack.31.place, f32[2,512,512]{2,1,0:T(8,128)S(1)} %whole_stats.1.damped, f32[4,64,512]{2,1,0:T(8,128)S(1)} %copy-done.1, bf16[128,512]{1,0:T(8,128)(2,1)S(1)} %pad_maximum_fusion.1.refs_0_, ...), custom_call_target="tpu_custom_call" | custom-call | flops 2684354560 | bytes 4194304 | tf_op jit(solution)/shard_map/precondition/pallas_call | solution.py:456
  51.9 0.5 collective-permute-start.19
  52.4 1.2 %collective-permute-done.19.sent_update = f32[64,512]{1,0:T(8,128)S(1)} collective-permute-done((f32[64,512]{1,0:T(8,128)S(1)}, f32[64,512]{1,0:T(8,128)S(1)}, u32[]{:S(2)}, u32[]{:S(2)}) %collective-permute-start.19) | collective-permute-done | bytes 131104 | tf_op jit(solution)/shard_map/ppermute | solution.py:26
  53.6 1.4 %finish.1 = (f32[4,64,512]{2,1,0:T(8,128)}, f32[2,64,512]{2,1,0:T(8,128)}) custom-call(s32[7]{0:T(128)S(1)} %stack.31.place, f32[4,64,512]{2,1,0:T(8,128)} %get-tuple-element.32.fresh, f32[4,64,512]{2,1,0:T(8,128)S(1)} %copy-done.1, f32[64,512]{1,0:T(8,128)S(1)} %get-tuple-element.33.own, ...), custom_call_target="tpu_custom_call", output_to_operand_aliasing={{0}: (1, {})} | custom-call | flops 131072 | bytes 1048576 | tf_op jit(solution)/shard_map/finish/pallas_call | solution.py:484
  (34 shorter events, 1.8 us)
Async XLA Ops:
  0.8 1.2 %copy-start = (bf16[512,1024]{1,0:T(8,128)(2,1)S(1)}, bf16[512,1024]{1,0:T(8,128)(2,1)}, u32[]{:S(2)}) copy-start(bf16[512,1024]{1,0:T(8,128)(2,1)} %grads.3) | copy-start | bytes 3145732
  2.0 1.0 %copy-start.2 = (bf16[512,512]{1,0:T(8,128)(2,1)S(1)}, bf16[512,512]{1,0:T(8,128)(2,1)}, u32[]{:S(2)}) copy-start(bf16[512,512]{1,0:T(8,128)(2,1)} %acts.3) | copy-start | bytes 1572868
  3.0 1.5 %copy-start.1 = (f32[4,64,512]{2,1,0:T(8,128)S(1)}, f32[4,64,512]{2,1,0:T(8,128)}, u32[]{:S(2)}) copy-start(f32[4,64,512]{2,1,0:T(8,128)} %stats.5) | copy-start | bytes 1572868
  4.0 2.8 %collective-permute-start.1 = (f32[512,512]{1,0:T(8,128)S(1)}, f32[512,512]{1,0:T(8,128)S(1)}, u32[]{:S(2)}, u32[]{:S(2)}) collective-permute-start(f32[512,512]{1,0:T(8,128)S(1)} %gradient_term.3), channel_id=1, source_target_pairs={{0,1},{1,0},{2,3},{3,2},{4,5},{5,4},{6,7},{7,6},{8,9},{9,8},{10,11... | collective-permute-start | bytes 3145736 | tf_op jit(solution)/shard_map/ppermute | solution.py:26
  7.1 7.6 %collective-permute-start.2 = (f32[128,512]{1,0:T(8,128)S(1)}, f32[128,512]{1,0:T(8,128)S(1)}, u32[]{:S(2)}, u32[]{:S(2)}) collective-permute-start(f32[128,512]{1,0:T(8,128)S(1)} %get-tuple-element.37), channel_id=1, source_target_pairs={{0,8},{1,17},{2,10},{3,19},{4,12},{5,21},{6,14},{7,23},{8,0},{9,25... | collective-permute-start | bytes 786440 | tf_op jit(solution)/shard_map/ppermute | solution.py:26
  10.0 6.6 %collective-permute-start.4 = (bf16[160,128]{1,0:T(8,128)(2,1)S(1)}, bf16[160,128]{1,0:T(8,128)(2,1)S(1)}, u32[]{:S(2)}, u32[]{:S(2)}) collective-permute-start(bf16[160,128]{1,0:T(8,128)(2,1)S(1)} %get-tuple-element.28), channel_id=1, source_target_pairs={{0,6},{1,7},{2,4},{3,5},{4,2},{5,3},{6,0},{7,1},{8,14},{9,15},{10,... | collective-permute-start | bytes 122888 | tf_op jit(solution)/shard_map/ppermute | solution.py:26
  13.6 5.8 %collective-permute-start.3 = (bf16[160,256]{1,0:T(8,128)(2,1)S(1)}, bf16[160,256]{1,0:T(8,128)(2,1)S(1)}, u32[]{:S(2)}, u32[]{:S(2)}) collective-permute-start(bf16[160,256]{1,0:T(8,128)(2,1)S(1)} %get-tuple-element.26), channel_id=1, source_target_pairs={{0,4},{1,5},{2,6},{3,7},{4,0},{5,1},{6,2},{7,3},{8,12},{9,13},{10,... | collective-permute-start | bytes 245768 | tf_op jit(solution)/shard_map/ppermute | solution.py:26
  13.6 6.6 %collective-permute-start = (bf16[160,384]{1,0:T(8,128)(2,1)S(1)}, bf16[160,384]{1,0:T(8,128)(2,1)S(1)}, u32[]{:S(2)}, u32[]{:S(2)}) collective-permute-start(bf16[160,384]{1,0:T(8,128)(2,1)S(1)} %get-tuple-element.24), channel_id=1, source_target_pairs={{0,2},{1,3},{2,0},{3,1},{4,6},{5,7},{6,4},{7,5},{8,10},{9,11},{10,... | collective-permute-start | bytes 368648 | tf_op jit(solution)/shard_map/ppermute | solution.py:26
  14.4 7.9 %collective-permute-start.7 = (f32[128,512]{1,0:T(8,128)S(1)}, f32[128,512]{1,0:T(8,128)S(1)}, u32[]{:S(2)}, u32[]{:S(2)}) collective-permute-start(f32[128,512]{1,0:T(8,128)S(1)} %get-tuple-element.36), channel_id=1, source_target_pairs={{0,8},{1,17},{2,10},{3,19},{4,12},{5,21},{6,14},{7,23},{8,0},{9,25... | collective-permute-start | bytes 786440 | tf_op jit(solution)/shard_map/ppermute | solution.py:26
  14.8 7.5 %collective-permute-start.8 = (f32[128,512]{1,0:T(8,128)S(1)}, f32[128,512]{1,0:T(8,128)S(1)}, u32[]{:S(2)}, u32[]{:S(2)}) collective-permute-start(f32[128,512]{1,0:T(8,128)S(1)} %slice_add_fusion.1), channel_id=1, source_target_pairs={{0,16},{1,9},{2,18},{3,11},{4,20},{5,13},{6,22},{7,15},{8,24},{9,1... | collective-permute-start | bytes 786440 | tf_op jit(solution)/shard_map/ppermute | solution.py:26
  20.3 6.6 %collective-permute-start.5 = (bf16[80,1792]{1,0:T(8,128)(2,1)S(1)}, bf16[80,1792]{1,0:T(8,128)(2,1)S(1)}, u32[]{:S(2)}, u32[]{:S(2)}) collective-permute-start(bf16[80,1792]{1,0:T(8,128)(2,1)S(1)} %join_stats.1), channel_id=1, source_target_pairs={{0,1},{1,0},{2,3},{3,2},{4,5},{5,4},{6,7},{7,6},{8,9},{9,8},{10,11... | collective-permute-start | bytes 860168 | tf_op jit(solution)/shard_map/ppermute | solution.py:26
  22.4 6.8 %collective-permute-start.9 = (f32[32,512]{1,0:T(8,128)S(1)}, f32[32,512]{1,0:T(8,128)S(1)}, u32[]{:S(2)}, u32[]{:S(2)}) collective-permute-start(f32[32,512]{1,0:T(8,128)S(1)} %get-tuple-element.38), channel_id=1, source_target_pairs={{0,6},{1,7},{2,4},{3,5},{4,2},{5,3},{6,0},{7,1},{8,14},{9,15},{10,... | collective-permute-start | bytes 196616 | tf_op jit(solution)/shard_map/ppermute | solution.py:26
  26.3 5.4 %collective-permute-start.11 = (f32[32,512]{1,0:T(8,128)S(1)}, f32[32,512]{1,0:T(8,128)S(1)}, u32[]{:S(2)}, u32[]{:S(2)}) collective-permute-start(f32[32,512]{1,0:T(8,128)S(1)} %get-tuple-element.39), channel_id=1, source_target_pairs={{0,4},{1,5},{2,6},{3,7},{4,0},{5,1},{6,2},{7,3},{8,12},{9,13},{10,... | collective-permute-start | bytes 196616 | tf_op jit(solution)/shard_map/ppermute | solution.py:26
  26.3 5.4 %collective-permute-start.10 = (f32[32,512]{1,0:T(8,128)S(1)}, f32[32,512]{1,0:T(8,128)S(1)}, u32[]{:S(2)}, u32[]{:S(2)}) collective-permute-start(f32[32,512]{1,0:T(8,128)S(1)} %get-tuple-element.40), channel_id=1, source_target_pairs={{0,2},{1,3},{2,0},{3,1},{4,6},{5,7},{6,4},{7,5},{8,10},{9,11},{10,... | collective-permute-start | bytes 196616 | tf_op jit(solution)/shard_map/ppermute | solution.py:26
  27.0 11.9 %collective-permute-start.6 = (bf16[160,768]{1,0:T(8,128)(2,1)S(1)}, bf16[160,768]{1,0:T(8,128)(2,1)S(1)}, u32[]{:S(2)}, u32[]{:S(2)}) collective-permute-start(bf16[160,768]{1,0:T(8,128)(2,1)S(1)} %pad_maximum_fusion.mine), channel_id=1, source_target_pairs={{0,8},{1,9},{2,10},{3,11},{4,12},{5,13},{6,14},{7,15},{8,0},{9,1},... | collective-permute-start | bytes 737288 | tf_op jit(solution)/shard_map/ppermute | solution.py:26
  31.7 5.8 %collective-permute-start.14 = (bf16[32,512]{1,0:T(8,128)(2,1)S(1)}, bf16[32,512]{1,0:T(8,128)(2,1)S(1)}, u32[]{:S(2)}, u32[]{:S(2)}) collective-permute-start(bf16[32,512]{1,0:T(8,128)(2,1)S(1)} %add_convert_fusion), channel_id=1, source_target_pairs={{0,6},{1,7},{2,4},{3,5},{4,2},{5,3},{6,0},{7,1},{8,14},{9,15},{10,... | collective-permute-start | bytes 98312 | tf_op jit(solution)/shard_map/ppermute | solution.py:26
  34.0 4.8 %collective-permute-start.13 = (bf16[32,512]{1,0:T(8,128)(2,1)S(1)}, bf16[32,512]{1,0:T(8,128)(2,1)S(1)}, u32[]{:S(2)}, u32[]{:S(2)}) collective-permute-start(bf16[32,512]{1,0:T(8,128)(2,1)S(1)} %add_convert_fusion), channel_id=1, source_target_pairs={{0,4},{1,5},{2,6},{3,7},{4,0},{5,1},{6,2},{7,3},{8,12},{9,13},{10,... | collective-permute-start | bytes 98312 | tf_op jit(solution)/shard_map/ppermute | solution.py:26
  34.0 4.8 %collective-permute-start.12 = (bf16[32,512]{1,0:T(8,128)(2,1)S(1)}, bf16[32,512]{1,0:T(8,128)(2,1)S(1)}, u32[]{:S(2)}, u32[]{:S(2)}) collective-permute-start(bf16[32,512]{1,0:T(8,128)(2,1)S(1)} %add_convert_fusion), channel_id=1, source_target_pairs={{0,2},{1,3},{2,0},{3,1},{4,6},{5,7},{6,4},{7,5},{8,10},{9,11},{10,... | collective-permute-start | bytes 98312 | tf_op jit(solution)/shard_map/ppermute | solution.py:26
  38.8 6.3 %collective-permute-start.17 = (bf16[128,512]{1,0:T(8,128)(2,1)S(1)}, bf16[128,512]{1,0:T(8,128)(2,1)S(1)}, u32[]{:S(2)}, u32[]{:S(2)}) collective-permute-start(bf16[128,512]{1,0:T(8,128)(2,1)S(1)} %pad_maximum_fusion.1.refs_0_), channel_id=1, source_target_pairs={{0,24},{1,25},{2,26},{3,27},{4,28},{5,29},{6,30},{7,31},{8,16},{9,... | collective-permute-start | bytes 393224 | tf_op jit(solution)/shard_map/ppermute | solution.py:26
  41.6 5.0 %collective-permute-start.16 = (bf16[128,512]{1,0:T(8,128)(2,1)S(1)}, bf16[128,512]{1,0:T(8,128)(2,1)S(1)}, u32[]{:S(2)}, u32[]{:S(2)}) collective-permute-start(bf16[128,512]{1,0:T(8,128)(2,1)S(1)} %pad_maximum_fusion.1.refs_0_), channel_id=1, source_target_pairs={{0,16},{1,9},{2,18},{3,11},{4,20},{5,13},{6,22},{7,15},{8,24},{9,1... | collective-permute-start | bytes 393224 | tf_op jit(solution)/shard_map/ppermute | solution.py:26
  42.1 5.0 %collective-permute-start.15 = (bf16[128,512]{1,0:T(8,128)(2,1)S(1)}, bf16[128,512]{1,0:T(8,128)(2,1)S(1)}, u32[]{:S(2)}, u32[]{:S(2)}) collective-permute-start(bf16[128,512]{1,0:T(8,128)(2,1)S(1)} %pad_maximum_fusion.1.refs_0_), channel_id=1, source_target_pairs={{0,8},{1,17},{2,10},{3,19},{4,12},{5,21},{6,14},{7,23},{8,0},{9,25... | collective-permute-start | bytes 393224 | tf_op jit(solution)/shard_map/ppermute | solution.py:26
  51.8 1.8 %collective-permute-start.18 = (f32[2,64,512]{2,1,0:T(8,128)S(1)}, f32[2,64,512]{2,1,0:T(8,128)S(1)}, u32[]{:S(2)}, u32[]{:S(2)}) collective-permute-start(f32[2,64,512]{2,1,0:T(8,128)S(1)} %get-tuple-element.34), channel_id=1, source_target_pairs={{0,1},{1,0},{2,3},{3,2},{4,5},{5,4},{6,7},{7,6},{8,9},{9,8},{10,11... | collective-permute-start | bytes 786440 | tf_op jit(solution)/shard_map/ppermute | solution.py:26
  51.9 1.7 %collective-permute-start.19 = (f32[64,512]{1,0:T(8,128)S(1)}, f32[64,512]{1,0:T(8,128)S(1)}, u32[]{:S(2)}, u32[]{:S(2)}) collective-permute-start(f32[64,512]{1,0:T(8,128)S(1)} %get-tuple-element.35), channel_id=1, source_target_pairs={{0,1},{1,0},{2,3},{3,2},{4,5},{5,4},{6,7},{7,6},{8,9},{9,8},{10,11... | collective-permute-start | bytes 393224 | tf_op jit(solution)/shard_map/ppermute | solution.py:26

commit v7 on v6

--- a/solution.py
+++ b/solution.py
@@ -324,12 +324,13 @@
         pltpu.make_async_copy(own, update.at[place[CORE]], sems.at[0]),
         pltpu.make_async_copy(sent_update, update.at[other], sems.at[1]),
     ]
+    for copy in copies:
+        copy.start()
     for side in range(2):
         chain = side * tiles + other
         added[side] = stats[chain] + sent[side]
         copies.append(pltpu.make_async_copy(added.at[side], out.at[chain], sems.at[2 + side]))
-    for copy in copies:
-        copy.start()
+        copies[-1].start()
     for copy in copies:
         copy.wait()
 

time: 55.2 us -> 55.2 us (level)
  no operation moved by 1% of the time
where the time goes in v7:
time: 55.2 us; the launch traced here: 54.9 us
  starting transfers between devices  24.7 us (45%)
  waiting for transfers between devices  15.8 us (29%)
  Pallas kernels  10.8 us (20%)
  local copies, waits for them, and re-layouts  2.43 us (4%)
  between operations  0.82 us (1%)
    ppermute x20, starting transfers between devices, swap(): return lax.ppermute(array, ('rep', 'grp'), pairs)  24.7 us
    ppermute x20, waiting for transfers between devices, swap(): return lax.ppermute(array, ('rep', 'grp'), pairs)  15.8 us
    pallas_call x1, Pallas kernels, on_device(): pl.pallas_call(functools.partial(step_kernel, numbers=numbers, rows=rows,...  4.74 us
    unnamed x6, local copies, waits for them, and re-layouts  2.27 us
    pallas_call x2, Pallas kernels, gradient_term(): pl.pallas_call(functools.partial(term_kernel, other=other, rows=rows), ou...  2.04 us
    pallas_call x1, Pallas kernels, whole_stats(): pl.pallas_call(kernel, out_shape=jax.ShapeDtypeStruct((2, order, order),...  1.95 us
    pallas_call x1, Pallas kernels, on_device(): pl.pallas_call(finish_kernel, out_shape=(new_shape, jax.ShapeDtypeStruct(...  1.36 us
  transfers between devices with their start and end apart: 20, of which 12 were waited for; matrix products, arithmetic and copies ran while one was open for 0% of the time, Pallas kernels for 7%

profile of v7, /device:TPU:0, one launch (start us, length us, event | category | flops | bytes accessed | tf_op | source)
XLA Modules:
  0.0 54.9 jit_solution(5278532807114596035)
XLA Ops:
  0.8 1.2 %copy-done = bf16[512,1024]{1,0:T(8,128)(2,1)S(1)} copy-done((bf16[512,1024]{1,0:T(8,128)(2,1)S(1)}, bf16[512,1024]{1,0:T(8,128)(2,1)}, u32[]{:S(2)}) %copy-start) | copy-done | bytes 1048600
  2.0 1.0 %copy-done.2 = bf16[512,512]{1,0:T(8,128)(2,1)S(1)} copy-done((bf16[512,512]{1,0:T(8,128)(2,1)S(1)}, bf16[512,512]{1,0:T(8,128)(2,1)}, u32[]{:S(2)}) %copy-start.2) | copy-done | bytes 524312
  3.0 1.0 %gradient_term.3 = f32[512,512]{1,0:T(8,128)S(1)} custom-call(s32[7]{0:T(128)S(1)} %stack.31.place, bf16[512,1024]{1,0:T(8,128)(2,1)S(1)} %copy-done, bf16[512,512]{1,0:T(8,128)(2,1)S(1)} %copy-done.2), custom_call_target="tpu_custom_call" | custom-call | flops 268435456 | bytes 1048576 | tf_op jit(solution)/shard_map/gradient_term/pallas_call | solution.py:115
  4.0 0.5 collective-permute-start.1
  4.6 0.7 %stage_stats.1 = (bf16[320,512]{1,0:T(8,128)(2,1)S(1)}, bf16[160,384]{1,0:T(8,128)(2,1)S(1)}, bf16[160,256]{1,0:T(8,128)(2,1)S(1)}, bf16[160,128]{1,0:T(8,128)(2,1)S(1)}) custom-call(s32[7]{0:T(128)S(1)} %stack.31.place, f32[4,64,512]{2,1,0:T(8,128)S(1)} %copy-done.1), custom_call_target="tpu_custom_call" | custom-call | flops 655360 | bytes 1048576 | tf_op jit(solution)/shard_map/stage_stats/pallas_call | solution.py:344
  5.3 1.0 %gradient_term.2 = f32[512,512]{1,0:T(8,128)S(1)} custom-call(s32[7]{0:T(128)S(1)} %stack.31.place, bf16[512,1024]{1,0:T(8,128)(2,1)S(1)} %copy-done, bf16[512,512]{1,0:T(8,128)(2,1)S(1)} %copy-done.2), custom_call_target="tpu_custom_call" | custom-call | flops 268435456 | bytes 1048576 | tf_op jit(solution)/shard_map/gradient_term/pallas_call | solution.py:115
  6.3 0.5 collective-permute-done.1
  7.1 2.9 %collective-permute-start.2 = (f32[128,512]{1,0:T(8,128)S(1)}, f32[128,512]{1,0:T(8,128)S(1)}, u32[]{:S(2)}, u32[]{:S(2)}) collective-permute-start(f32[128,512]{1,0:T(8,128)S(1)} %get-tuple-element.37), channel_id=1, source_target_pairs={{0,8},{1,17},{2,10},{3,19},{4,12},{5,21},{6,14},{7,23},{8,0},{9,25... | collective-permute-start | bytes 786440 | tf_op jit(solution)/shard_map/ppermute | solution.py:26
  10.0 3.6 %collective-permute-start.4 = (bf16[160,128]{1,0:T(8,128)(2,1)S(1)}, bf16[160,128]{1,0:T(8,128)(2,1)S(1)}, u32[]{:S(2)}, u32[]{:S(2)}) collective-permute-start(bf16[160,128]{1,0:T(8,128)(2,1)S(1)} %get-tuple-element.28), channel_id=1, source_target_pairs={{0,6},{1,7},{2,4},{3,5},{4,2},{5,3},{6,0},{7,1},{8,14},{9,15},{10,... | collective-permute-start | bytes 122888 | tf_op jit(solution)/shard_map/ppermute | solution.py:26
  13.6 0.8 %collective-permute-start = (bf16[160,384]{1,0:T(8,128)(2,1)S(1)}, bf16[160,384]{1,0:T(8,128)(2,1)S(1)}, u32[]{:S(2)}, u32[]{:S(2)}) collective-permute-start(bf16[160,384]{1,0:T(8,128)(2,1)S(1)} %get-tuple-element.24), channel_id=1, source_target_pairs={{0,2},{1,3},{2,0},{3,1},{4,6},{5,7},{6,4},{7,5},{8,10},{9,11},{10,... | collective-permute-start | bytes 368648 | tf_op jit(solution)/shard_map/ppermute | solution.py:26
  14.8 1.8 %collective-permute-start.8 = (f32[128,512]{1,0:T(8,128)S(1)}, f32[128,512]{1,0:T(8,128)S(1)}, u32[]{:S(2)}, u32[]{:S(2)}) collective-permute-start(f32[128,512]{1,0:T(8,128)S(1)} %slice_add_fusion.1), channel_id=1, source_target_pairs={{0,16},{1,9},{2,18},{3,11},{4,20},{5,13},{6,22},{7,15},{8,24},{9,1... | collective-permute-start | bytes 786440 | tf_op jit(solution)/shard_map/ppermute | solution.py:26
  16.6 2.9 %collective-permute-done.3.refs_1_ = bf16[160,256]{1,0:T(8,128)(2,1)S(1)} collective-permute-done((bf16[160,256]{1,0:T(8,128)(2,1)S(1)}, bf16[160,256]{1,0:T(8,128)(2,1)S(1)}, u32[]{:S(2)}, u32[]{:S(2)}) %collective-permute-start.3) | collective-permute-done | bytes 81952 | tf_op jit(solution)/shard_map/ppermute | solution.py:26
  19.5 0.8 %collective-permute-done.refs_0_ = bf16[160,384]{1,0:T(8,128)(2,1)S(1)} collective-permute-done((bf16[160,384]{1,0:T(8,128)(2,1)S(1)}, bf16[160,384]{1,0:T(8,128)(2,1)S(1)}, u32[]{:S(2)}, u32[]{:S(2)}) %collective-permute-start) | collective-permute-done | bytes 122912 | tf_op jit(solution)/shard_map/ppermute | solution.py:26
  20.4 1.9 %collective-permute-done.7 = f32[128,512]{1,0:T(8,128)S(1)} collective-permute-done((f32[128,512]{1,0:T(8,128)S(1)}, f32[128,512]{1,0:T(8,128)S(1)}, u32[]{:S(2)}, u32[]{:S(2)}) %collective-permute-start.7) | collective-permute-done | bytes 262176 | tf_op jit(solution)/shard_map/ppermute | solution.py:26
  22.4 3.9 %collective-permute-start.9 = (f32[32,512]{1,0:T(8,128)S(1)}, f32[32,512]{1,0:T(8,128)S(1)}, u32[]{:S(2)}, u32[]{:S(2)}) collective-permute-start(f32[32,512]{1,0:T(8,128)S(1)} %get-tuple-element.38), channel_id=1, source_target_pairs={{0,6},{1,7},{2,4},{3,5},{4,2},{5,3},{6,0},{7,1},{8,14},{9,15},{10,... | collective-permute-start | bytes 196616 | tf_op jit(solution)/shard_map/ppermute | solution.py:26
  26.3 0.6 %collective-permute-start.10 = (f32[32,512]{1,0:T(8,128)S(1)}, f32[32,512]{1,0:T(8,128)S(1)}, u32[]{:S(2)}, u32[]{:S(2)}) collective-permute-start(f32[32,512]{1,0:T(8,128)S(1)} %get-tuple-element.40), channel_id=1, source_target_pairs={{0,2},{1,3},{2,0},{3,1},{4,6},{5,7},{6,4},{7,5},{8,10},{9,11},{10,... | collective-permute-start | bytes 196616 | tf_op jit(solution)/shard_map/ppermute | solution.py:26
  27.0 1.6 %collective-permute-start.6 = (bf16[160,768]{1,0:T(8,128)(2,1)S(1)}, bf16[160,768]{1,0:T(8,128)(2,1)S(1)}, u32[]{:S(2)}, u32[]{:S(2)}) collective-permute-start(bf16[160,768]{1,0:T(8,128)(2,1)S(1)} %pad_maximum_fusion.mine), channel_id=1, source_target_pairs={{0,8},{1,9},{2,10},{3,11},{4,12},{5,13},{6,14},{7,15},{8,0},{9,1},... | collective-permute-start | bytes 737288 | tf_op jit(solution)/shard_map/ppermute | solution.py:26
  28.5 0.6 %collective-permute-done.9 = f32[32,512]{1,0:T(8,128)S(1)} collective-permute-done((f32[32,512]{1,0:T(8,128)S(1)}, f32[32,512]{1,0:T(8,128)S(1)}, u32[]{:S(2)}, u32[]{:S(2)}) %collective-permute-start.9) | collective-permute-done | bytes 65568 | tf_op jit(solution)/shard_map/ppermute | solution.py:26
  29.1 2.5 %collective-permute-done.11 = f32[32,512]{1,0:T(8,128)S(1)} collective-permute-done((f32[32,512]{1,0:T(8,128)S(1)}, f32[32,512]{1,0:T(8,128)S(1)}, u32[]{:S(2)}, u32[]{:S(2)}) %collective-permute-start.11) | collective-permute-done | bytes 65568 | tf_op jit(solution)/shard_map/ppermute | solution.py:26
  31.7 2.3 %collective-permute-start.14 = (bf16[32,512]{1,0:T(8,128)(2,1)S(1)}, bf16[32,512]{1,0:T(8,128)(2,1)S(1)}, u32[]{:S(2)}, u32[]{:S(2)}) collective-permute-start(bf16[32,512]{1,0:T(8,128)(2,1)S(1)} %add_convert_fusion), channel_id=1, source_target_pairs={{0,6},{1,7},{2,4},{3,5},{4,2},{5,3},{6,0},{7,1},{8,14},{9,15},{10,... | collective-permute-start | bytes 98312 | tf_op jit(solution)/shard_map/ppermute | solution.py:26
  34.0 2.1 %collective-permute-start.12 = (bf16[32,512]{1,0:T(8,128)(2,1)S(1)}, bf16[32,512]{1,0:T(8,128)(2,1)S(1)}, u32[]{:S(2)}, u32[]{:S(2)}) collective-permute-start(bf16[32,512]{1,0:T(8,128)(2,1)S(1)} %add_convert_fusion), channel_id=1, source_target_pairs={{0,2},{1,3},{2,0},{3,1},{4,6},{5,7},{6,4},{7,5},{8,10},{9,11},{10,... | collective-permute-start | bytes 98312 | tf_op jit(solution)/shard_map/ppermute | solution.py:26
  36.1 1.3 %collective-permute-done.14 = bf16[32,512]{1,0:T(8,128)(2,1)S(1)} collective-permute-done((bf16[32,512]{1,0:T(8,128)(2,1)S(1)}, bf16[32,512]{1,0:T(8,128)(2,1)S(1)}, u32[]{:S(2)}, u32[]{:S(2)}) %collective-permute-start.14) | collective-permute-done | bytes 32800 | tf_op jit(solution)/shard_map/ppermute | solution.py:26
  37.4 1.4 %collective-permute-done.13 = bf16[32,512]{1,0:T(8,128)(2,1)S(1)} collective-permute-done((bf16[32,512]{1,0:T(8,128)(2,1)S(1)}, bf16[32,512]{1,0:T(8,128)(2,1)S(1)}, u32[]{:S(2)}, u32[]{:S(2)}) %collective-permute-start.13) | collective-permute-done | bytes 32800 | tf_op jit(solution)/shard_map/ppermute | solution.py:26
  38.8 2.8 %collective-permute-start.17 = (bf16[128,512]{1,0:T(8,128)(2,1)S(1)}, bf16[128,512]{1,0:T(8,128)(2,1)S(1)}, u32[]{:S(2)}, u32[]{:S(2)}) collective-permute-start(bf16[128,512]{1,0:T(8,128)(2,1)S(1)} %pad_maximum_fusion.1.refs_0_), channel_id=1, source_target_pairs={{0,24},{1,25},{2,26},{3,27},{4,28},{5,29},{6,30},{7,31},{8,16},{9,... | collective-permute-start | bytes 393224 | tf_op jit(solution)/shard_map/ppermute | solution.py:26
  41.6 0.5 collective-permute-start.16
  42.4 1.9 %whole_stats.1.damped = f32[2,512,512]{2,1,0:T(8,128)S(1)} custom-call(s32[7]{0:T(128)S(1)} %stack.31.place, bf16[320,512]{1,0:T(8,128)(2,1)S(1)} %get-tuple-element.23.whole, bf16[80,1792]{1,0:T(8,128)(2,1)S(1)} %collective-permute-done.5.received, bf16[160,768]{1,0:T(8,128)(2,1)S(1)} %pad_maximum_fusion.mine, ...), custom_call_target="tpu_custom_call" | custom-call | flops 2097152 | bytes 3145728 | tf_op jit(solution)/shard_map/whole_stats/pallas_call | solution.py:394
  44.3 0.8 %collective-permute-done.17.refs_3_ = bf16[128,512]{1,0:T(8,128)(2,1)S(1)} collective-permute-done((bf16[128,512]{1,0:T(8,128)(2,1)S(1)}, bf16[128,512]{1,0:T(8,128)(2,1)S(1)}, u32[]{:S(2)}, u32[]{:S(2)}) %collective-permute-start.17) | collective-permute-done | bytes 131104 | tf_op jit(solution)/shard_map/ppermute | solution.py:26
  45.1 1.4 %collective-permute-done.16.refs_2_ = bf16[128,512]{1,0:T(8,128)(2,1)S(1)} collective-permute-done((bf16[128,512]{1,0:T(8,128)(2,1)S(1)}, bf16[128,512]{1,0:T(8,128)(2,1)S(1)}, u32[]{:S(2)}, u32[]{:S(2)}) %collective-permute-start.16) | collective-permute-done | bytes 131104 | tf_op jit(solution)/shard_map/ppermute | solution.py:26
  47.0 4.7 %precondition.1 = (f32[4,64,512]{2,1,0:T(8,128)}, f32[64,512]{1,0:T(8,128)S(1)}, f32[2,64,512]{2,1,0:T(8,128)S(1)}, f32[64,512]{1,0:T(8,128)S(1)}) custom-call(s32[7]{0:T(128)S(1)} %stack.31.place, f32[2,512,512]{2,1,0:T(8,128)S(1)} %whole_stats.1.damped, f32[4,64,512]{2,1,0:T(8,128)S(1)} %copy-done.1, bf16[128,512]{1,0:T(8,128)(2,1)S(1)} %pad_maximum_fusion.1.refs_0_, ...), custom_call_target="tpu_custom_call" | custom-call | flops 2684354560 | bytes 4194304 | tf_op jit(solution)/shard_map/precondition/pallas_call | solution.py:457
  51.9 0.5 collective-permute-start.19
  52.4 1.2 %collective-permute-done.19.sent_update = f32[64,512]{1,0:T(8,128)S(1)} collective-permute-done((f32[64,512]{1,0:T(8,128)S(1)}, f32[64,512]{1,0:T(8,128)S(1)}, u32[]{:S(2)}, u32[]{:S(2)}) %collective-permute-start.19) | collective-permute-done | bytes 131104 | tf_op jit(solution)/shard_map/ppermute | solution.py:26
  53.6 1.4 %finish.1 = (f32[4,64,512]{2,1,0:T(8,128)}, f32[2,64,512]{2,1,0:T(8,128)}) custom-call(s32[7]{0:T(128)S(1)} %stack.31.place, f32[4,64,512]{2,1,0:T(8,128)} %get-tuple-element.32.fresh, f32[4,64,512]{2,1,0:T(8,128)S(1)} %copy-done.1, f32[64,512]{1,0:T(8,128)S(1)} %get-tuple-element.33.own, ...), custom_call_target="tpu_custom_call", output_to_operand_aliasing={{0}: (1, {})} | custom-call | flops 131072 | bytes 1048576 | tf_op jit(solution)/shard_map/finish/pallas_call | solution.py:485
  (34 shorter events, 1.8 us)
Async XLA Ops:
  0.8 1.2 %copy-start = (bf16[512,1024]{1,0:T(8,128)(2,1)S(1)}, bf16[512,1024]{1,0:T(8,128)(2,1)}, u32[]{:S(2)}) copy-start(bf16[512,1024]{1,0:T(8,128)(2,1)} %grads.3) | copy-start | bytes 3145732
  2.0 1.0 %copy-start.2 = (bf16[512,512]{1,0:T(8,128)(2,1)S(1)}, bf16[512,512]{1,0:T(8,128)(2,1)}, u32[]{:S(2)}) copy-start(bf16[512,512]{1,0:T(8,128)(2,1)} %acts.3) | copy-start | bytes 1572868
  3.0 1.5 %copy-start.1 = (f32[4,64,512]{2,1,0:T(8,128)S(1)}, f32[4,64,512]{2,1,0:T(8,128)}, u32[]{:S(2)}) copy-start(f32[4,64,512]{2,1,0:T(8,128)} %stats.5) | copy-start | bytes 1572868
  4.0 2.8 %collective-permute-start.1 = (f32[512,512]{1,0:T(8,128)S(1)}, f32[512,512]{1,0:T(8,128)S(1)}, u32[]{:S(2)}, u32[]{:S(2)}) collective-permute-start(f32[512,512]{1,0:T(8,128)S(1)} %gradient_term.3), channel_id=1, source_target_pairs={{0,1},{1,0},{2,3},{3,2},{4,5},{5,4},{6,7},{7,6},{8,9},{9,8},{10,11... | collective-permute-start | bytes 3145736 | tf_op jit(solution)/shard_map/ppermute | solution.py:26
  7.1 7.6 %collective-permute-start.2 = (f32[128,512]{1,0:T(8,128)S(1)}, f32[128,512]{1,0:T(8,128)S(1)}, u32[]{:S(2)}, u32[]{:S(2)}) collective-permute-start(f32[128,512]{1,0:T(8,128)S(1)} %get-tuple-element.37), channel_id=1, source_target_pairs={{0,8},{1,17},{2,10},{3,19},{4,12},{5,21},{6,14},{7,23},{8,0},{9,25... | collective-permute-start | bytes 786440 | tf_op jit(solution)/shard_map/ppermute | solution.py:26
  10.0 6.6 %collective-permute-start.4 = (bf16[160,128]{1,0:T(8,128)(2,1)S(1)}, bf16[160,128]{1,0:T(8,128)(2,1)S(1)}, u32[]{:S(2)}, u32[]{:S(2)}) collective-permute-start(bf16[160,128]{1,0:T(8,128)(2,1)S(1)} %get-tuple-element.28), channel_id=1, source_target_pairs={{0,6},{1,7},{2,4},{3,5},{4,2},{5,3},{6,0},{7,1},{8,14},{9,15},{10,... | collective-permute-start | bytes 122888 | tf_op jit(solution)/shard_map/ppermute | solution.py:26
  13.6 5.8 %collective-permute-start.3 = (bf16[160,256]{1,0:T(8,128)(2,1)S(1)}, bf16[160,256]{1,0:T(8,128)(2,1)S(1)}, u32[]{:S(2)}, u32[]{:S(2)}) collective-permute-start(bf16[160,256]{1,0:T(8,128)(2,1)S(1)} %get-tuple-element.26), channel_id=1, source_target_pairs={{0,4},{1,5},{2,6},{3,7},{4,0},{5,1},{6,2},{7,3},{8,12},{9,13},{10,... | collective-permute-start | bytes 245768 | tf_op jit(solution)/shard_map/ppermute | solution.py:26
  13.6 6.6 %collective-permute-start = (bf16[160,384]{1,0:T(8,128)(2,1)S(1)}, bf16[160,384]{1,0:T(8,128)(2,1)S(1)}, u32[]{:S(2)}, u32[]{:S(2)}) collective-permute-start(bf16[160,384]{1,0:T(8,128)(2,1)S(1)} %get-tuple-element.24), channel_id=1, source_target_pairs={{0,2},{1,3},{2,0},{3,1},{4,6},{5,7},{6,4},{7,5},{8,10},{9,11},{10,... | collective-permute-start | bytes 368648 | tf_op jit(solution)/shard_map/ppermute | solution.py:26
  14.4 7.9 %collective-permute-start.7 = (f32[128,512]{1,0:T(8,128)S(1)}, f32[128,512]{1,0:T(8,128)S(1)}, u32[]{:S(2)}, u32[]{:S(2)}) collective-permute-start(f32[128,512]{1,0:T(8,128)S(1)} %get-tuple-element.36), channel_id=1, source_target_pairs={{0,8},{1,17},{2,10},{3,19},{4,12},{5,21},{6,14},{7,23},{8,0},{9,25... | collective-permute-start | bytes 786440 | tf_op jit(solution)/shard_map/ppermute | solution.py:26
  14.8 7.5 %collective-permute-start.8 = (f32[128,512]{1,0:T(8,128)S(1)}, f32[128,512]{1,0:T(8,128)S(1)}, u32[]{:S(2)}, u32[]{:S(2)}) collective-permute-start(f32[128,512]{1,0:T(8,128)S(1)} %slice_add_fusion.1), channel_id=1, source_target_pairs={{0,16},{1,9},{2,18},{3,11},{4,20},{5,13},{6,22},{7,15},{8,24},{9,1... | collective-permute-start | bytes 786440 | tf_op jit(solution)/shard_map/ppermute | solution.py:26
  20.3 6.6 %collective-permute-start.5 = (bf16[80,1792]{1,0:T(8,128)(2,1)S(1)}, bf16[80,1792]{1,0:T(8,128)(2,1)S(1)}, u32[]{:S(2)}, u32[]{:S(2)}) collective-permute-start(bf16[80,1792]{1,0:T(8,128)(2,1)S(1)} %join_stats.1), channel_id=1, source_target_pairs={{0,1},{1,0},{2,3},{3,2},{4,5},{5,4},{6,7},{7,6},{8,9},{9,8},{10,11... | collective-permute-start | bytes 860168 | tf_op jit(solution)/shard_map/ppermute | solution.py:26
  22.4 6.8 %collective-permute-start.9 = (f32[32,512]{1,0:T(8,128)S(1)}, f32[32,512]{1,0:T(8,128)S(1)}, u32[]{:S(2)}, u32[]{:S(2)}) collective-permute-start(f32[32,512]{1,0:T(8,128)S(1)} %get-tuple-element.38), channel_id=1, source_target_pairs={{0,6},{1,7},{2,4},{3,5},{4,2},{5,3},{6,0},{7,1},{8,14},{9,15},{10,... | collective-permute-start | bytes 196616 | tf_op jit(solution)/shard_map/ppermute | solution.py:26
  26.3 5.4 %collective-permute-start.11 = (f32[32,512]{1,0:T(8,128)S(1)}, f32[32,512]{1,0:T(8,128)S(1)}, u32[]{:S(2)}, u32[]{:S(2)}) collective-permute-start(f32[32,512]{1,0:T(8,128)S(1)} %get-tuple-element.39), channel_id=1, source_target_pairs={{0,4},{1,5},{2,6},{3,7},{4,0},{5,1},{6,2},{7,3},{8,12},{9,13},{10,... | collective-permute-start | bytes 196616 | tf_op jit(solution)/shard_map/ppermute | solution.py:26
  26.3 5.4 %collective-permute-start.10 = (f32[32,512]{1,0:T(8,128)S(1)}, f32[32,512]{1,0:T(8,128)S(1)}, u32[]{:S(2)}, u32[]{:S(2)}) collective-permute-start(f32[32,512]{1,0:T(8,128)S(1)} %get-tuple-element.40), channel_id=1, source_target_pairs={{0,2},{1,3},{2,0},{3,1},{4,6},{5,7},{6,4},{7,5},{8,10},{9,11},{10,... | collective-permute-start | bytes 196616 | tf_op jit(solution)/shard_map/ppermute | solution.py:26
  27.0 11.9 %collective-permute-start.6 = (bf16[160,768]{1,0:T(8,128)(2,1)S(1)}, bf16[160,768]{1,0:T(8,128)(2,1)S(1)}, u32[]{:S(2)}, u32[]{:S(2)}) collective-permute-start(bf16[160,768]{1,0:T(8,128)(2,1)S(1)} %pad_maximum_fusion.mine), channel_id=1, source_target_pairs={{0,8},{1,9},{2,10},{3,11},{4,12},{5,13},{6,14},{7,15},{8,0},{9,1},... | collective-permute-start | bytes 737288 | tf_op jit(solution)/shard_map/ppermute | solution.py:26
  31.7 5.8 %collective-permute-start.14 = (bf16[32,512]{1,0:T(8,128)(2,1)S(1)}, bf16[32,512]{1,0:T(8,128)(2,1)S(1)}, u32[]{:S(2)}, u32[]{:S(2)}) collective-permute-start(bf16[32,512]{1,0:T(8,128)(2,1)S(1)} %add_convert_fusion), channel_id=1, source_target_pairs={{0,6},{1,7},{2,4},{3,5},{4,2},{5,3},{6,0},{7,1},{8,14},{9,15},{10,... | collective-permute-start | bytes 98312 | tf_op jit(solution)/shard_map/ppermute | solution.py:26
  34.0 4.8 %collective-permute-start.13 = (bf16[32,512]{1,0:T(8,128)(2,1)S(1)}, bf16[32,512]{1,0:T(8,128)(2,1)S(1)}, u32[]{:S(2)}, u32[]{:S(2)}) collective-permute-start(bf16[32,512]{1,0:T(8,128)(2,1)S(1)} %add_convert_fusion), channel_id=1, source_target_pairs={{0,4},{1,5},{2,6},{3,7},{4,0},{5,1},{6,2},{7,3},{8,12},{9,13},{10,... | collective-permute-start | bytes 98312 | tf_op jit(solution)/shard_map/ppermute | solution.py:26
  34.0 4.8 %collective-permute-start.12 = (bf16[32,512]{1,0:T(8,128)(2,1)S(1)}, bf16[32,512]{1,0:T(8,128)(2,1)S(1)}, u32[]{:S(2)}, u32[]{:S(2)}) collective-permute-start(bf16[32,512]{1,0:T(8,128)(2,1)S(1)} %add_convert_fusion), channel_id=1, source_target_pairs={{0,2},{1,3},{2,0},{3,1},{4,6},{5,7},{6,4},{7,5},{8,10},{9,11},{10,... | collective-permute-start | bytes 98312 | tf_op jit(solution)/shard_map/ppermute | solution.py:26
  38.8 6.3 %collective-permute-start.17 = (bf16[128,512]{1,0:T(8,128)(2,1)S(1)}, bf16[128,512]{1,0:T(8,128)(2,1)S(1)}, u32[]{:S(2)}, u32[]{:S(2)}) collective-permute-start(bf16[128,512]{1,0:T(8,128)(2,1)S(1)} %pad_maximum_fusion.1.refs_0_), channel_id=1, source_target_pairs={{0,24},{1,25},{2,26},{3,27},{4,28},{5,29},{6,30},{7,31},{8,16},{9,... | collective-permute-start | bytes 393224 | tf_op jit(solution)/shard_map/ppermute | solution.py:26
  41.6 5.0 %collective-permute-start.16 = (bf16[128,512]{1,0:T(8,128)(2,1)S(1)}, bf16[128,512]{1,0:T(8,128)(2,1)S(1)}, u32[]{:S(2)}, u32[]{:S(2)}) collective-permute-start(bf16[128,512]{1,0:T(8,128)(2,1)S(1)} %pad_maximum_fusion.1.refs_0_), channel_id=1, source_target_pairs={{0,16},{1,9},{2,18},{3,11},{4,20},{5,13},{6,22},{7,15},{8,24},{9,1... | collective-permute-start | bytes 393224 | tf_op jit(solution)/shard_map/ppermute | solution.py:26
  42.1 5.0 %collective-permute-start.15 = (bf16[128,512]{1,0:T(8,128)(2,1)S(1)}, bf16[128,512]{1,0:T(8,128)(2,1)S(1)}, u32[]{:S(2)}, u32[]{:S(2)}) collective-permute-start(bf16[128,512]{1,0:T(8,128)(2,1)S(1)} %pad_maximum_fusion.1.refs_0_), channel_id=1, source_target_pairs={{0,8},{1,17},{2,10},{3,19},{4,12},{5,21},{6,14},{7,23},{8,0},{9,25... | collective-permute-start | bytes 393224 | tf_op jit(solution)/shard_map/ppermute | solution.py:26
  51.8 1.8 %collective-permute-start.18 = (f32[2,64,512]{2,1,0:T(8,128)S(1)}, f32[2,64,512]{2,1,0:T(8,128)S(1)}, u32[]{:S(2)}, u32[]{:S(2)}) collective-permute-start(f32[2,64,512]{2,1,0:T(8,128)S(1)} %get-tuple-element.34), channel_id=1, source_target_pairs={{0,1},{1,0},{2,3},{3,2},{4,5},{5,4},{6,7},{7,6},{8,9},{9,8},{10,11... | collective-permute-start | bytes 786440 | tf_op jit(solution)/shard_map/ppermute | solution.py:26
  51.9 1.7 %collective-permute-start.19 = (f32[64,512]{1,0:T(8,128)S(1)}, f32[64,512]{1,0:T(8,128)S(1)}, u32[]{:S(2)}, u32[]{:S(2)}) collective-permute-start(f32[64,512]{1,0:T(8,128)S(1)} %get-tuple-element.35), channel_id=1, source_target_pairs={{0,1},{1,0},{2,3},{3,2},{4,5},{5,4},{6,7},{7,6},{8,9},{9,8},{10,11... | collective-permute-start | bytes 393224 | tf_op jit(solution)/shard_map/ppermute | solution.py:26
